TPU v7x, 32 devices: a whole 2x2x4 slice. The times are simulated.
32 devices in a mesh: section: 2 (over x), dp: 4 (over y, core), mp: 4 (over z).
Axes of the slice: x: 2, y: 2, z: 4, core: 2. Of those that a mesh axis runs over, the one named last changes fastest.
Arguments:
- tokens: bfloat16 [8, 768, 768], P('dp', 'mp'), may hold values from -6 to 6
- attn_gain: float32 [2, 768], P('section'), may hold values from 0.5 to 1.5
- w_query: bfloat16 [2, 768, 768], P('section', None, 'mp'), may hold values from -0.02734375 to 0.02734375
- w_key: bfloat16 [2, 768, 768], P('section', None, 'mp'), may hold values from -0.21875 to 0.21875
- w_value: bfloat16 [2, 768, 768], P('section', None, 'mp'), may hold values from -0.21875 to 0.21875
- w_out: bfloat16 [2, 768, 768], P('section', 'mp'), may hold values from -1.25 to 1.25
- ffn_gain: float32 [2, 768], P('section'), may hold values from 0.5 to 1.5
- w_gate: bfloat16 [2, 768, 2048], P('section', None, 'mp'), may hold values from -0.21875 to 0.21875
- w_up: bfloat16 [2, 768, 2048], P('section', None, 'mp'), may hold values from -0.21875 to 0.21875
- w_down: bfloat16 [2, 2048, 768], P('section', 'mp'), may hold values from -0.125 to 0.125
- rel_table: float32 [32, 12], P(None, 'mp'), may hold values from -4 to 4
- final_gain: float32 [768], replicated, may hold values from 0.5 to 1.5
- w_proj: bfloat16 [768, 128], replicated, may hold values from -0.21875 to 0.21875
- positives: int32 [64, 4], P('dp'), may hold values from -1 to 7, as said below
- retrieved: int32 [64, 32, 32], P('dp'), may hold values from 0 to 4095
Outputs:
- loss: float32 [], replicated
- d_inputs: bfloat16 [2, 8, 768, 768], P('section', 'dp', 'mp')
- grad_attn_gain: float32 [2, 768], P('section')
- grad_w_query: float32 [2, 768, 768], P('section', None, 'mp')
- grad_w_key: float32 [2, 768, 768], P('section', None, 'mp')
- grad_w_value: float32 [2, 768, 768], P('section', None, 'mp')
- grad_w_out: float32 [2, 768, 768], P('section', 'mp')
- grad_ffn_gain: float32 [2, 768], P('section')
- grad_w_gate: float32 [2, 768, 2048], P('section', None, 'mp')
- grad_w_up: float32 [2, 768, 2048], P('section', None, 'mp')
- grad_w_down: float32 [2, 2048, 768], P('section', 'mp')
- grad_rel_table: float32 [32, 12], P(None, 'mp')
- grad_final_gain: float32 [768], replicated
- grad_w_proj: float32 [768, 128], P(None, 'mp')
Inputs may be any that keep to these rules, and one draw needn't show every extreme that they name: `positives`: each row lists 1 to 4 different document numbers first and -1 in its remaining slots; some row lists 4, some row one.
All inputs are finite; a program needn't handle non-finite values.
Results may differ from a plain program's by a relative error of at most 0.035.
Values may be sent and summed in bfloat16 or wider, within the bound.
No kernel may reach another device: no remote copies, remote signals or barrier semaphores. Data moves between devices by JAX's collectives and lax.ppermute only.
A program may use at most 192 MiB of HBM per device.

v0:
```python
import jax
import jax.numpy as jnp
from jax import lax
from jax.sharding import PartitionSpec as P

HEAD_DIM = 64
PROJ = 128
DOC_LEN = 512
QRY_LEN = 32
DOCS_MB = 1
QRYS_MB = 8


bucket_edges = (8, 12, 16, 23, 32, 46, 64, 91)
norm_eps = 1e-06
logit_scale = 16.0
highest = lax.Precision.HIGHEST


def from_behind(shard, axis, by):
    devices = lax.axis_size(axis)
    pairs = [(i, i + by) for i in range(devices) if 0 <= i + by < devices]
    return lax.ppermute(shard, axis, pairs)


def bucket_of(length, half_count):
    places = jnp.arange(length, dtype=jnp.int32)
    offset = places[None, :] - places[:, None]
    spread = jnp.abs(offset)
    far_bucket = 7 + sum(
        ((spread >= bucket_edge).astype(jnp.int32) for bucket_edge in bucket_edges)
    )
    near_bucket = jnp.where(spread < 8, spread, far_bucket)
    return near_bucket + half_count * (offset > 0).astype(jnp.int32)


def rms_norm(values, gain_vector):
    return (
        values
        * lax.rsqrt(jnp.mean(values * values, axis=-1, keepdims=True) + norm_eps)
        * gain_vector
    )


def matmul(left_side, right_side):
    return jnp.dot(left_side, right_side, preferred_element_type=jnp.float32)


def contract_rows(left_side, right_side):
    return lax.dot_general(
        left_side, right_side, (((0,), (0,)), ((), ())), preferred_element_type=jnp.float32
    )


def times_transposed(left_side, right_side):
    return lax.dot_general(
        left_side, right_side, (((1,), (1,)), ((), ())), preferred_element_type=jnp.float32
    )


def gather_rows(values):
    return lax.all_gather(values, "mp", axis=0, tiled=True)


def spread_rows(values):
    return lax.psum_scatter(
        values.astype(jnp.bfloat16), "mp", scatter_dimension=0, tiled=True
    ).astype(jnp.float32)


def gather_grads(values):
    return lax.all_gather(values, "mp", axis=0, tiled=True)


def spread_grads(values):
    return lax.psum_scatter(
        values.astype(jnp.bfloat16), "mp", scatter_dimension=0, tiled=True
    ).astype(jnp.float32)


def bias_of(pick_table, rel_grid):
    return jnp.einsum("ijb,bh->hij", pick_table, rel_grid, precision=highest)


def split_segments(block_rows, head_count):
    doc_rows = DOCS_MB * DOC_LEN
    return (
        block_rows[:doc_rows].reshape(DOCS_MB, DOC_LEN, head_count, HEAD_DIM),
        block_rows[doc_rows:].reshape(QRYS_MB, QRY_LEN, head_count, HEAD_DIM),
    )


def join_segments(pieces):
    return jnp.concatenate(
        [one_piece.reshape(-1, one_piece.shape[2] * one_piece.shape[3]) for one_piece in pieces],
        axis=0,
    )


def attend(query_rows, key_rows, value_rows, bias_rows):
    scores = (
        jnp.einsum("bihd,bjhd->bhij", query_rows, key_rows, preferred_element_type=jnp.float32)
        + bias_rows[None]
    )
    row_peak = jnp.max(scores, axis=-1, keepdims=True)
    weights = jnp.exp(scores - row_peak)
    row_total = jnp.sum(weights, axis=-1, keepdims=True)
    mixed_rows = jnp.einsum(
        "bhij,bjhd->bihd",
        (weights / row_total).astype(jnp.bfloat16),
        value_rows,
        preferred_element_type=jnp.float32,
    )
    return (mixed_rows.astype(jnp.bfloat16), row_peak + jnp.log(row_total))


def attend_back(query_rows, key_rows, value_rows, bias_rows, log_total, grad_mixed):
    scores = (
        jnp.einsum("bihd,bjhd->bhij", query_rows, key_rows, preferred_element_type=jnp.float32)
        + bias_rows[None]
    )
    prob_rows = jnp.exp(scores - log_total)
    grad_probs = jnp.einsum(
        "bihd,bjhd->bhij", grad_mixed, value_rows, preferred_element_type=jnp.float32
    )
    grad_scores = (
        prob_rows * (grad_probs - jnp.sum(prob_rows * grad_probs, axis=-1, keepdims=True))
    ).astype(jnp.bfloat16)
    grad_query = jnp.einsum(
        "bhij,bjhd->bihd", grad_scores, key_rows, preferred_element_type=jnp.float32
    ).astype(jnp.bfloat16)
    grad_key = jnp.einsum(
        "bhij,bihd->bjhd", grad_scores, query_rows, preferred_element_type=jnp.float32
    ).astype(jnp.bfloat16)
    grad_value = jnp.einsum(
        "bhij,bihd->bjhd",
        prob_rows.astype(jnp.bfloat16),
        grad_mixed,
        preferred_element_type=jnp.float32,
    ).astype(jnp.bfloat16)
    return (grad_query, grad_key, grad_value, jnp.sum(grad_scores.astype(jnp.float32), axis=0))


def self_attend(query_rows, key_rows, value_rows, rel_grid, pick_tables):
    head_count = rel_grid.shape[1]
    queries = split_segments(query_rows, head_count)
    keys_all = split_segments(key_rows, head_count)
    values_all = split_segments(value_rows, head_count)
    mixed_parts, log_totals = ([], [])
    for segment in range(2):
        joined, log_total = attend(
            queries[segment],
            keys_all[segment],
            values_all[segment],
            bias_of(pick_tables[segment], rel_grid),
        )
        mixed_parts.append(joined)
        log_totals.append(log_total)
    return (join_segments(mixed_parts), tuple(log_totals))


def self_attend_back(
    query_rows, key_rows, value_rows, rel_grid, pick_tables, log_totals, grad_mixed
):
    head_count = rel_grid.shape[1]
    queries = split_segments(query_rows, head_count)
    keys_all = split_segments(key_rows, head_count)
    values_all = split_segments(value_rows, head_count)
    grads_mixed = split_segments(grad_mixed, head_count)
    grad_queries, grad_keys, grad_values = ([], [], [])
    grad_grid = jnp.zeros(rel_grid.shape, jnp.float32)
    for segment in range(2):
        grad_query, grad_key, grad_value, score_sum = attend_back(
            queries[segment],
            keys_all[segment],
            values_all[segment],
            bias_of(pick_tables[segment], rel_grid),
            log_totals[segment],
            grads_mixed[segment],
        )
        grad_queries.append(grad_query)
        grad_keys.append(grad_key)
        grad_values.append(grad_value)
        grad_grid = grad_grid + jnp.einsum(
            "hij,ijb->bh", score_sum, pick_tables[segment], precision=highest
        )
    return (
        join_segments(grad_queries),
        join_segments(grad_keys),
        join_segments(grad_values),
        grad_grid,
    )


def layer_forward(entry_rows, weights, pick_tables):
    attn_gain, w_query, w_key, w_value, w_out, ffn_gain, w_gate, w_up, w_down, rel_grid = weights
    residual = entry_rows.astype(jnp.float32)
    normed = gather_rows(rms_norm(residual, attn_gain).astype(jnp.bfloat16))
    query_rows = matmul(normed, w_query).astype(jnp.bfloat16)
    key_rows = matmul(normed, w_key).astype(jnp.bfloat16)
    value_rows = matmul(normed, w_value).astype(jnp.bfloat16)
    mixed_rows, log_totals = self_attend(query_rows, key_rows, value_rows, rel_grid, pick_tables)
    middle = residual + spread_rows(matmul(mixed_rows, w_out))
    normed_ffn = gather_rows(rms_norm(middle, ffn_gain).astype(jnp.bfloat16))
    gate_rows = matmul(normed_ffn, w_gate)
    up_proj = matmul(normed_ffn, w_up)
    hidden = (jax.nn.gelu(gate_rows, approximate=True) * up_proj).astype(jnp.bfloat16)
    result = middle + spread_rows(matmul(hidden, w_down))
    return (
        result,
        (
            normed,
            query_rows,
            key_rows,
            value_rows,
            mixed_rows,
            log_totals,
            middle,
            normed_ffn,
            gate_rows,
            up_proj,
            hidden,
        ),
    )


def layer_backward(entry_rows, kept_values, weights, pick_tables, grad_out):
    attn_gain, w_query, w_key, w_value, w_out, ffn_gain, w_gate, w_up, w_down, rel_grid = weights
    (
        normed,
        query_rows,
        key_rows,
        value_rows,
        mixed_rows,
        log_totals,
        middle,
        normed_ffn,
        gate_rows,
        up_proj,
        hidden,
    ) = kept_values
    residual = entry_rows.astype(jnp.float32)
    grad_full = gather_grads(grad_out.astype(jnp.bfloat16))
    grad_w_down = contract_rows(hidden, grad_full)
    grad_hidden = times_transposed(grad_full, w_down)
    _, gelu_back = jax.vjp(
        lambda gate_in, up_in: jax.nn.gelu(gate_in, approximate=True) * up_in, gate_rows, up_proj
    )
    grad_gate, grad_up = gelu_back(grad_hidden)
    grad_gate = grad_gate.astype(jnp.bfloat16)
    grad_up = grad_up.astype(jnp.bfloat16)
    grad_w_gate = contract_rows(normed_ffn, grad_gate)
    grad_w_up = contract_rows(normed_ffn, grad_up)
    grad_normed_ffn = spread_grads(
        times_transposed(grad_gate, w_gate) + times_transposed(grad_up, w_up)
    )
    _, norm_back = jax.vjp(rms_norm, middle, ffn_gain)
    grad_middle_norm, grad_ffn_gain = norm_back(grad_normed_ffn)
    grad_middle = grad_out + grad_middle_norm
    grad_branch = gather_grads(grad_middle.astype(jnp.bfloat16))
    grad_w_out = contract_rows(mixed_rows, grad_branch)
    grad_mixed = times_transposed(grad_branch, w_out).astype(jnp.bfloat16)
    grad_query, grad_key, grad_value, grad_grid = self_attend_back(
        query_rows, key_rows, value_rows, rel_grid, pick_tables, log_totals, grad_mixed
    )
    grad_w_query = contract_rows(normed, grad_query)
    grad_w_key = contract_rows(normed, grad_key)
    grad_w_value = contract_rows(normed, grad_value)
    grad_normed = spread_grads(
        times_transposed(grad_query, w_query)
        + times_transposed(grad_key, w_key)
        + times_transposed(grad_value, w_value)
    )
    _, norm_back = jax.vjp(rms_norm, residual, attn_gain)
    grad_entry_norm, grad_attn_gain = norm_back(grad_normed)
    grad_entry = grad_middle + grad_entry_norm
    weight_grads = (
        grad_w_query,
        grad_w_key,
        grad_w_value,
        grad_w_out,
        grad_w_gate,
        grad_w_up,
        grad_w_down,
    )
    return (grad_entry, weight_grads, (grad_attn_gain, grad_ffn_gain), grad_grid)


def retrieval_loss(raw_scores, owner_hot, chosen, query_count):
    doc_mass = jnp.einsum(
        "qik,qikd->qid", jnp.exp(raw_scores * PROJ ** (-0.5)), owner_hot, precision=highest
    )
    doc_logit = logit_scale * jnp.mean(jnp.log1p(doc_mass), axis=1)
    row_peak = jnp.max(doc_logit, axis=-1, keepdims=True)
    spread = jnp.exp(doc_logit - row_peak)
    all_term = jnp.log(jnp.sum(spread, axis=-1))
    pos_term = jnp.log(jnp.sum(chosen * spread, axis=-1))
    return jnp.sum(all_term - pos_term) / query_count


def masked(tree_value, is_live):
    return jax.tree.map(lambda member: jnp.where(is_live, member, 0.0), tree_value)


def on_device(
    tokens,
    attn_gain,
    w_query,
    w_key,
    w_value,
    w_out,
    ffn_gain,
    w_gate,
    w_up,
    w_down,
    rel_table,
    final_gain,
    w_proj,
    positives,
    retrieved,
):
    section_index = lax.axis_index("section")
    upstream = section_index == 0
    downstream = jnp.logical_not(upstream)
    mp_index = lax.axis_index("mp")
    mp_count = lax.axis_size("mp")
    weights = (
        attn_gain[0],
        w_query[0],
        w_key[0],
        w_value[0],
        w_out[0],
        ffn_gain[0],
        w_gate[0],
        w_up[0],
        w_down[0],
        rel_table,
    )
    bucket_ids = jnp.arange(rel_table.shape[0], dtype=jnp.int32)
    half_count = rel_table.shape[0] // 2
    pick_tables = tuple(
        (
            (bucket_of(length, half_count)[:, :, None] == bucket_ids).astype(jnp.float32)
            for length in (DOC_LEN, QRY_LEN)
        )
    )
    micro_count = tokens.shape[0]
    shard_rows = tokens.shape[1]
    inbox_rows = jnp.zeros_like(tokens[0])
    entries, results, records = ([], [], [])
    for turn_number in range(micro_count + 1):
        entry_rows = jnp.where(upstream, tokens[min(turn_number, micro_count - 1)], inbox_rows)
        result, kept_values = layer_forward(entry_rows, weights, pick_tables)
        entries.append(entry_rows)
        results.append(result)
        records.append(kept_values)
        if turn_number < micro_count:
            inbox_rows = from_behind(result.astype(jnp.bfloat16), "section", 1)
    doc_rows = DOCS_MB * DOC_LEN
    qry_rows = QRYS_MB * QRY_LEN
    normed_final = [
        gather_rows(rms_norm(result, final_gain).astype(jnp.bfloat16)) for result in results[1:]
    ]
    doc_normed = jnp.concatenate([normed[:doc_rows] for normed in normed_final], axis=0)
    qry_normed = jnp.concatenate([normed[doc_rows:] for normed in normed_final], axis=0)
    queries_dev = positives.shape[0]
    query_count = queries_dev * lax.axis_size("dp")
    doc_count = doc_normed.shape[0] * lax.axis_size("dp") // DOC_LEN
    doc_ids = jnp.arange(doc_count, dtype=jnp.int32)
    owner_hot = ((retrieved // DOC_LEN)[..., None] == doc_ids).astype(jnp.float32)
    chosen = jnp.any(positives[:, :, None] == doc_ids, axis=1).astype(jnp.float32)
    flat_index = retrieved.reshape(-1)
    col_width = w_proj.shape[1] // mp_count
    col_start = mp_index * col_width

    def loss_of(raw_scores):
        return retrieval_loss(raw_scores, owner_hot, chosen, query_count)

    grad_finals = []
    doc_embed = matmul(doc_normed, w_proj).astype(jnp.bfloat16)
    qry_embed = matmul(qry_normed, w_proj).astype(jnp.bfloat16).reshape(queries_dev, QRY_LEN, -1)
    doc_pool = lax.all_gather(doc_embed, "dp", axis=0, tiled=True)
    picked = jnp.take(doc_pool, flat_index, axis=0).reshape(retrieved.shape + (doc_pool.shape[1],))
    raw_scores = jnp.einsum("qip,qikp->qik", qry_embed, picked, preferred_element_type=jnp.float32)
    loss_part, loss_back = jax.vjp(loss_of, raw_scores)
    (grad_raw,) = loss_back(jnp.ones((), jnp.float32))
    grad_qry_embed = jnp.einsum(
        "qik,qikp->qip", grad_raw, picked.astype(jnp.float32), precision=highest
    )
    grad_picked = grad_raw[..., None] * qry_embed.astype(jnp.float32)[:, :, None, :]
    dense_grads = (
        jnp.zeros(doc_pool.shape, jnp.float32)
        .at[flat_index]
        .add(grad_picked.reshape(-1, doc_pool.shape[1]))
    )
    grad_doc_embed = lax.psum_scatter(
        dense_grads.astype(jnp.bfloat16), "dp", scatter_dimension=0, tiled=True
    )
    grad_qry_embed = grad_qry_embed.reshape(-1, doc_pool.shape[1]).astype(jnp.bfloat16)
    grad_proj = contract_rows(doc_normed, grad_doc_embed) + contract_rows(
        qry_normed, grad_qry_embed
    )
    proj_mask = jnp.arange(w_proj.shape[1]) // col_width == mp_index
    proj_full = jnp.where(proj_mask[None, :], grad_proj, 0.0)
    grad_doc_normed = times_transposed(grad_doc_embed, w_proj)
    grad_qry_normed = times_transposed(grad_qry_embed, w_proj)
    for segment in range(micro_count):
        whole_rows = jnp.concatenate(
            [
                grad_doc_normed[segment * doc_rows : (segment + 1) * doc_rows],
                grad_qry_normed[segment * qry_rows : (segment + 1) * qry_rows],
            ],
            axis=0,
        )
        grad_finals.append(
            lax.dynamic_slice_in_dim(whole_rows, mp_index * shard_rows, shard_rows, 0)
        )
    grad_tail = []
    grad_final_gain = jnp.zeros(final_gain.shape, jnp.float32)
    for segment in range(micro_count):
        _, norm_back = jax.vjp(rms_norm, results[segment + 1], final_gain)
        grad_hidden_rows, grad_gain_rows = norm_back(grad_finals[segment])
        grad_tail.append(grad_hidden_rows)
        grad_final_gain = grad_final_gain + grad_gain_rows
    grad_inbox = jnp.zeros_like(tokens[0])
    weight_totals, gain_totals = (None, None)
    table_total = jnp.zeros(rel_table.shape, jnp.float32)
    grad_entries = []
    for turn_number in range(micro_count + 1):
        record_at = micro_count - turn_number
        grad_out = jnp.where(
            upstream,
            grad_inbox.astype(jnp.float32),
            grad_tail[max(micro_count - 1 - turn_number, 0)],
        )
        kept_values = records[record_at]
        grad_entry, weight_grads, gain_grads, table_grad = layer_backward(
            entries[record_at], kept_values, weights, pick_tables, grad_out
        )
        is_live = jnp.where(upstream, turn_number >= 1, turn_number < micro_count)
        weight_grads = masked(weight_grads, is_live)
        gain_grads = masked(gain_grads, is_live)
        table_total = table_total + masked(table_grad, is_live)
        if weight_totals is None:
            weight_totals, gain_totals = (weight_grads, gain_grads)
        else:
            weight_totals = jax.tree.map(jnp.add, weight_totals, weight_grads)
            gain_totals = jax.tree.map(jnp.add, gain_totals, gain_grads)
        sent_grads = grad_entry.astype(jnp.bfloat16)
        grad_entries.append(sent_grads)
        if turn_number < micro_count:
            grad_inbox = from_behind(sent_grads, "section", -1)
    sum_query, sum_key, sum_value, sum_out, sum_gate, sum_up, sum_down = (
        lax.psum(weight_totals[0].astype(jnp.bfloat16), "dp").astype(jnp.float32),
        lax.psum(weight_totals[1].astype(jnp.bfloat16), "dp").astype(jnp.float32),
        lax.psum(weight_totals[2].astype(jnp.bfloat16), "dp").astype(jnp.float32),
        lax.psum(weight_totals[3].astype(jnp.bfloat16), "dp").astype(jnp.float32),
        lax.psum(weight_totals[4].astype(jnp.bfloat16), "dp").astype(jnp.float32),
        lax.psum(weight_totals[5].astype(jnp.bfloat16), "dp").astype(jnp.float32),
        lax.psum(weight_totals[6].astype(jnp.bfloat16), "dp").astype(jnp.float32),
    )
    heads_dev = rel_table.shape[1]
    gain_rows = lax.dynamic_update_slice(
        jnp.zeros((2, lax.axis_size("section"), attn_gain.shape[1]), jnp.float32),
        jnp.stack([gain_totals[0], gain_totals[1]])[:, None, :],
        (0, section_index, 0),
    )
    table_full = lax.dynamic_update_slice(
        jnp.zeros((rel_table.shape[0], heads_dev * mp_count), jnp.float32),
        table_total,
        (0, mp_index * heads_dev),
    )
    head_gain = jnp.where(downstream, grad_final_gain, 0.0)
    proj_part = jnp.where(downstream, proj_full, 0.0)
    loss_share = jnp.where(jnp.logical_and(downstream, mp_index == 0), loss_part, 0.0)
    gain_sum, table_sum, head_sum, proj_sum, loss_value = lax.psum(
        (gain_rows, table_full, head_gain, proj_part, loss_share), ("section", "dp", "mp")
    )
    grad_attn_gain = lax.dynamic_slice_in_dim(gain_sum[0], section_index, 1, 0)
    grad_ffn_gain = lax.dynamic_slice_in_dim(gain_sum[1], section_index, 1, 0)
    grad_rel_table = lax.dynamic_slice_in_dim(table_sum, mp_index * heads_dev, heads_dev, 1)
    grad_w_proj = lax.dynamic_slice_in_dim(proj_sum, col_start, col_width, 1)
    d_inputs = jnp.stack(
        [
            jnp.where(
                upstream,
                grad_entries[micro_count - segment],
                grad_entries[micro_count - 1 - segment],
            )
            for segment in range(micro_count)
        ]
    )[None]
    return (
        loss_value,
        d_inputs,
        grad_attn_gain,
        sum_query[None],
        sum_key[None],
        sum_value[None],
        sum_out[None],
        grad_ffn_gain,
        sum_gate[None],
        sum_up[None],
        sum_down[None],
        grad_rel_table,
        head_sum,
        grad_w_proj,
    )


def solution(mesh):
    return jax.shard_map(
        on_device,
        mesh=mesh,
        in_specs=(
            P("dp", "mp", None),
            P("section", None),
            P("section", None, "mp"),
            P("section", None, "mp"),
            P("section", None, "mp"),
            P("section", "mp", None),
            P("section", None),
            P("section", None, "mp"),
            P("section", None, "mp"),
            P("section", "mp", None),
            P(None, "mp"),
            P(),
            P(),
            P("dp", None),
            P("dp", None, None),
        ),
        out_specs=(
            P(),
            P("section", "dp", "mp", None),
            P("section", None),
            P("section", None, "mp"),
            P("section", None, "mp"),
            P("section", None, "mp"),
            P("section", "mp", None),
            P("section", None),
            P("section", None, "mp"),
            P("section", None, "mp"),
            P("section", "mp", None),
            P(None, "mp"),
            P(),
            P(None, "mp"),
        ),
        check_vma=False,
    )
```

profile of v0, /device:TPU:8, one launch (start us, length us, event | category | flops | bytes accessed | tf_op | source)
XLA Modules:
  0.0 1528.9 jit_solution(16195743785026044991)
XLA Ops:
  15.0 11.5 fusion.3
  31.5 11.2 all-gather.16.cloned.1.call-done
  56.7 26.9 %reduce-scatter.14.cloned.1.call-done = bf16[192,768]{1,0:T(8,128)(2,1)} async-done(((bf16[768,768]{1,0:T(8,128)(2,1)}), bf16[192,768]{1,0:T(8,128)(2,1)}) %reduce-scatter.14.cloned.1.call-update) | async-done | bytes 294928 | tf_op jit(solution)/shard_map/reduce_scatter | solution.py:66
  86.9 30.5 %all-gather.18.cloned.1.call-done = bf16[768,768]{1,0:T(8,128)(2,1)} async-done(((bf16[192,768]{1,0:T(8,128)(2,1)}), bf16[768,768]{1,0:T(8,128)(2,1)}) %all-gather.18.cloned.1.call-update) | async-done | bytes 1179664 | tf_op jit(solution)/shard_map/all_gather | solution.py:62
  124.7 26.9 %reduce-scatter.16.cloned.1.call-done = bf16[192,768]{1,0:T(8,128)(2,1)} async-done(((bf16[768,768]{1,0:T(8,128)(2,1)}), bf16[192,768]{1,0:T(8,128)(2,1)}) %reduce-scatter.16.cloned.1.call-update) | async-done | bytes 294928 | tf_op jit(solution)/shard_map/reduce_scatter | solution.py:66
  163.4 31.9 %all-gather.20.cloned.1.call-done = bf16[768,768]{1,0:T(8,128)(2,1)} async-done(((bf16[192,768]{1,0:T(8,128)(2,1)}), bf16[768,768]{1,0:T(8,128)(2,1)}) %all-gather.20.cloned.1.call-update) | async-done | bytes 1179664 | tf_op jit(solution)/shard_map/all_gather | solution.py:62
  221.3 26.9 %reduce-scatter.18.cloned.1.call-done = bf16[192,768]{1,0:T(8,128)(2,1)} async-done(((bf16[768,768]{1,0:T(8,128)(2,1)}), bf16[192,768]{1,0:T(8,128)(2,1)}) %reduce-scatter.18.cloned.1.call-update) | async-done | bytes 294928 | tf_op jit(solution)/shard_map/reduce_scatter | solution.py:66
  251.3 30.7 %all-gather.22.cloned.1.call-done = bf16[768,768]{1,0:T(8,128)(2,1)} async-done(((bf16[192,768]{1,0:T(8,128)(2,1)}), bf16[768,768]{1,0:T(8,128)(2,1)}) %all-gather.22.cloned.1.call-update) | async-done | bytes 1179664 | tf_op jit(solution)/shard_map/all_gather | solution.py:62
  289.3 26.9 %reduce-scatter.20.cloned.1.call-done = bf16[192,768]{1,0:T(8,128)(2,1)} async-done(((bf16[768,768]{1,0:T(8,128)(2,1)}), bf16[192,768]{1,0:T(8,128)(2,1)}) %reduce-scatter.20.cloned.1.call-update) | async-done | bytes 294928 | tf_op jit(solution)/shard_map/reduce_scatter | solution.py:66
  329.5 31.4 %all-gather.26.cloned.1.call-done = bf16[768,768]{1,0:T(8,128)(2,1)} async-done(((bf16[192,768]{1,0:T(8,128)(2,1)}), bf16[768,768]{1,0:T(8,128)(2,1)}) %all-gather.26.cloned.1.call-update) | async-done | bytes 1179664 | tf_op jit(solution)/shard_map/all_gather | solution.py:62
  393.4 26.9 %reduce-scatter.22.cloned.1.call-done = bf16[192,768]{1,0:T(8,128)(2,1)} async-done(((bf16[768,768]{1,0:T(8,128)(2,1)}), bf16[192,768]{1,0:T(8,128)(2,1)}) %reduce-scatter.22.cloned.1.call-update) | async-done | bytes 294928 | tf_op jit(solution)/shard_map/reduce_scatter | solution.py:66
  423.3 30.7 %all-gather.28.cloned.1.call-done = bf16[768,768]{1,0:T(8,128)(2,1)} async-done(((bf16[192,768]{1,0:T(8,128)(2,1)}), bf16[768,768]{1,0:T(8,128)(2,1)}) %all-gather.28.cloned.1.call-update) | async-done | bytes 1179664 | tf_op jit(solution)/shard_map/all_gather | solution.py:62
  462.1 26.2 %reduce-scatter.24.cloned.1.call-done = bf16[192,768]{1,0:T(8,128)(2,1)} async-done(((bf16[768,768]{1,0:T(8,128)(2,1)}), bf16[192,768]{1,0:T(8,128)(2,1)}) %reduce-scatter.24.cloned.1.call-update) | async-done | bytes 294928 | tf_op jit(solution)/shard_map/reduce_scatter | solution.py:66
  492.7 28.4 %all-gather.24.cloned.1.call-done = bf16[768,768]{1,0:T(8,128)(2,1)} async-done(((bf16[192,768]{1,0:T(8,128)(2,1)}), bf16[768,768]{1,0:T(8,128)(2,1)}) %all-gather.24.cloned.1.call-update) | async-done | bytes 1179664 | tf_op jit(solution)/shard_map/all_gather | solution.py:62
  523.2 29.5 %all-gather.30.cloned.1.call-done = bf16[768,768]{1,0:T(8,128)(2,1)} async-done(((bf16[192,768]{1,0:T(8,128)(2,1)}), bf16[768,768]{1,0:T(8,128)(2,1)}) %all-gather.30.cloned.1.call-update) | async-done | bytes 1179664 | tf_op jit(solution)/shard_map/all_gather | solution.py:62
  572.7 56.7 %gather_fusion = bf16[16384,128]{1,0:T(8,128)(2,1)} fusion(bf16[4096,128]{1,0:T(8,128)(2,1)} %all-gather.32.cloned.1.call-done, s32[16384]{0:T(1024)S(1)} %broadcast_clamp_fusion), kind=kCustom, calls=%fused_computation | custom fusion | bytes 8454144 | tf_op jit(solution)/shard_map/jit(_take)/gather | solution.py:383
  653.9 89.1 %scatter_custom_fusion = f32[4096,128]{1,0:T(8,128)} fusion(s32[16384]{0:T(1024)} %bitcast.578, f32[16384,128]{1,0:T(8,128)} %bitcast_multiply_fusion, f32[]{:T(128)} %constant.66.clone.1), kind=kCustom, calls=%fused_computation.223 | custom fusion | flops 2097152 | bytes 2097664 | tf_op jit(solution)/shard_map/scatter-add | solution.py:394
  754.7 16.0 %reduce-scatter.26.cloned.1.call-done = bf16[1024,128]{1,0:T(8,128)(2,1)} async-done(((bf16[4096,128]{1,0:T(8,128)(2,1)}), bf16[1024,128]{1,0:T(8,128)(2,1)}) %reduce-scatter.26.cloned.1.call-update) | async-done | bytes 262160 | tf_op jit(solution)/shard_map/reduce_scatter | solution.py:396
  776.8 30.0 %all-gather.34.cloned.1.call-done = bf16[768,768]{1,0:T(8,128)(2,1)} async-done(((bf16[192,768]{1,0:T(8,128)(2,1)}), bf16[768,768]{1,0:T(8,128)(2,1)}) %all-gather.34.cloned.1.call-update) | async-done | bytes 1179664 | tf_op jit(solution)/shard_map/all_gather | solution.py:72
  814.6 26.9 %reduce-scatter.28.cloned.1.call-done = bf16[192,768]{1,0:T(8,128)(2,1)} async-done(((bf16[768,768]{1,0:T(8,128)(2,1)}), bf16[192,768]{1,0:T(8,128)(2,1)}) %reduce-scatter.28.cloned.1.call-update) | async-done | bytes 294928 | tf_op jit(solution)/shard_map/reduce_scatter | solution.py:76
  849.0 29.1 %all-gather.36.cloned.1.call-done = bf16[768,768]{1,0:T(8,128)(2,1)} async-done(((bf16[192,768]{1,0:T(8,128)(2,1)}), bf16[768,768]{1,0:T(8,128)(2,1)}) %all-gather.36.cloned.1.call-update) | async-done | bytes 1179664 | tf_op jit(solution)/shard_map/all_gather | solution.py:72
  910.4 26.9 %reduce-scatter.30.cloned.1.call-done = bf16[192,768]{1,0:T(8,128)(2,1)} async-done(((bf16[768,768]{1,0:T(8,128)(2,1)}), bf16[192,768]{1,0:T(8,128)(2,1)}) %reduce-scatter.30.cloned.1.call-update) | async-done | bytes 294928 | tf_op jit(solution)/shard_map/reduce_scatter | solution.py:76
  953.9 29.9 %all-gather.38.cloned.1.call-done = bf16[768,768]{1,0:T(8,128)(2,1)} async-done(((bf16[192,768]{1,0:T(8,128)(2,1)}), bf16[768,768]{1,0:T(8,128)(2,1)}) %all-gather.38.cloned.1.call-update) | async-done | bytes 1179664 | tf_op jit(solution)/shard_map/all_gather | solution.py:72
  991.5 26.9 %reduce-scatter.32.cloned.1.call-done = bf16[192,768]{1,0:T(8,128)(2,1)} async-done(((bf16[768,768]{1,0:T(8,128)(2,1)}), bf16[192,768]{1,0:T(8,128)(2,1)}) %reduce-scatter.32.cloned.1.call-update) | async-done | bytes 294928 | tf_op jit(solution)/shard_map/reduce_scatter | solution.py:76
  1025.5 28.7 %all-gather.40.cloned.1.call-done = bf16[768,768]{1,0:T(8,128)(2,1)} async-done(((bf16[192,768]{1,0:T(8,128)(2,1)}), bf16[768,768]{1,0:T(8,128)(2,1)}) %all-gather.40.cloned.1.call-update) | async-done | bytes 1179664 | tf_op jit(solution)/shard_map/all_gather | solution.py:72
  1088.6 26.9 %reduce-scatter.34.cloned.1.call-done = bf16[192,768]{1,0:T(8,128)(2,1)} async-done(((bf16[768,768]{1,0:T(8,128)(2,1)}), bf16[192,768]{1,0:T(8,128)(2,1)}) %reduce-scatter.34.cloned.1.call-update) | async-done | bytes 294928 | tf_op jit(solution)/shard_map/reduce_scatter | solution.py:76
  1133.4 29.9 %all-gather.42.cloned.1.call-done = bf16[768,768]{1,0:T(8,128)(2,1)} async-done(((bf16[192,768]{1,0:T(8,128)(2,1)}), bf16[768,768]{1,0:T(8,128)(2,1)}) %all-gather.42.cloned.1.call-update) | async-done | bytes 1179664 | tf_op jit(solution)/shard_map/all_gather | solution.py:72
  1171.0 26.9 %reduce-scatter.36.cloned.1.call-done = bf16[192,768]{1,0:T(8,128)(2,1)} async-done(((bf16[768,768]{1,0:T(8,128)(2,1)}), bf16[192,768]{1,0:T(8,128)(2,1)}) %reduce-scatter.36.cloned.1.call-update) | async-done | bytes 294928 | tf_op jit(solution)/shard_map/reduce_scatter | solution.py:76
  1266.4 100.1 %all-reduce.5.cloned.1.call-done = f32[768,128]{0,1:T(8,128)} async-done(((f32[768,128]{0,1:T(8,128)}), f32[768,128]{0,1:T(8,128)}) %all-reduce.5.cloned.1.call-update) | async-done | bytes 393232 | tf_op jit(solution)/shard_map/psum | solution.py:476
  1403.4 41.6 %all-reduce.7.cloned.1.call-done = (bf16[1,768,192]{1,2,0:T(8,128)(2,1)}, bf16[1,768,192]{1,2,0:T(8,128)(2,1)}, bf16[1,768,192]{1,2,0:T(8,128)(2,1)}, bf16[1,192...) async-done(((bf16[1,768,192]{1,2,0:T(8,128)(2,1)}, bf16[1,768,192]{1,2,0:T(8,128)(2,1)}, ...) | async-done | bytes 3538960 | tf_op jit(solution)/shard_map/psum | solution.py:454
  1454.5 20.1 %reduce-scatter.38.cloned.1.call-done = bf16[192,768]{1,0:T(8,128)(2,1)} async-done(((bf16[768,768]{1,0:T(8,128)(2,1)}), bf16[192,768]{1,0:T(8,128)(2,1)}) %reduce-scatter.38.cloned.1.call-update) | async-done | bytes 294928 | tf_op jit(solution)/shard_map/reduce_scatter | solution.py:76
  1476.0 41.9 %all-reduce = (f32[]{:T(128)}, f32[2,2,768]{2,1,0:T(2,128)S(1)}, f32[32,12]{0,1:T(8,128)S(1)}, f32[768]{0:T(1024)}) all-reduce(f32[]{:T(128)S(6)} %select_n.323, f32[2,2,768]{2,1,0:T(2,128)S(1)} %dynamic_update_slice.6, f32[32,12]{0,1:T(8,128)S(1)} %dynamic_update_slice.7, ...), channel_id=1, replica_groups=mesh['section'=2,'dp'=4,'mp'=4] {'section','dp','mp'}, use_global_device_ids=true, to_apply=%region_32.33 | all-reduce | flops 4225 | bytes 33800 | tf_op jit(solution)/shard_map/psum | solution.py:476
  (902 shorter events, 466.4 us)
Async XLA Ops:
  7.2 35.6 %all-gather.16.cloned.1.call-start = ((), (), s32[]{:S(2)}) async-start(), calls=%async_computation.13 | async-start | bytes 1474560 | tf_op jit(solution)/shard_map/all_gather | solution.py:62
  11.5 72.1 %reduce-scatter.14.cloned.1.call-start = ((), (), s32[]{:S(2)}) async-start(), calls=%async_computation.14 | async-start | bytes 1474560 | tf_op jit(solution)/shard_map/reduce_scatter | solution.py:66
  56.6 60.8 %all-gather.18.cloned.1.call-start = ((), (), s32[]{:S(2)}) async-start(), calls=%async_computation.15 | async-start | bytes 1474560 | tf_op jit(solution)/shard_map/all_gather | solution.py:62
  86.6 65.0 %reduce-scatter.16.cloned.1.call-start = ((), (), s32[]{:S(2)}) async-start(), calls=%async_computation.16 | async-start | bytes 1474560 | tf_op jit(solution)/shard_map/reduce_scatter | solution.py:66
  124.6 70.7 %all-gather.20.cloned.1.call-start = ((), (), s32[]{:S(2)}) async-start(), calls=%async_computation.17 | async-start | bytes 1474560 | tf_op jit(solution)/shard_map/all_gather | solution.py:62
  163.4 84.8 %reduce-scatter.18.cloned.1.call-start = ((), (), s32[]{:S(2)}) async-start(), calls=%async_computation.18 | async-start | bytes 1474560 | tf_op jit(solution)/shard_map/reduce_scatter | solution.py:66
  221.2 60.7 %all-gather.22.cloned.1.call-start = ((), (), s32[]{:S(2)}) async-start(), calls=%async_computation.19 | async-start | bytes 1474560 | tf_op jit(solution)/shard_map/all_gather | solution.py:62
  251.2 65.1 %reduce-scatter.20.cloned.1.call-start = ((), (), s32[]{:S(2)}) async-start(), calls=%async_computation.20 | async-start | bytes 1474560 | tf_op jit(solution)/shard_map/reduce_scatter | solution.py:66
  289.3 71.7 %all-gather.26.cloned.1.call-start = ((), (), s32[]{:S(2)}) async-start(), calls=%async_computation.22 | async-start | bytes 1474560 | tf_op jit(solution)/shard_map/all_gather | solution.py:62
  329.1 91.2 %reduce-scatter.22.cloned.1.call-start = ((), (), s32[]{:S(2)}) async-start(), calls=%async_computation.23 | async-start | bytes 1474560 | tf_op jit(solution)/shard_map/reduce_scatter | solution.py:66
  393.3 60.7 %all-gather.28.cloned.1.call-start = ((), (), s32[]{:S(2)}) async-start(), calls=%async_computation.24 | async-start | bytes 1474560 | tf_op jit(solution)/shard_map/all_gather | solution.py:62
  423.3 65.0 %reduce-scatter.24.cloned.1.call-start = ((), (), s32[]{:S(2)}) async-start(), calls=%async_computation.25 | async-start | bytes 1474560 | tf_op jit(solution)/shard_map/reduce_scatter | solution.py:66
  461.3 59.8 %all-gather.24.cloned.1.call-start = ((), (), s32[]{:S(2)}) async-start(), calls=%async_computation.21 | async-start | bytes 1474560 | tf_op jit(solution)/shard_map/all_gather | solution.py:62
  462.1 90.6 %all-gather.30.cloned.1.call-start = ((), (), s32[]{:S(2)}) async-start(), calls=%async_computation.26 | async-start | bytes 1474560 | tf_op jit(solution)/shard_map/all_gather | solution.py:62
  491.5 81.2 %all-gather.32.cloned.1.call-start = ((), (), s32[]{:S(2)}) async-start(), calls=%async_computation.27 | async-start | bytes 1310720 | tf_op jit(solution)/shard_map/all_gather | solution.py:382
  556.2 214.6 %reduce-scatter.26.cloned.1.call-start = ((), (), s32[]{:S(2)}) async-start(), calls=%async_computation.28 | async-start | bytes 1310720 | tf_op jit(solution)/shard_map/reduce_scatter | solution.py:396
  745.7 61.2 %all-gather.34.cloned.1.call-start = ((), (), s32[]{:S(2)}) async-start(), calls=%async_computation.29 | async-start | bytes 1474560 | tf_op jit(solution)/shard_map/all_gather | solution.py:72
  776.8 64.7 %reduce-scatter.28.cloned.1.call-start = ((), (), s32[]{:S(2)}) async-start(), calls=%async_computation.30 | async-start | bytes 1474560 | tf_op jit(solution)/shard_map/reduce_scatter | solution.py:76
  814.5 63.6 %all-gather.36.cloned.1.call-start = ((), (), s32[]{:S(2)}) async-start(), calls=%async_computation.31 | async-start | bytes 1474560 | tf_op jit(solution)/shard_map/all_gather | solution.py:72
  847.3 90.0 %reduce-scatter.30.cloned.1.call-start = ((), (), s32[]{:S(2)}) async-start(), calls=%async_computation.32 | async-start | bytes 1474560 | tf_op jit(solution)/shard_map/reduce_scatter | solution.py:76
  910.3 73.4 %all-gather.38.cloned.1.call-start = ((), (), s32[]{:S(2)}) async-start(), calls=%async_computation.33 | async-start | bytes 1474560 | tf_op jit(solution)/shard_map/all_gather | solution.py:72
  941.3 10.6 collective-permute-start.2
  953.8 64.6 %reduce-scatter.32.cloned.1.call-start = ((), (), s32[]{:S(2)}) async-start(), calls=%async_computation.34 | async-start | bytes 1474560 | tf_op jit(solution)/shard_map/reduce_scatter | solution.py:76
  991.4 62.7 %all-gather.40.cloned.1.call-start = ((), (), s32[]{:S(2)}) async-start(), calls=%async_computation.35 | async-start | bytes 1474560 | tf_op jit(solution)/shard_map/all_gather | solution.py:72
  1023.2 92.3 %reduce-scatter.34.cloned.1.call-start = ((), (), s32[]{:S(2)}) async-start(), calls=%async_computation.36 | async-start | bytes 1474560 | tf_op jit(solution)/shard_map/reduce_scatter | solution.py:76
  1088.5 74.8 %all-gather.42.cloned.1.call-start = ((), (), s32[]{:S(2)}) async-start(), calls=%async_computation.37 | async-start | bytes 1474560 | tf_op jit(solution)/shard_map/all_gather | solution.py:72
  1121.2 10.6 collective-permute-start.3
  1133.3 64.6 %reduce-scatter.36.cloned.1.call-start = ((), (), s32[]{:S(2)}) async-start(), calls=%async_computation.38 | async-start | bytes 1474560 | tf_op jit(solution)/shard_map/reduce_scatter | solution.py:76
  1171.0 62.3 %all-gather.44.cloned.1.call-start = ((), (), s32[]{:S(2)}) async-start(), calls=%async_computation.39 | async-start | bytes 1474560 | tf_op jit(solution)/shard_map/all_gather | solution.py:72
  1202.3 164.3 %all-reduce.5.cloned.1.call-start = ((), (), s32[]{:S(2)}) async-start(), calls=%async_computation.41 | async-start | bytes 786432 | tf_op jit(solution)/shard_map/psum | solution.py:476
  1207.5 237.6 %all-reduce.7.cloned.1.call-start = ((), (), s32[]{:S(2)}) async-start(), calls=%async_computation.42 | async-start | bytes 7077888 | tf_op jit(solution)/shard_map/psum | solution.py:454
  1265.6 209.0 %reduce-scatter.38.cloned.1.call-start = ((), (), s32[]{:S(2)}) async-start(), calls=%async_computation.40 | async-start | bytes 1474560 | tf_op jit(solution)/shard_map/reduce_scatter | solution.py:76
  (259 other events, 3194.0 us)
Sparse Core Ops, SparseCore 0:
  11.6 31.0 all-gather.15
  56.7 26.8 reduce-scatter.13
  86.7 30.6 all-gather.17
  124.8 26.8 reduce-scatter.15
  163.5 31.7 all-gather.19
  221.4 26.8 reduce-scatter.17
  251.3 30.6 all-gather.21
  289.4 26.8 reduce-scatter.19
  329.2 31.7 all-gather.25
  393.4 26.8 reduce-scatter.21
  423.4 30.6 all-gather.27
  461.4 26.8 reduce-scatter.23
  490.4 30.6 all-gather.23
  523.1 29.5 all-gather.29
  556.3 16.3 all-gather.31
  745.8 24.9 reduce-scatter.25
  776.9 29.9 all-gather.33
  814.6 26.8 reduce-scatter.27
  847.4 30.6 all-gather.35
  910.5 26.8 reduce-scatter.29
  953.9 29.7 all-gather.37
  991.6 26.8 reduce-scatter.31
  1023.3 30.7 all-gather.39
  1088.6 26.8 reduce-scatter.33
  1133.5 29.8 all-gather.41
  1171.1 26.7 reduce-scatter.35
  1202.4 30.8 all-gather.43
  1239.4 127.0 all-reduce.4
  1370.0 75.0 all-reduce.6
  1447.2 27.3 reduce-scatter.37
where the time goes:
time: 1540 us; the launch traced here: 1530 us
  waiting for transfers between devices  890 us (58%)
  matrix products  196 us (13%)
  local copies, waits for them, and re-layouts  189 us (12%)
  other arithmetic  182 us (12%)
  blocking collectives  41.9 us (3%)
  between operations  18.1 us (1%)
    all_gather x8, waiting for transfers between devices, gather_rows(): return lax.all_gather(values, 'mp', axis=0, tiled=True)  224 us
    reduce_scatter x6, waiting for transfers between devices, spread_rows(): lax.psum_scatter(values.astype(jnp.bfloat16), 'mp', scatter_dimension=0,...  161 us
    reduce_scatter x6, waiting for transfers between devices, spread_grads(): lax.psum_scatter(values.astype(jnp.bfloat16), 'mp', scatter_dimension=0,...  155 us
    all_gather x6, waiting for transfers between devices, gather_grads(): return lax.all_gather(values, 'mp', axis=0, tiled=True)  153 us
    psum x1, waiting for transfers between devices, on_device(): lax.psum((gain_rows, table_full, head_gain, proj_part, loss_share), ('sec...  100 us
    scatter-add x1, other arithmetic, on_device(): dense_grads = jnp.zeros(doc_pool.shape, jnp.float32).at[flat_index].add(g...  89.1 us
    gather x1, local copies, waits for them, and re-layouts, on_device(): jnp.take(doc_pool, flat_index, axis=0)  56.7 us
    psum x1, blocking collectives, on_device(): lax.psum((gain_rows, table_full, head_gain, proj_part, loss_share), ('sec...  41.9 us
  transfers between devices with their start and end apart: 34, of which 34 were waited for; matrix products, arithmetic and copies ran while one was open for 9% of the time, Pallas kernels for 0%

commit v1 on v0

v1 whole, which is shorter than its diff:
```python
import functools

import jax
import jax.numpy as jnp
from jax import lax
from jax.experimental import pallas as pl
from jax.experimental.pallas import tpu as pltpu
from jax.sharding import PartitionSpec as P

D = 768
HEAD_DIM = 64
FF = 2048
PROJ = 128
DOC_LEN = 512
QRY_LEN = 32
QRYS_MB = 8
QRY_ROWS = QRYS_MB * QRY_LEN
MP = 4
QUARTER = D // MP
FQ = FF // MP
HEADS_Q = QUARTER // HEAD_DIM
BLK = 128
NBLK = DOC_LEN // BLK

bucket_edges = (8, 12, 16, 23, 32, 46, 64, 91)
norm_eps = 1e-06
logit_scale = 16.0
highest = lax.Precision.HIGHEST
f32 = jnp.float32
bf16 = jnp.bfloat16

ACT, IS_DOC, ZPOS, RPOS = range(4)
VMEM_LIMIT = 56 * 1024 * 1024


def mm(a, b):
    return jnp.dot(a, b, preferred_element_type=f32)


def mm_t(a, b):
    return lax.dot_general(a, b, (((1,), (1,)), ((), ())), preferred_element_type=f32)


def t_mm(a, b):
    return lax.dot_general(a, b, (((0,), (0,)), ((), ())), preferred_element_type=f32)


def bucket_of(offset, half_count):
    spread = jnp.abs(offset)
    far_bucket = 7 + sum((spread >= edge).astype(jnp.int32) for edge in bucket_edges)
    near_bucket = jnp.where(spread < 8, spread, far_bucket)
    return near_bucket + half_count * (offset > 0).astype(jnp.int32)


def start_weight_copies(flags, groups, sem):
    z0 = flags[ZPOS]
    r0 = flags[RPOS]
    copies = []
    at = 0
    for owns, slots, place_own, place in groups:
        for k, own in enumerate(owns):
            copies.append(pltpu.make_async_copy(own, place_own(z0, k), sem.at[at]))
            at += 1
        for j, (slot, rbit) in enumerate(zip(slots, (0, 2, 1, 3))):
            for i, zbit in enumerate((2, 1, 3)):
                for src, dst in place(slot.at[i], z0 ^ zbit, r0 ^ rbit):
                    copies.append(pltpu.make_async_copy(src, dst, sem.at[at]))
                    at += 1
    for copy in copies:
        copy.start()
    return copies


def rows_at(index, size):
    return pl.ds(pl.multiple_of(index * size, size), size)


def qkv_group(own, slots, wa):
    return (
        (own,),
        slots,
        lambda z, k: wa.at[z],
        lambda src, z, r: [(src, wa.at[z, rows_at(r, QUARTER), :])],
    )


def ffn_group(own_gate, own_up, slots, wg):
    return (
        (own_gate, own_up),
        slots,
        lambda z, k: wg.at[z, :, pl.ds(k * FQ, FQ)],
        lambda src, z, r: [(src, wg.at[z, rows_at(r, QUARTER), :])],
    )


def down_group(own_down, own_out, slots, wd, wo):
    return (
        (own_down, own_out),
        slots,
        lambda z, k: wd.at[z] if k == 0 else wo.at[z],
        lambda src, z, r: [
            (src.at[pl.ds(0, FQ // 4), :], wd.at[z, rows_at(r, FQ // 4), :]),
            (src.at[pl.ds(FQ // 4, QUARTER // 4), :], wo.at[z, rows_at(r, QUARTER // 4), :]),
        ],
    )


def bias_matrix(bias_ref, table_ref, head, heads):
    far_up = jnp.full((BLK, BLK), table_ref[31, head], f32)
    far_low = jnp.full((BLK, BLK), table_ref[15, head], f32)
    near = {0: bias_ref[head, 0], 1: bias_ref[head, 1], -1: bias_ref[head, 2]}

    def block(bj, bi):
        if bj - bi in near:
            return near[bj - bi]
        return far_up if bj > bi else far_low

    return jnp.concatenate(
        [jnp.concatenate([block(bj, bi) for bi in range(NBLK)], axis=1) for bj in range(NBLK)], axis=0
    )


def rms_parts(values):
    return lax.rsqrt(jnp.mean(values * values, axis=-1, keepdims=True) + norm_eps)


def rms_back(values, gain, grad):
    scale = rms_parts(values)
    weighted = grad * gain
    inner = jnp.mean(values * weighted, axis=-1, keepdims=True)
    out = scale * (weighted - values * (scale * scale * inner))
    gain_grad = jnp.sum(grad * values * scale, axis=0, keepdims=True)
    return out, gain_grad


def attn_fwd_kernel(
    flags, table, x_ref, gain_ref, bias_ref, own, s0, s1, s2, s3,
    normed_ref, qkv_ref, lse_ref, mixed_ref, wa, sem,
):
    heads = MP * HEADS_Q
    copies = start_weight_copies(flags, [qkv_group(own, (s0, s1, s2, s3), wa)], sem)
    x = x_ref[...].astype(f32)
    normed_ref[...] = (x * rms_parts(x) * gain_ref[...]).astype(bf16)
    for copy in copies:
        copy.wait()

    @pl.loop(0, MP)
    def _(z):
        qkv_ref[z] = mm(normed_ref[...], wa[z]).astype(bf16)

    def one_head(z, hh, rows, bias):
        at = hh * HEAD_DIM
        q = qkv_ref[z, rows, at : at + HEAD_DIM]
        k = qkv_ref[z, rows, QUARTER + at : QUARTER + at + HEAD_DIM]
        v = qkv_ref[z, rows, 2 * QUARTER + at : 2 * QUARTER + at + HEAD_DIM]
        scores = mm_t(k, q) + bias
        peak = jnp.max(scores, axis=0, keepdims=True)
        weights = jnp.exp(scores - peak)
        total = jnp.sum(weights, axis=0, keepdims=True)
        mixed = t_mm(v, weights.astype(bf16)) * (1.0 / total)
        lse_ref[z, hh : hh + 1, rows] = peak + jnp.log(total)
        mixed_ref[z, rows, at : at + HEAD_DIM] = mixed.T.astype(bf16)

    @pl.when(flags[IS_DOC] == 1)
    def _():
        @pl.loop(0, MP)
        def _(z):
            for hh in range(HEADS_Q):
                one_head(z, hh, slice(0, DOC_LEN), bias_matrix(bias_ref, table, z * HEADS_Q + hh, heads))

    @pl.when(flags[IS_DOC] == 0)
    def _():
        mixed_ref[...] = jnp.zeros_like(mixed_ref)
        lse_ref[...] = jnp.zeros_like(lse_ref)

        @pl.loop(0, MP)
        def _(z):
            for hh in range(HEADS_Q):
                for b in range(QRY_ROWS // BLK):
                    one_head(z, hh, slice(b * BLK, (b + 1) * BLK), bias_ref[z * HEADS_Q + hh, 0])


def ffn_fwd_kernel(
    flags, x_ref, mixed_ref, gain_ref, own_gate, own_up, g0, g1, g2, g3, own_down, own_out, d0, d1, d2, d3,
    out_ref, middle_ref, normed_ref, hidden_ref, ga_ref, gb_ref, wg, wd, wo, sem,
):
    copies = start_weight_copies(
        flags,
        [
            down_group(own_down, own_out, (d0, d1, d2, d3), wd, wo),
            ffn_group(own_gate, own_up, (g0, g1, g2, g3), wg),
        ],
        sem,
    )
    for copy in copies:
        copy.wait()
    middle = x_ref[...].astype(f32)
    for z in range(MP):
        middle = middle + mm(mixed_ref[z], wo[z])
    middle_ref[...] = middle
    normed_ref[...] = (middle * rms_parts(middle) * gain_ref[...]).astype(bf16)
    out_ref[...] = middle

    @pl.loop(0, MP)
    def _(z):
        normed = normed_ref[...]
        gate = mm(normed, wg[z, :, :FQ])
        up = mm(normed, wg[z, :, FQ:])
        coef = 0.7978845608028654
        square = gate * gate
        tanh = jnp.tanh(coef * gate * (1.0 + 0.044715 * square))
        half = 0.5 + 0.5 * tanh
        gelu = gate * half
        slope = half + (0.5 * coef) * gate * (1.0 - tanh * tanh) * (1.0 + 3 * 0.044715 * square)
        hidden = (gelu * up).astype(bf16)
        hidden_ref[z] = hidden
        ga_ref[z] = (up * slope).astype(bf16)
        gb_ref[z] = gelu.astype(bf16)
        out_ref[...] += mm(hidden, wd[z])


def ffn_bwd_kernel(
    flags, gout_ref, middle_ref, gain_ref, normed_ref, hidden_ref, ga_ref, gb_ref,
    own_gate, own_up, g0, g1, g2, g3, own_down, own_out, d0, d1, d2, d3,
    *refs,
):
    prev, refs = refs[:-16], refs[-16:]
    gmid_ref, dgain_ref, dgk, dgs, ddk, dds, wg, wd, wo, goutb, normed_t, dg_buf, dd_buf, gn, sem, osem = refs

    @pl.when(flags[ACT] == 0)
    def _():
        dgain_ref[...] = prev[0][...] if prev else jnp.zeros_like(dgain_ref)
        gmid_ref[...] = jnp.zeros_like(gmid_ref)

    @pl.when(flags[ACT] == 1)
    def _():
        core = flags[RPOS] % 2
        copies = start_weight_copies(
            flags,
            [
                down_group(own_down, own_out, (d0, d1, d2, d3), wd, wo),
                ffn_group(own_gate, own_up, (g0, g1, g2, g3), wg),
            ],
            sem,
        )
        goutb[...] = gout_ref[...].astype(bf16)
        normed_t[...] = normed_ref[...].T
        gn[...] = jnp.zeros_like(gn)
        for copy in copies:
            copy.wait()

        def outs(z):
            half_g, half_d = D // 2, FQ // 2
            return (
                pltpu.make_async_copy(dg_buf.at[z % 2, rows_at(core, half_g), :], dgk.at[z], osem.at[z % 2, 0]),
                pltpu.make_async_copy(dg_buf.at[z % 2, rows_at(1 - core, half_g), :], dgs.at[z], osem.at[z % 2, 1]),
                pltpu.make_async_copy(dd_buf.at[z % 2, rows_at(core, half_d), :], ddk.at[z], osem.at[z % 2, 2]),
                pltpu.make_async_copy(dd_buf.at[z % 2, rows_at(1 - core, half_d), :], dds.at[z], osem.at[z % 2, 3]),
            )

        for z in range(MP):
            if z >= 2:
                for copy in outs(z - 2):
                    copy.wait()
            grad_hidden = mm_t(goutb[...], wd[z])
            grad_gate = (grad_hidden * ga_ref[z].astype(f32)).astype(bf16)
            grad_up = (grad_hidden * gb_ref[z].astype(f32)).astype(bf16)
            dd_buf[z % 2] = t_mm(hidden_ref[z], goutb[...]).astype(bf16)
            dg_buf[z % 2, :, :FQ] = mm(normed_t[...], grad_gate).astype(bf16)
            dg_buf[z % 2, :, FQ:] = mm(normed_t[...], grad_up).astype(bf16)
            for copy in outs(z):
                copy.start()
            gn[...] += mm_t(grad_gate, wg[z, :, :FQ]) + mm_t(grad_up, wg[z, :, FQ:])
        back, gain_grad = rms_back(middle_ref[...], gain_ref[...], gn[...])
        gmid_ref[...] = gout_ref[...] + back
        dgain_ref[...] = gain_grad
        for z in (MP - 2, MP - 1):
            for copy in outs(z):
                copy.wait()


def attn_bwd_kernel(
    flags, table, gmid_ref, x_ref, gain_ref, bias_ref, normed_ref, qkv_ref, lse_ref, mixed_ref,
    own, s0, s1, s2, s3, own_out, d0, d1, d2, d3,
    *refs,
):
    prev, refs = refs[:-18], refs[-18:]
    gx_ref, dgain_ref, diag_ref, dak, das, dok, dos = refs[:7]
    wa, wo, gmb, normed_t, gmix, gqkv, da_buf, do_buf, gn, sem, osem = refs[7:]
    heads = MP * HEADS_Q

    @pl.when(flags[ACT] == 0)
    def _():
        for at, ref in enumerate((gx_ref, dgain_ref, diag_ref)):
            ref[...] = prev[at][...] if prev else jnp.zeros_like(ref)

    def out_group():
        return (
            (own_out,),
            (d0, d1, d2, d3),
            lambda z, k: wo.at[z],
            lambda src, z, r: [(src.at[pl.ds(FQ // 4, QUARTER // 4), :], wo.at[z, rows_at(r, QUARTER // 4), :])],
        )

    def one_head(z, hh, rows, bias):
        at = hh * HEAD_DIM
        q = qkv_ref[z, rows, at : at + HEAD_DIM]
        k = qkv_ref[z, rows, QUARTER + at : QUARTER + at + HEAD_DIM]
        v = qkv_ref[z, rows, 2 * QUARTER + at : 2 * QUARTER + at + HEAD_DIM]
        go = gmix[rows, at : at + HEAD_DIM]
        out = mixed_ref[z, rows, at : at + HEAD_DIM].astype(f32)
        delta = jnp.sum((go.astype(f32) * out).T, axis=0, keepdims=True)
        probs = jnp.exp(mm_t(k, q) + bias - lse_ref[z, hh : hh + 1, rows])
        grad_probs = mm_t(v, go)
        grad_scores = probs * (grad_probs - delta)
        low = grad_scores.astype(bf16)
        gqkv[z, rows, at : at + HEAD_DIM] = t_mm(k, low).T.astype(bf16)
        gqkv[z, rows, QUARTER + at : QUARTER + at + HEAD_DIM] = mm(low, q).astype(bf16)
        gqkv[z, rows, 2 * QUARTER + at : 2 * QUARTER + at + HEAD_DIM] = mm(probs.astype(bf16), go).astype(bf16)
        return grad_scores

    def band_sums(up, mid, low):
        blank = jnp.zeros((BLK, BLK), f32)
        band = jnp.concatenate([up, mid, low, blank], axis=1)
        width = 4 * BLK

        def left(part, by):
            return pltpu.roll(part, width - by, 1) if by else part

        eight = functools.reduce(jnp.add, [left(band[g : g + 8], g) for g in range(0, BLK, 8)])
        return functools.reduce(jnp.add, [left(eight[r : r + 1], r) for r in range(8)])

    @pl.when(flags[ACT] == 1)
    def _():
        core = flags[RPOS] % 2
        copies = start_weight_copies(
            flags, [out_group(), qkv_group(own, (s0, s1, s2, s3), wa)], sem
        )
        gmb[...] = gmid_ref[...].astype(bf16)
        normed_t[...] = normed_ref[...].T
        gn[...] = jnp.zeros_like(gn)
        for copy in copies:
            copy.wait()

        def outs(z):
            half_a, half_o = D // 2, QUARTER // 2
            return (
                pltpu.make_async_copy(da_buf.at[z % 2, rows_at(core, half_a), :], dak.at[z], osem.at[z % 2, 0]),
                pltpu.make_async_copy(da_buf.at[z % 2, rows_at(1 - core, half_a), :], das.at[z], osem.at[z % 2, 1]),
                pltpu.make_async_copy(do_buf.at[z % 2, rows_at(core, half_o), :], dok.at[z], osem.at[z % 2, 2]),
                pltpu.make_async_copy(do_buf.at[z % 2, rows_at(1 - core, half_o), :], dos.at[z], osem.at[z % 2, 3]),
            )

        for z in range(MP):
            if z >= 2:
                for copy in outs(z - 2):
                    copy.wait()
            gmix[...] = mm_t(gmb[...], wo[z]).astype(bf16)
            do_buf[z % 2] = t_mm(mixed_ref[z], gmb[...]).astype(bf16)

            @pl.when(flags[IS_DOC] == 1)
            def _():
                for hh in range(HEADS_Q):
                    grads = one_head(
                        z, hh, slice(0, DOC_LEN), bias_matrix(bias_ref, table, z * HEADS_Q + hh, heads)
                    )

                    def blocks(test):
                        picked = [
                            grads[bj * BLK : (bj + 1) * BLK, bi * BLK : (bi + 1) * BLK]
                            for bj in range(NBLK)
                            for bi in range(NBLK)
                            if test(bj - bi)
                        ]
                        return functools.reduce(jnp.add, picked)

                    sums = band_sums(blocks(lambda d: d == 1), blocks(lambda d: d == 0), blocks(lambda d: d == -1))
                    far_up = jnp.sum(blocks(lambda d: d > 1), axis=0, keepdims=True)
                    far_low = jnp.sum(blocks(lambda d: d < -1), axis=0, keepdims=True)
                    diag_ref[z, hh : hh + 1, :] = jnp.concatenate([sums, far_up, far_low], axis=1)

            @pl.when(flags[IS_DOC] == 0)
            def _():
                gqkv[z] = jnp.zeros((DOC_LEN, 3 * QUARTER), bf16)
                for hh in range(HEADS_Q):
                    grads = jnp.zeros((BLK, BLK), f32)
                    for b in range(QRY_ROWS // BLK):
                        grads = grads + one_head(
                            z, hh, slice(b * BLK, (b + 1) * BLK), bias_ref[z * HEADS_Q + hh, 0]
                        )
                    blank = jnp.zeros((BLK, BLK), f32)
                    sums = band_sums(blank, grads, blank)
                    diag_ref[z, hh : hh + 1, :] = jnp.concatenate([sums, jnp.zeros((1, 2 * BLK), f32)], axis=1)

            grads = gqkv[z]
            da_buf[z % 2] = mm(normed_t[...], grads).astype(bf16)
            for copy in outs(z):
                copy.start()
            gn[...] += mm_t(grads, wa[z])
        back, gain_grad = rms_back(x_ref[...].astype(f32), gain_ref[...], gn[...])
        gx_ref[...] = (gmid_ref[...] + back).astype(bf16)
        dgain_ref[...] = gain_grad
        for z in (MP - 2, MP - 1):
            for copy in outs(z):
                copy.wait()


def vmem():
    return pl.BlockSpec(memory_space=pltpu.VMEM)


def smem():
    return pl.BlockSpec(memory_space=pltpu.SMEM)


def hbm():
    return pl.BlockSpec(memory_space=pl.ANY)


def shape(dims, kind):
    return jax.ShapeDtypeStruct(dims, kind)


def params():
    return pltpu.CompilerParams(vmem_limit_bytes=VMEM_LIMIT)


def attn_fwd(flags, table, x, gain, bias, wa_parts):
    return pl.pallas_call(
        attn_fwd_kernel,
        in_specs=[smem(), smem()] + [vmem()] * 3 + [hbm()] * 5,
        out_specs=[vmem()] * 4,
        out_shape=[
            shape((DOC_LEN, D), bf16),
            shape((MP, DOC_LEN, 3 * QUARTER), bf16),
            shape((MP, 8, DOC_LEN), f32),
            shape((MP, DOC_LEN, QUARTER), bf16),
        ],
        scratch_shapes=[pltpu.VMEM((MP, D, 3 * QUARTER), bf16), pltpu.SemaphoreType.DMA((13,))],
        compiler_params=params(),
        name="attn_fwd",
    )(flags, table, x, gain, bias, *wa_parts)


def ffn_fwd(flags, x, mixed, gain, wg_parts, wd_parts):
    quarter = (MP, DOC_LEN, FQ)
    return pl.pallas_call(
        ffn_fwd_kernel,
        in_specs=[smem()] + [vmem()] * 3 + [hbm()] * 12,
        out_specs=[vmem()] * 6,
        out_shape=[
            shape((DOC_LEN, D), f32),
            shape((DOC_LEN, D), f32),
            shape((DOC_LEN, D), bf16),
            shape(quarter, bf16),
            shape(quarter, bf16),
            shape(quarter, bf16),
        ],
        scratch_shapes=[
            pltpu.VMEM((MP, D, 2 * FQ), bf16),
            pltpu.VMEM((MP, FQ, D), bf16),
            pltpu.VMEM((MP, QUARTER, D), bf16),
            pltpu.SemaphoreType.DMA((40,)),
        ],
        compiler_params=params(),
        name="ffn_fwd",
    )(flags, x, mixed, gain, *wg_parts, *wd_parts)


def ffn_bwd(flags, gout, middle, gain, normed, hidden, ga, gb, wg_parts, wd_parts, prev):
    n_in = 8 + 12
    big = [
        shape((MP, D // 2, 2 * FQ), bf16),
        shape((MP, D // 2, 2 * FQ), bf16),
        shape((MP, FQ // 2, D), bf16),
        shape((MP, FQ // 2, D), bf16),
    ]
    prev = prev or []
    return pl.pallas_call(
        ffn_bwd_kernel,
        in_specs=[smem()] + [vmem()] * 7 + [hbm()] * 12 + ([vmem()] + [hbm()] * 4 if prev else []),
        out_specs=[vmem()] * 2 + [hbm()] * 4,
        out_shape=[shape((DOC_LEN, D), f32), shape((1, D), f32)] + big,
        input_output_aliases={n_in + 1 + i: 2 + i for i in range(4)} if prev else {},
        scratch_shapes=[
            pltpu.VMEM((MP, D, 2 * FQ), bf16),
            pltpu.VMEM((MP, FQ, D), bf16),
            pltpu.VMEM((MP, QUARTER, D), bf16),
            pltpu.VMEM((DOC_LEN, D), bf16),
            pltpu.VMEM((D, DOC_LEN), bf16),
            pltpu.VMEM((2, D, 2 * FQ), bf16),
            pltpu.VMEM((2, FQ, D), bf16),
            pltpu.VMEM((DOC_LEN, D), f32),
            pltpu.SemaphoreType.DMA((40,)),
            pltpu.SemaphoreType.DMA((2, 4)),
        ],
        compiler_params=params(),
        name="ffn_bwd",
    )(flags, gout, middle, gain, normed, hidden, ga, gb, *wg_parts, *wd_parts, *prev)


def attn_bwd(flags, table, gmid, x, gain, bias, normed, qkv, lse, mixed, wa_parts, wo_parts, prev):
    n_in = 10 + 10
    small = [shape((DOC_LEN, D), bf16), shape((1, D), f32), shape((MP, 8, 6 * BLK), f32)]
    big = [
        shape((MP, D // 2, 3 * QUARTER), bf16),
        shape((MP, D // 2, 3 * QUARTER), bf16),
        shape((MP, QUARTER // 2, D), bf16),
        shape((MP, QUARTER // 2, D), bf16),
    ]
    prev = prev or []
    return pl.pallas_call(
        attn_bwd_kernel,
        in_specs=[smem()] * 2 + [vmem()] * 8 + [hbm()] * 10 + ([vmem()] * 3 + [hbm()] * 4 if prev else []),
        out_specs=[vmem()] * 3 + [hbm()] * 4,
        out_shape=small + big,
        input_output_aliases={n_in + 3 + i: 3 + i for i in range(4)} if prev else {},
        scratch_shapes=[
            pltpu.VMEM((MP, D, 3 * QUARTER), bf16),
            pltpu.VMEM((MP, QUARTER, D), bf16),
            pltpu.VMEM((DOC_LEN, D), bf16),
            pltpu.VMEM((D, DOC_LEN), bf16),
            pltpu.VMEM((DOC_LEN, QUARTER), bf16),
            pltpu.VMEM((MP, DOC_LEN, 3 * QUARTER), bf16),
            pltpu.VMEM((2, D, 3 * QUARTER), bf16),
            pltpu.VMEM((2, QUARTER, D), bf16),
            pltpu.VMEM((DOC_LEN, D), f32),
            pltpu.SemaphoreType.DMA((26,)),
            pltpu.SemaphoreType.DMA((2, 4)),
        ],
        compiler_params=params(),
        name="attn_bwd",
    )(flags, table, gmid, x, gain, bias, normed, qkv, lse, mixed, *wa_parts, *wo_parts, *prev)


def swap(values, axis, bit):
    count = lax.axis_size(axis)
    return lax.ppermute(values, axis, [(i, i ^ bit) for i in range(count)])


def gather_pieces(piece):
    far = swap(piece, "mp", 2)
    near = swap(jnp.stack([piece, far]), "mp", 1)
    mine = jnp.concatenate([far[None], near])
    across = swap(mine, "dp", 2)
    return (mine, across, swap(mine, "dp", 1), swap(across, "dp", 1))


def pick(values, axis, index):
    return lax.dynamic_index_in_dim(values, index, axis, keepdims=False)


def add_low(a, b):
    return (a.astype(f32) + b.astype(f32)).astype(bf16)


def split_step(values, dim, axis, bit, mine):
    return add_low(pick(values, dim, mine), swap(pick(values, dim, 1 - mine), axis, bit))


def join_step(values, axis, bit, mine):
    other = swap(values, axis, bit)
    return jnp.where(mine == 0, jnp.stack([values, other]), jnp.stack([other, values]))


def reduce_chunk(keep, send, place, y_first):
    core, y, z = place
    total = add_low(keep, swap(send, "dp", 1))
    total = total.reshape(2, 2, 2, total.shape[1] // 2, total.shape[2])
    if y_first:
        total = split_step(total, 2, "dp", 2, y)
    total = split_step(total, 1, "mp", 1, z % 2)
    total = split_step(total, 0, "mp", 2, z // 2)
    if not y_first:
        total = add_low(total, swap(total, "dp", 2))
    bit = 4
    while bit < lax.axis_size("dp"):
        total = add_low(total, swap(total, "dp", bit))
        bit *= 2
    if y_first:
        total = join_step(total, "dp", 2, y)
    return join_step(total, "dp", 1, core)


def spread_tokens(tokens, place, pairs):
    core, _, z = place
    got = []
    for turn in range(2):
        perm = []
        for j in range(pairs):
            for c in range(2):
                for zz in range(MP):
                    u = (turn + zz) % 2
                    perm.append(((2 * j + c) * MP + zz, (2 * j + zz // 2) * MP + 2 * c + u))
        block = pick(tokens, 0, (turn + z) % 2)
        got.append(lax.ppermute(block, ("dp", "mp"), perm))
    low, high = jnp.where(z % 2 == 0, jnp.stack(got), jnp.stack(got[::-1]))
    cut = DOC_LEN - 2 * QUARTER
    tail = swap(low[:cut], "dp", 1)
    doc = jnp.concatenate([low, high, tail])
    qry = jnp.concatenate([low[cut:], high, jnp.zeros((DOC_LEN - QRY_ROWS, D), low.dtype)])
    return jnp.where(core == 0, doc, qry)


def collect_rows(rows, place, pairs):
    core, _, z = place
    cut = DOC_LEN - 2 * QUARTER
    tail = swap(rows[2 * QUARTER :], "dp", 1)
    low_q = jnp.concatenate([tail, rows[: QUARTER - cut]])
    high_q = rows[QUARTER - cut : QRY_ROWS]
    low = jnp.where(core == 0, rows[:QUARTER], low_q)
    high = jnp.where(core == 0, rows[QUARTER : 2 * QUARTER], high_q)
    got = []
    for turn in range(2):
        perm = []
        for j in range(pairs):
            for c in range(2):
                for zz in range(MP):
                    u = (turn + zz) % 2
                    perm.append(((2 * j + zz // 2) * MP + 2 * c + u, (2 * j + c) * MP + zz))
        block = jnp.where((z + turn) % 2 == 0, low, high)
        got.append(lax.ppermute(block, ("dp", "mp"), perm))
    return jnp.where(z % 2 == 0, jnp.stack(got), jnp.stack(got[::-1]))


def gather_slots(values, steps):
    for axis, bit in steps:
        values = jnp.concatenate([values, swap(values, axis, bit)])
    return values


def scatter_slots(values, steps):
    for axis, bit in reversed(steps):
        half = values.shape[0] // 2
        values = add_low(values[:half], swap(values[half:], axis, bit))
    return values[0]


def on_device(
    tokens,
    attn_gain,
    w_query,
    w_key,
    w_value,
    w_out,
    ffn_gain,
    w_gate,
    w_up,
    w_down,
    rel_table,
    final_gain,
    w_proj,
    positives,
    retrieved,
):
    section = lax.axis_index("section")
    dp = lax.axis_index("dp")
    dp_count = lax.axis_size("dp")
    z = lax.axis_index("mp")
    core, y = dp % 2, (dp // 2) % 2
    place = (core, y, z)
    pairs = dp_count // 2
    chip = (dp // 2) * MP + z
    chips = pairs * MP
    is_doc = core == 0
    first = section == 0
    quad = dp % 4

    qkv_own = jnp.concatenate([w_query[0], w_key[0], w_value[0]], axis=1)
    qkv_piece = lax.dynamic_slice_in_dim(qkv_own, quad * QUARTER, QUARTER, 0)
    gate_piece = jnp.concatenate(
        [lax.dynamic_slice_in_dim(w[0], quad * QUARTER, QUARTER, 0) for w in (w_gate, w_up)], axis=1
    )
    down_piece = jnp.concatenate(
        [
            lax.dynamic_slice_in_dim(w_down[0], quad * (FQ // 4), FQ // 4, 0),
            lax.dynamic_slice_in_dim(w_out[0], quad * (QUARTER // 4), QUARTER // 4, 0),
        ]
    )
    x_first = spread_tokens(tokens, place, pairs)
    wa_parts = (qkv_own,) + gather_pieces(qkv_piece)
    down_slots = gather_pieces(down_piece)
    wg_parts = (w_gate[0], w_up[0]) + gather_pieces(gate_piece)
    wd_parts = (w_down[0], w_out[0]) + down_slots
    wo_parts = (w_out[0],) + down_slots

    heads_dev = rel_table.shape[1]
    buckets = rel_table.shape[0]
    half_count = buckets // 2
    table = lax.all_gather(rel_table, "mp", axis=1, tiled=True)
    at = jnp.arange(BLK, dtype=jnp.int32)
    offset = at[:, None] - at[None, :]
    offsets = jnp.stack([offset, offset + BLK, offset - BLK])
    bucket_ids = jnp.arange(buckets, dtype=jnp.int32)
    pick_near = (bucket_of(offsets, half_count)[..., None] == bucket_ids).astype(f32)
    bias = jnp.einsum("bh,mjib->hmji", table, pick_near, precision=highest)
    same_query = (at[:, None] // QRY_LEN) == (at[None, :] // QRY_LEN)
    bias = jnp.where(jnp.logical_or(is_doc, same_query), bias, -1e30)

    def flags_for(active):
        return jnp.stack([jnp.asarray(active).astype(jnp.int32), is_doc.astype(jnp.int32), z, quad])

    slot_ids = jnp.arange(chips, dtype=jnp.int32)
    mb_of_slot = chip ^ slot_ids
    all_retrieved = lax.all_gather(retrieved, "dp", axis=0, tiled=True)
    all_positives = lax.all_gather(positives, "dp", axis=0, tiled=True)
    topk = retrieved.shape[2]
    slot_retrieved = jnp.take(all_retrieved.reshape(chips, QRY_ROWS, topk), mb_of_slot, axis=0)
    places = jnp.arange(DOC_LEN, dtype=jnp.int32) + chip * DOC_LEN
    counts = jnp.sum(
        (slot_retrieved.reshape(-1, topk)[:, :, None] == places).astype(f32), axis=1
    )

    flags_f = flags_for(1)
    kept = []
    x = x_first
    for step in range(2):
        normed, qkv, lse, mixed = attn_fwd(flags_f, table, x, attn_gain, bias, wa_parts)
        out, middle, normed_ffn, hidden, ga, gb = ffn_fwd(flags_f, x, mixed, ffn_gain, wg_parts, wd_parts)
        kept.append((x, normed, qkv, lse, mixed, middle, normed_ffn, hidden, ga, gb))
        if step == 0:
            x = lax.ppermute(out.astype(bf16), "section", [(0, 1)])

    scale = PROJ ** (-0.5)
    normed_final = (out * rms_parts(out) * final_gain).astype(bf16)
    embed = mm(normed_final, w_proj).astype(bf16)
    steps = [("mp", 1), ("mp", 2)]
    bit = 2
    while bit < dp_count:
        steps.append(("dp", bit))
        bit *= 2
    query_slots = swap(gather_slots(embed[None, :QRY_ROWS], steps), "dp", 1).reshape(-1, PROJ)
    sims = mm_t(query_slots, embed)
    weighted = jnp.exp(sims * scale) * counts
    mass = jnp.sum(weighted, axis=1)
    logit = logit_scale * jnp.mean(jnp.log1p(mass).reshape(chips * QRYS_MB, QRY_LEN), axis=1)
    logit = jnp.take(logit.reshape(chips, QRYS_MB), mb_of_slot, axis=0).reshape(1, -1)
    logits = gather_slots(logit, steps)
    chosen = jnp.any(all_positives[None] == mb_of_slot[:, None, None], axis=2).astype(f32)
    peak = jnp.max(logits, axis=0)
    spread = jnp.exp(logits - peak)
    all_total = jnp.sum(spread, axis=0)
    pos_total = jnp.sum(chosen * spread, axis=0)
    n_queries = logits.shape[1]
    loss_here = jnp.sum(jnp.log(all_total) - jnp.log(pos_total)) / n_queries
    grad_logit = (spread[0] / all_total - chosen[0] * spread[0] / pos_total) / n_queries
    grad_logit = jnp.take(grad_logit.reshape(chips, QRYS_MB), mb_of_slot, axis=0).reshape(-1)
    coef = jnp.repeat(grad_logit * (logit_scale / QRY_LEN * scale), QRY_LEN) / (1.0 + mass)
    grad_sims = (weighted * coef[:, None]).astype(bf16)
    grad_doc = t_mm(grad_sims, query_slots).astype(bf16)
    grad_query = mm(grad_sims, embed).astype(bf16).reshape(chips, QRY_ROWS, PROJ)
    grad_query = scatter_slots(swap(grad_query, "dp", 1), steps)
    grad_query = jnp.concatenate([grad_query, jnp.zeros((DOC_LEN - QRY_ROWS, PROJ), bf16)])
    grad_embed = jnp.where(is_doc, grad_doc, grad_query)
    grad_proj = t_mm(normed_final, grad_embed)
    grad_final, grad_final_gain = rms_back(out, final_gain, mm_t(grad_embed, w_proj))
    live = jnp.logical_not(first)
    lead = jnp.logical_and(live, jnp.logical_and(dp == 0, z == 0))
    early = jnp.concatenate(
        [
            jnp.where(live, grad_proj, 0.0),
            jnp.where(live, grad_final_gain, 0.0).reshape(-1, PROJ),
            jnp.full((2, PROJ), jnp.where(lead, loss_here, 0.0)),
        ]
    )
    early = lax.psum(early, ("section", "dp", "mp"))

    grad_out = grad_final
    ffn_prev = attn_prev = None
    for step in (1, 0):
        x, normed, qkv, lse, mixed, middle, normed_ffn, hidden, ga, gb = kept[step]
        flags_b = flags_for(section == step)
        gmid, *ffn_prev = ffn_bwd(
            flags_b, grad_out, middle, ffn_gain, normed_ffn, hidden, ga, gb, wg_parts, wd_parts, ffn_prev
        )
        attn_prev = attn_bwd(
            flags_b, table, gmid, x, attn_gain, bias, normed, qkv, lse, mixed, wa_parts, wo_parts, attn_prev
        )
        if step == 1:
            grad_out = lax.ppermute(attn_prev[0], "section", [(1, 0)]).astype(f32)
    grad_ffn_gain, dgk, dgs, ddk, dds = ffn_prev
    gx, grad_attn_gain, diag, dak, das, dok, dos = attn_prev

    sum_gate = reduce_chunk(dgk, dgs, place, True).reshape(D, 2 * FQ)
    sum_down = reduce_chunk(ddk, dds, place, False).reshape(FQ, D)
    lanes = jnp.arange(4 * BLK, dtype=jnp.int32)
    band_offset = jnp.where(lanes <= 2 * BLK + BLK - 1, BLK - lanes, 5 * BLK - lanes)
    band_bucket = jnp.concatenate(
        [
            bucket_of(band_offset, half_count),
            jnp.full((BLK,), buckets - 1, jnp.int32),
            jnp.full((BLK,), half_count - 1, jnp.int32),
        ]
    )
    pick_band = (band_bucket[:, None] == bucket_ids).astype(f32)
    table_part = jnp.einsum("zhc,cb->zhb", diag[:, :heads_dev], pick_band, precision=highest)
    table_part = table_part + swap(table_part, "section", 1)
    small = jnp.concatenate(
        [
            jnp.broadcast_to(grad_attn_gain[None], (MP, 1, D)),
            jnp.broadcast_to(grad_ffn_gain[None], (MP, 1, D)),
            jnp.pad(table_part.reshape(MP, 1, -1), ((0, 0), (0, 0), (0, D - heads_dev * buckets))),
            jnp.zeros((MP, 13, D), f32),
        ],
        axis=1,
    ).astype(bf16)
    small = jnp.broadcast_to(small[:, None], (MP, 2, 16, D))

    def with_small(values):
        parts = values.reshape(MP, 2, QUARTER // 4, D)
        return jnp.concatenate([parts, small], axis=2).reshape(MP, -1, D)

    sum_out = reduce_chunk(with_small(dok), with_small(dos), place, False)
    sum_qkv = reduce_chunk(dak, das, place, True).reshape(D, 3 * QUARTER).astype(f32)
    small_sum = sum_out[0, 0, QUARTER // 4 :].astype(f32)
    sum_out = sum_out[:, :, : QUARTER // 4].reshape(QUARTER, D).astype(f32)
    grad_table = small_sum[2, : heads_dev * buckets].reshape(heads_dev, buckets).T
    d_inputs = collect_rows(gx, place, pairs)[None]
    col_width = w_proj.shape[1] // MP
    sum_gate = sum_gate.astype(f32)
    return (
        early[-1, 0],
        d_inputs,
        small_sum[0:1],
        sum_qkv[None, :, :QUARTER],
        sum_qkv[None, :, QUARTER : 2 * QUARTER],
        sum_qkv[None, :, 2 * QUARTER :],
        sum_out[None],
        small_sum[1:2],
        sum_gate[None, :, :FQ],
        sum_gate[None, :, FQ:],
        sum_down.astype(f32)[None],
        grad_table,
        early[D : D + D // PROJ].reshape(D),
        lax.dynamic_slice_in_dim(early[:D], z * col_width, col_width, 1),
    )


def solution(mesh):
    return jax.shard_map(
        on_device,
        mesh=mesh,
        in_specs=(
            P("dp", "mp", None),
            P("section", None),
            P("section", None, "mp"),
            P("section", None, "mp"),
            P("section", None, "mp"),
            P("section", "mp", None),
            P("section", None),
            P("section", None, "mp"),
            P("section", None, "mp"),
            P("section", "mp", None),
            P(None, "mp"),
            P(),
            P(),
            P("dp", None),
            P("dp", None, None),
        ),
        out_specs=(
            P(),
            P("section", "dp", "mp", None),
            P("section", None),
            P("section", None, "mp"),
            P("section", None, "mp"),
            P("section", None, "mp"),
            P("section", "mp", None),
            P("section", None),
            P("section", None, "mp"),
            P("section", None, "mp"),
            P("section", "mp", None),
            P(None, "mp"),
            P(),
            P(None, "mp"),
        ),
        check_vma=False,
    )
```

time: 1540 us -> 789 us (0.51)
  waiting for transfers between devices: 890 us -> 369 us
  matrix products: 196 us -> 17.2 us
  local copies, waits for them, and re-layouts: 189 us -> 46 us
  Pallas kernels: 0 us -> 136 us
  other arithmetic: 182 us -> 80.1 us
  starting transfers between devices: 12.4 us -> 63.2 us
    all_gather x15 -> x0, waiting for transfers between devices: 385 us -> none  [the longest x8 224 us: gather_rows(): return lax.all_gather(values, 'mp', axis=0, tiled=True)]
    reduce_scatter x13 -> x0, waiting for transfers between devices: 332 us -> none  [the longest x6 161 us: spread_rows(): lax.psum_scatter(values.astype(jnp.bfloat16), 'mp', scatter_dimension=0,...]
    ppermute x4 -> x57, waiting for transfers between devices: 30.3 us -> 247 us  [the longest x51 188 us: swap(): return lax.ppermute(values, axis, [(i, i ^ bit) for i in range(count)])]
    dot_general x117 -> x8, matrix products: 196 us -> 17.2 us  [the longest x2 5.73 us: mm_t(): lax.dot_general(a, b, (((1,), (1,)), ((), ())), preferred_element_type=f32)]
    pallas_call x0 -> x8, Pallas kernels: none -> 136 us  [the longest x2 42.2 us: attn_bwd(): pl.pallas_call(attn_bwd_kernel, in_specs=[smem()] * 2 + [vmem()] * 8 + [h...]
    scatter-add x1 -> x0, other arithmetic: 89.1 us -> none  [on_device(): dense_grads = jnp.zeros(doc_pool.shape, jnp.float32).at[flat_index].add(g...]
    reshape x49 -> x4, local copies, waits for them, and re-layouts: 67.6 us -> 0.84 us  [the longest x1 0.6 us: on_device(): early[D:D + D // PROJ].reshape(D)]
    gather x1 -> x3, local copies, waits for them, and re-layouts: 56.7 us -> 2.71 us  [the longest x1 1.58 us: on_device(): jnp.take(all_retrieved.reshape(chips, QRY_ROWS, topk), mb_of_slot, axis=0)]
  transfers between devices with their start and end apart: 34 -> 58, of which waited for: 34 -> 25; matrix products, arithmetic and copies ran while one was open for 9% -> 14% of each run, Pallas kernels for 0% -> 2%
where the time goes in v1:
time: 789 us; the launch traced here: 776 us
  waiting for transfers between devices  369 us (47%)
  Pallas kernels  136 us (17%)
  other arithmetic  80.1 us (10%)
  starting transfers between devices  63.2 us (8%)
  blocking collectives  48.6 us (6%)
  local copies, waits for them, and re-layouts  46 us (6%)
  matrix products  17.2 us (2%)
  between operations  16.4 us (2%)
    ppermute x51, waiting for transfers between devices, swap(): return lax.ppermute(values, axis, [(i, i ^ bit) for i in range(count)])  188 us
    psum x1, waiting for transfers between devices, on_device(): early = lax.psum(early, ('section', 'dp', 'mp'))  122 us
    ppermute x51, starting transfers between devices, swap(): return lax.ppermute(values, axis, [(i, i ^ bit) for i in range(count)])  48.3 us
    ppermute x1, waiting for transfers between devices, on_device(): grad_out = lax.ppermute(attn_prev[0], 'section', [(1, 0)]).astype(f32)  42.9 us
    pallas_call x2, Pallas kernels, attn_bwd(): pl.pallas_call(attn_bwd_kernel, in_specs=[smem()] * 2 + [vmem()] * 8 + [h...  42.2 us
    pallas_call x2, Pallas kernels, attn_fwd(): pl.pallas_call(attn_fwd_kernel, in_specs=[smem(), smem()] + [vmem()] * 3...  33.8 us
    all_gather x1, blocking collectives, on_device(): table = lax.all_gather(rel_table, 'mp', axis=1, tiled=True)  33 us
    pallas_call x2, Pallas kernels, ffn_fwd(): pl.pallas_call(ffn_fwd_kernel, in_specs=[smem()] + [vmem()] * 3 + [hbm()]...  32.4 us
  transfers between devices with their start and end apart: 58, of which 25 were waited for; matrix products, arithmetic and copies ran while one was open for 14% of the time, Pallas kernels for 2%

profile of v1, /device:TPU:8, one launch (start us, length us, event | category | flops | bytes accessed | tf_op | source)
XLA Modules:
  0.0 776.1 jit_solution(16758013085395551460)
XLA Ops:
  13.0 14.8 %collective-permute-done.8 = bf16[192,1024]{1,0:T(8,128)(2,1)S(1)} collective-permute-done((bf16[192,1024]{1,0:T(8,128)(2,1)S(1)}, bf16[192,1024]{1,0:T(8,128)(2,1)S(1)}, u32[]{:S(2)}, u32[]{:S(2)}) %collective-permute-start.8) | collective-permute-done | bytes 393248 | tf_op jit(solution)/shard_map/ppermute | solution.py:538
  42.1 33.0 %all-gather = f32[4,3,32]{2,1,0:T(4,128)S(1)} all-gather(f32[1,3,32]{2,1,0:T(4,128)S(1)} %bitcast.256), channel_id=1, replica_groups=mesh['section'=2,'dp'=4,'mp'=4] {'mp'}, dimensions={0}, use_global_device_ids=true | all-gather | bytes 1920 | tf_op jit(solution)/shard_map/all_gather | solution.py:690
  88.9 11.0 %collective-permute-done.14 = bf16[2,176,768]{2,1,0:T(8,128)(2,1)S(1)} collective-permute-done((bf16[2,176,768]{2,1,0:T(8,128)(2,1)}, bf16[2,176,768]{2,1,0:T(8,128)(2,1)S(1)}, u32[]{:S(2)}, u32[]{:S(2)}) %collective-permute-start.14) | collective-permute-done | bytes 540704 | tf_op jit(solution)/shard_map/ppermute | solution.py:538
  100.6 7.8 %collective-permute-done.4 = bf16[2,192,576]{2,1,0:T(8,128)(2,1)S(1)} collective-permute-done((bf16[2,192,576]{2,1,0:T(8,128)(2,1)S(1)}, bf16[2,192,576]{2,1,0:T(8,128)(2,1)S(1)}, u32[]{:S(2)}, u32[]{:S(2)}) %collective-permute-start.4) | collective-permute-done | bytes 442400 | tf_op jit(solution)/shard_map/ppermute | solution.py:538
  115.8 8.4 %collective-permute-done.15.d1 = bf16[3,176,768]{2,1,0:T(8,128)(2,1)S(1)} collective-permute-done((bf16[3,176,768]{2,1,0:T(8,128)(2,1)S(1)}, bf16[3,176,768]{2,1,0:T(8,128)(2,1)S(1)}, u32[]{:S(2)}, u32[]{:S(2)}) %collective-permute-start.15) | collective-permute-done | bytes 811040 | tf_op jit(solution)/shard_map/ppermute | solution.py:538
  124.8 14.4 %collective-permute-done.5.s1 = bf16[3,192,576]{2,1,0:T(8,128)(2,1)} collective-permute-done((bf16[3,192,576]{2,1,0:T(8,128)(2,1)S(1)}, bf16[3,192,576]{2,1,0:T(8,128)(2,1)}, u32[]{:S(2)}, u32[]{:S(2)}) %collective-permute-start.5) | collective-permute-done | bytes 663584 | tf_op jit(solution)/shard_map/ppermute | solution.py:538
  142.5 17.0 %attn_fwd.2 = (bf16[512,768]{1,0:T(8,128)(2,1)}, bf16[4,512,576]{2,1,0:T(8,128)(2,1)}, f32[4,8,512]{2,1,0:T(8,128)}, bf16[4,512,192]{2,1,0:T(8,128)(2,1)}) custom-call(s32[4]{0:T(128)} %add_add_fusion.flags, f32[32,12]{1,0:T(8,128)} %bitcast.252, bf16[512,768]{1,0:T(8,128)(2,1)} %maximum_select_fusion.2.x_ref, f32[1,768]{1,0:T(1,128)} %gain_ref.15, ...), custom_call_target="tpu_custom_call" | custom-call | tf_op jit(solution)/shard_map/attn_fwd/pallas_call | solution.py:429
  160.7 16.2 %ffn_fwd.2 = (f32[512,768]{1,0:T(8,128)}, f32[512,768]{1,0:T(8,128)}, bf16[512,768]{1,0:T(8,128)(2,1)}, bf16[4,512,512]{2,1,0:T(8,128)(2,1)}, bf16[4,512,512]{2,...) custom-call(s32[4]{0:T(128)} %add_add_fusion.flags, bf16[512,768]{1,0:T(8,128)(2,1)} %maximum_select_fusion.2.x_ref, ...), custom_call_target="tpu_custom_call" | custom-call | tf_op jit(solution)/shard_map/ffn_fwd/pallas_call | solution.py:447
  181.9 15.4 %collective-permute-done.18.x_ref = bf16[512,768]{1,0:T(8,128)(2,1)S(1)} collective-permute-done((bf16[512,768]{1,0:T(8,128)(2,1)S(1)}, bf16[512,768]{1,0:T(8,128)(2,1)S(1)}, u32[]{:S(2)}, u32[]{:S(2)}) %collective-permute-start.18) | collective-permute-done | bytes 786464 | tf_op jit(solution)/shard_map/ppermute | solution.py:722
  198.2 16.8 %attn_fwd.3 = (bf16[512,768]{1,0:T(8,128)(2,1)}, bf16[4,512,576]{2,1,0:T(8,128)(2,1)}, f32[4,8,512]{2,1,0:T(8,128)}, bf16[4,512,192]{2,1,0:T(8,128)(2,1)}) custom-call(s32[4]{0:T(128)} %add_add_fusion.flags, f32[32,12]{1,0:T(8,128)} %bitcast.253, bf16[512,768]{1,0:T(8,128)(2,1)} %copy-done.17, f32[1,768]{1,0:T(1,128)} %gain_ref.15, ...), custom_call_target="tpu_custom_call" | custom-call | tf_op jit(solution)/shard_map/attn_fwd/pallas_call | solution.py:429
  215.0 16.2 %ffn_fwd.3 = (f32[512,768]{1,0:T(8,128)}, f32[512,768]{1,0:T(8,128)}, bf16[512,768]{1,0:T(8,128)(2,1)}, bf16[4,512,512]{2,1,0:T(8,128)(2,1)}, bf16[4,512,512]{2,...) custom-call(s32[4]{0:T(128)} %add_add_fusion.flags, bf16[512,768]{1,0:T(8,128)(2,1)} %copy-done.17, ...), custom_call_target="tpu_custom_call" | custom-call | tf_op jit(solution)/shard_map/ffn_fwd/pallas_call | solution.py:447
  233.6 4.4 collective-permute-done.19
  240.0 10.4 %all_gather.10 = s32[64,32,32]{2,1,0:T(8,128)S(1)} all-gather(s32[16,32,32]{2,1,0:T(8,128)S(1)} %copy-done.30), channel_id=1, replica_groups=mesh['section'=2,'dp'=4,'mp'=4] {'dp'}, dimensions={0}, use_global_device_ids=true | all-gather | bytes 327680 | tf_op jit(solution)/shard_map/all_gather | solution.py:705
  254.3 6.6 collective-permute-done.21
  262.7 24.2 %convert_reduce_fusion = f32[2048,512]{1,0:T(8,128)} fusion(s32[512]{0:T(512)S(1)} %iota_add_fusion, s32[2048,32]{1,0:T(8,128)S(1)} %bitcast_select_fusion), kind=kLoop, calls=%fused_computation.3 | loop fusion | flops 99614720 | bytes 4458496 | tf_op jit(solution)/shard_map/reduce_sum | solution.py:710
  286.8 5.4 copy.83
  292.3 5.1 fusion.41
  298.5 5.2 all-gather.1
  318.7 7.8 %collective-permute-done.27 = bf16[4,256,128]{2,1,0:T(8,128)(2,1)S(1)} collective-permute-done((bf16[4,256,128]{2,1,0:T(8,128)(2,1)S(1)}, bf16[4,256,128]{2,1,0:T(8,128)(2,1)S(1)}, u32[]{:S(2)}, u32[]{:S(2)}) %collective-permute-start.27) | collective-permute-done | bytes 262176 | tf_op jit(solution)/shard_map/ppermute | solution.py:538
  329.4 5.0 collective-permute-done.28
  344.0 6.0 ffn_bwd.2
  350.0 15.1 %attn_bwd.2 = (bf16[512,768]{1,0:T(8,128)(2,1)}, f32[1,768]{1,0:T(1,128)}, f32[4,8,768]{2,1,0:T(8,128)}, bf16[4,384,576]{2,1,0:T(8,128)(2,1)}, bf16[4,384,576]{2...) custom-call(s32[4]{0:T(128)} %add_add_fusion.2.flags, f32[32,12]{1,0:T(8,128)} %bitcast.254, ...), custom_call_target="tpu_custom_call" | custom-call | tf_op jit(solution)/shard_map/attn_bwd/pallas_call | solution.py:512
  367.2 42.9 %collective-permute-done.30 = bf16[512,768]{1,0:T(8,128)(2,1)S(1)} collective-permute-done((bf16[512,768]{1,0:T(8,128)(2,1)}, bf16[512,768]{1,0:T(8,128)(2,1)S(1)}, u32[]{:S(2)}, u32[]{:S(2)}) %collective-permute-start.30) | collective-permute-done | bytes 786464 | tf_op jit(solution)/shard_map/ppermute | solution.py:780
  411.3 21.3 %ffn_bwd.3 = (f32[512,768]{1,0:T(8,128)}, f32[1,768]{1,0:T(1,128)}, bf16[4,384,1024]{2,1,0:T(8,128)(2,1)}, bf16[4,384,1024]{2,1,0:T(8,128)(2,1)}, bf16[4,256,768...) custom-call(s32[4]{0:T(128)} %add_add_fusion.1.flags, ...), custom_call_target="tpu_custom_call", output_to_operand_aliasing={{2}: (21, {}), {3}: (22, {}), {4}: (23, {}), {5}: (24, {})} | custom-call | tf_op jit(solution)/shard_map/ffn_bwd/pallas_call | solution.py:479
  432.6 27.1 %attn_bwd.3 = (bf16[512,768]{1,0:T(8,128)(2,1)}, f32[1,768]{1,0:T(1,128)}, f32[4,8,768]{2,1,0:T(8,128)}, bf16[4,384,576]{2,1,0:T(8,128)(2,1)}, bf16[4,384,576]{2...) custom-call(s32[4]{0:T(128)} %add_add_fusion.1.flags, ...), custom_call_target="tpu_custom_call", output_to_operand_aliasing={{3}: (23, {}), {4}: (24, {}), {5}: (25, {}), {6}: (26, {})} | custom-call | tf_op jit(solution)/shard_map/attn_bwd/pallas_call | solution.py:512
  476.3 122.0 %all-reduce.4.cloned.1.call-done = f32[776,128]{1,0:T(8,128)} async-done(((f32[776,128]{1,0:T(8,128)}), f32[776,128]{1,0:T(8,128)}) %all-reduce.4.cloned.1.call-update) | async-done | bytes 397328 | tf_op jit(solution)/shard_map/psum | solution.py:766
  611.3 6.8 collective-permute-done.37
  651.0 44.6 %collective-permute-done.41 = bf16[2,2,192,576]{3,2,0,1:T(8,128)(2,1)} collective-permute-done((bf16[2,2,192,576]{3,2,0,1:T(8,128)(2,1)}, bf16[2,2,192,576]{3,2,0,1:T(8,128)(2,1)}, u32[]{:S(2)}, u32[]{:S(2)}) %collective-permute-start.41) | collective-permute-done | bytes 884768 | tf_op jit(solution)/shard_map/ppermute | solution.py:538
  703.7 7.7 collective-permute-done.42
  712.8 16.8 %collective-permute-done.48 = bf16[2,192,1024]{2,1,0:T(8,128)(2,1)S(1)} collective-permute-done((bf16[2,192,1024]{2,1,0:T(8,128)(2,1)S(1)}, bf16[2,192,1024]{2,1,0:T(8,128)(2,1)S(1)}, u32[]{:S(2)}, u32[]{:S(2)}) %collective-permute-start.48) | collective-permute-done | bytes 786464 | tf_op jit(solution)/shard_map/ppermute | solution.py:538
  735.4 12.8 %collective-permute-done.49 = bf16[192,1024]{1,0:T(8,128)(2,1)S(1)} collective-permute-done((bf16[192,1024]{1,0:T(8,128)(2,1)S(1)}, bf16[192,1024]{1,0:T(8,128)(2,1)S(1)}, u32[]{:S(2)}, u32[]{:S(2)}) %collective-permute-start.49) | collective-permute-done | bytes 393248 | tf_op jit(solution)/shard_map/ppermute | solution.py:538
  754.2 5.2 collective-permute-done.50
  (355 shorter events, 186.2 us)
Async XLA Ops:
  7.2 591.1 %all-reduce.4.cloned.1.call-start = ((), (), s32[]{:S(2)}) async-start(), calls=%async_computation | async-start | bytes 794624 | tf_op jit(solution)/shard_map/psum | solution.py:766
  8.5 19.3 %collective-permute-start.8 = (bf16[192,1024]{1,0:T(8,128)(2,1)S(1)}, bf16[192,1024]{1,0:T(8,128)(2,1)S(1)}, u32[]{:S(2)}, u32[]{:S(2)}) collective-permute-start(bf16[192,1024]{1,0:T(8,128)(2,1)S(1)} %get-tuple-element.184), channel_id=1, source_target_pairs={{0,2},{1,3},{2,0},{3,1},{4,6},{5,7},{6,4},{7,5},{8,10},{9,11},{10,... | collective-permute-start | bytes 1179656 | tf_op jit(solution)/shard_map/ppermute | solution.py:538
  28.7 46.7 %collective-permute-start.9 = (bf16[2,192,1024]{2,1,0:T(8,128)(2,1)}, bf16[2,192,1024]{2,1,0:T(8,128)(2,1)}, u32[]{:S(2)}, u32[]{:S(2)}) collective-permute-start(bf16[2,192,1024]{2,1,0:T(8,128)(2,1)} %pad_maximum_fusion.5), channel_id=1, source_target_pairs={{0,1},{1,0},{2,3},{3,2},{4,5},{5,4},{6,7},{7,6},{8,9},{9,8},{10,11... | collective-permute-start | bytes 2359304 | tf_op jit(solution)/shard_map/ppermute | solution.py:538
  30.8 52.1 %collective-permute-start.13 = (bf16[176,768]{1,0:T(8,128)(2,1)}, bf16[176,768]{1,0:T(8,128)(2,1)S(1)}, u32[]{:S(2)}, u32[]{:S(2)}) collective-permute-start(bf16[176,768]{1,0:T(8,128)(2,1)} %get-tuple-element.186), channel_id=1, source_target_pairs={{0,2},{1,3},{2,0},{3,1},{4,6},{5,7},{6,4},{7,5},{8,10},{9,11},{10,... | collective-permute-start | bytes 811016 | tf_op jit(solution)/shard_map/ppermute | solution.py:538
  34.6 52.0 %collective-permute-start.3 = (bf16[192,576]{1,0:T(8,128)(2,1)}, bf16[192,576]{1,0:T(8,128)(2,1)S(1)}, u32[]{:S(2)}, u32[]{:S(2)}) collective-permute-start(bf16[192,576]{1,0:T(8,128)(2,1)} %constant_dynamic-slice_fusion.3), channel_id=1, source_target_pairs={{0,2},{1,3},{2,0},{3,1},{4,6},{5,7},{6,4},{7,5},{8,10},{9,11},{10,... | collective-permute-start | bytes 663560 | tf_op jit(solution)/shard_map/ppermute | solution.py:538
  37.2 49.6 %collective-permute-start = (bf16[192,768]{1,0:T(8,128)(2,1)}, bf16[192,768]{1,0:T(8,128)(2,1)}, u32[]{:S(2)}, u32[]{:S(2)}) collective-permute-start(bf16[192,768]{1,0:T(8,128)(2,1)} %get-tuple-element.179), channel_id=1, source_target_pairs={{0,0},{1,1},{2,4},{3,5},{4,2},{5,3},{6,6},{7,7},{8,8},{9,9},{10,12... | collective-permute-start | bytes 884744 | tf_op jit(solution)/shard_map/ppermute | solution.py:596
  40.9 45.8 %collective-permute-start.1 = (bf16[192,768]{1,0:T(8,128)(2,1)S(1)}, bf16[192,768]{1,0:T(8,128)(2,1)}, u32[]{:S(2)}, u32[]{:S(2)}) collective-permute-start(bf16[192,768]{1,0:T(8,128)(2,1)S(1)} %get-tuple-element.180), channel_id=1, source_target_pairs={{0,1},{1,0},{2,5},{3,4},{4,3},{5,2},{6,7},{7,6},{8,9},{9,8},{10,13... | collective-permute-start | bytes 884744 | tf_op jit(solution)/shard_map/ppermute | solution.py:596
  77.7 32.3 %collective-permute-start.10 = (bf16[3,192,1024]{2,1,0:T(8,128)(2,1)}, bf16[3,192,1024]{2,1,0:T(8,128)(2,1)}, u32[]{:S(2)}, u32[]{:S(2)}) collective-permute-start(bf16[3,192,1024]{2,1,0:T(8,128)(2,1)} %pad_maximum_fusion.g0), channel_id=1, source_target_pairs={{0,8},{4,12},{8,0},{12,4},{1,9},{5,13},{9,1},{13,5},{2,10},{6,14},... | collective-permute-start | bytes 3538952 | tf_op jit(solution)/shard_map/ppermute | solution.py:538
  86.7 21.8 %collective-permute-start.4 = (bf16[2,192,576]{2,1,0:T(8,128)(2,1)S(1)}, bf16[2,192,576]{2,1,0:T(8,128)(2,1)S(1)}, u32[]{:S(2)}, u32[]{:S(2)}) collective-permute-start(bf16[2,192,576]{2,1,0:T(8,128)(2,1)S(1)} %pad_maximum_fusion.9), channel_id=1, source_target_pairs={{0,1},{1,0},{2,3},{3,2},{4,5},{5,4},{6,7},{7,6},{8,9},{9,8},{10,11... | collective-permute-start | bytes 1327112 | tf_op jit(solution)/shard_map/ppermute | solution.py:538
  88.1 21.1 %collective-permute-start.2 = (bf16[128,768]{1,0:T(8,128)(2,1)S(1)}, bf16[128,768]{1,0:T(8,128)(2,1)S(1)}, u32[]{:S(2)}, u32[]{:S(2)}) collective-permute-start(bf16[128,768]{1,0:T(8,128)(2,1)S(1)} %slice_bitcast_fusion.7), channel_id=1, source_target_pairs={{0,4},{4,0},{8,12},{12,8},{1,5},{5,1},{9,13},{13,9},{2,6},{6,2},{1... | collective-permute-start | bytes 589832 | tf_op jit(solution)/shard_map/ppermute | solution.py:538
  100.0 24.1 %collective-permute-start.15 = (bf16[3,176,768]{2,1,0:T(8,128)(2,1)S(1)}, bf16[3,176,768]{2,1,0:T(8,128)(2,1)S(1)}, u32[]{:S(2)}, u32[]{:S(2)}) collective-permute-start(bf16[3,176,768]{2,1,0:T(8,128)(2,1)S(1)} %pad_maximum_fusion.4.d0), channel_id=1, source_target_pairs={{0,8},{4,12},{8,0},{12,4},{1,9},{5,13},{9,1},{13,5},{2,10},{6,14},... | collective-permute-start | bytes 2433032 | tf_op jit(solution)/shard_map/ppermute | solution.py:538
  108.6 30.5 %collective-permute-start.5 = (bf16[3,192,576]{2,1,0:T(8,128)(2,1)S(1)}, bf16[3,192,576]{2,1,0:T(8,128)(2,1)}, u32[]{:S(2)}, u32[]{:S(2)}) collective-permute-start(bf16[3,192,576]{2,1,0:T(8,128)(2,1)S(1)} %pad_maximum_fusion.6.s0), channel_id=1, source_target_pairs={{0,8},{4,12},{8,0},{12,4},{1,9},{5,13},{9,1},{13,5},{2,10},{6,14},... | collective-permute-start | bytes 1990664 | tf_op jit(solution)/shard_map/ppermute | solution.py:538
  109.9 49.7 %collective-permute-start.11 = (bf16[3,192,1024]{2,1,0:T(8,128)(2,1)}, bf16[3,192,1024]{2,1,0:T(8,128)(2,1)}, u32[]{:S(2)}, u32[]{:S(2)}) collective-permute-start(bf16[3,192,1024]{2,1,0:T(8,128)(2,1)} %pad_maximum_fusion.g0), channel_id=1, source_target_pairs={{0,4},{4,0},{8,12},{12,8},{1,5},{5,1},{9,13},{13,9},{2,6},{6,2},{1... | collective-permute-start | bytes 3538952 | tf_op jit(solution)/shard_map/ppermute | solution.py:538
  110.1 49.5 %collective-permute-start.12 = (bf16[3,192,1024]{2,1,0:T(8,128)(2,1)}, bf16[3,192,1024]{2,1,0:T(8,128)(2,1)}, u32[]{:S(2)}, u32[]{:S(2)}) collective-permute-start(bf16[3,192,1024]{2,1,0:T(8,128)(2,1)} %collective-permute-done.10.g1), channel_id=1, source_target_pairs={{0,4},{4,0},{8,12},{12,8},{1,5},{5,1},{9,13},{13,9},{2,6},{6,2},{1... | collective-permute-start | bytes 3538952 | tf_op jit(solution)/shard_map/ppermute | solution.py:538
  115.5 44.0 %collective-permute-start.16 = (bf16[3,176,768]{2,1,0:T(8,128)(2,1)S(1)}, bf16[3,176,768]{2,1,0:T(8,128)(2,1)S(1)}, u32[]{:S(2)}, u32[]{:S(2)}) collective-permute-start(bf16[3,176,768]{2,1,0:T(8,128)(2,1)S(1)} %pad_maximum_fusion.4.d0), channel_id=1, source_target_pairs={{0,4},{4,0},{8,12},{12,8},{1,5},{5,1},{9,13},{13,9},{2,6},{6,2},{1... | collective-permute-start | bytes 2433032 | tf_op jit(solution)/shard_map/ppermute | solution.py:538
  124.1 35.4 %collective-permute-start.17 = (bf16[3,176,768]{2,1,0:T(8,128)(2,1)S(1)}, bf16[3,176,768]{2,1,0:T(8,128)(2,1)S(1)}, u32[]{:S(2)}, u32[]{:S(2)}) collective-permute-start(bf16[3,176,768]{2,1,0:T(8,128)(2,1)S(1)} %collective-permute-done.15.d1), channel_id=1, source_target_pairs={{0,4},{4,0},{8,12},{12,8},{1,5},{5,1},{9,13},{13,9},{2,6},{6,2},{1... | collective-permute-start | bytes 2433032 | tf_op jit(solution)/shard_map/ppermute | solution.py:538
  262.7 29.6 %collective-permute-start.22 = (bf16[8,256,128]{2,1,0:T(8,128)(2,1)}, bf16[8,256,128]{2,1,0:T(8,128)(2,1)S(1)}, u32[]{:S(2)}, u32[]{:S(2)}) collective-permute-start(bf16[8,256,128]{2,1,0:T(8,128)(2,1)} %pad_maximum_fusion.8), channel_id=1, source_target_pairs={{0,4},{4,0},{8,12},{12,8},{1,5},{5,1},{9,13},{13,9},{2,6},{6,2},{1... | collective-permute-start | bytes 1572872 | tf_op jit(solution)/shard_map/ppermute | solution.py:538
  365.1 45.0 %collective-permute-start.30 = (bf16[512,768]{1,0:T(8,128)(2,1)}, bf16[512,768]{1,0:T(8,128)(2,1)S(1)}, u32[]{:S(2)}, u32[]{:S(2)}) collective-permute-start(bf16[512,768]{1,0:T(8,128)(2,1)} %get-tuple-element.74.refs_0_), channel_id=1, source_target_pairs={{16,0},{17,1},{18,2},{19,3},{20,4},{21,5},{22,6},{23,7},{24,8},{25... | collective-permute-start | bytes 2359304 | tf_op jit(solution)/shard_map/ppermute | solution.py:780
  461.7 170.1 %collective-permute-start.46 = (bf16[4,384,1024]{2,1,0:T(8,128)(2,1)}, bf16[4,384,1024]{2,1,0:T(8,128)(2,1)}, u32[]{:S(2)}, u32[]{:S(2)}) collective-permute-start(bf16[4,384,1024]{2,1,0:T(8,128)(2,1)} %get-tuple-element.104), channel_id=1, source_target_pairs={{0,4},{4,0},{8,12},{12,8},{1,5},{5,1},{9,13},{13,9},{2,6},{6,2},{1... | collective-permute-start | bytes 9437192 | tf_op jit(solution)/shard_map/ppermute | solution.py:538
  470.6 148.8 %collective-permute-start.52 = (bf16[4,256,768]{2,1,0:T(8,128)(2,1)}, bf16[4,256,768]{2,1,0:T(8,128)(2,1)}, u32[]{:S(2)}, u32[]{:S(2)}) collective-permute-start(bf16[4,256,768]{2,1,0:T(8,128)(2,1)} %get-tuple-element.106), channel_id=1, source_target_pairs={{0,4},{4,0},{8,12},{12,8},{1,5},{5,1},{9,13},{13,9},{2,6},{6,2},{1... | collective-permute-start | bytes 4718600 | tf_op jit(solution)/shard_map/ppermute | solution.py:538
  474.5 129.1 %collective-permute-start.36 = (bf16[2,2,64,768]{3,2,1,0:T(8,128)(2,1)}, bf16[2,2,64,768]{3,2,1,0:T(8,128)(2,1)}, u32[]{:S(2)}, u32[]{:S(2)}) collective-permute-start(bf16[2,2,64,768]{3,2,1,0:T(8,128)(2,1)} %dynamic-slice_bitcast_fusion.6), channel_id=1, source_target_pairs={{0,1},{1,0},{2,3},{3,2},{4,5},{5,4},{6,7},{7,6},{8,9},{9,8},{10,11... | collective-permute-start | bytes 1179656 | tf_op jit(solution)/shard_map/ppermute | solution.py:538
  600.6 25.4 %collective-permute-start.40 = (bf16[4,384,576]{1,2,0:T(8,128)(2,1)}, bf16[4,384,576]{1,2,0:T(8,128)(2,1)}, u32[]{:S(2)}, u32[]{:S(2)}) collective-permute-start(bf16[4,384,576]{1,2,0:T(8,128)(2,1)} %copy.86), channel_id=1, source_target_pairs={{0,4},{4,0},{8,12},{12,8},{1,5},{5,1},{9,13},{13,9},{2,6},{6,2},{1... | collective-permute-start | bytes 5308424 | tf_op jit(solution)/shard_map/ppermute | solution.py:538
  607.3 33.6 %collective-permute-start.32 = (bf16[192,768]{1,0:T(8,128)(2,1)}, bf16[192,768]{1,0:T(8,128)(2,1)}, u32[]{:S(2)}, u32[]{:S(2)}) collective-permute-start(bf16[192,768]{1,0:T(8,128)(2,1)} %get-tuple-element.175), channel_id=1, source_target_pairs={{0,0},{1,1},{4,2},{5,3},{2,4},{3,5},{6,6},{7,7},{8,8},{9,9},{12,10... | collective-permute-start | bytes 884744 | tf_op jit(solution)/shard_map/ppermute | solution.py:622
  618.1 26.7 %collective-permute-start.33 = (bf16[192,768]{1,0:T(8,128)(2,1)}, bf16[192,768]{1,0:T(8,128)(2,1)}, u32[]{:S(2)}, u32[]{:S(2)}) collective-permute-start(bf16[192,768]{1,0:T(8,128)(2,1)} %get-tuple-element.176), channel_id=1, source_target_pairs={{1,0},{0,1},{5,2},{4,3},{3,4},{2,5},{7,6},{6,7},{9,8},{8,9},{13,10... | collective-permute-start | bytes 884744 | tf_op jit(solution)/shard_map/ppermute | solution.py:622
  625.1 23.0 %collective-permute-start.53 = (bf16[2,2,128,768]{3,2,1,0:T(8,128)(2,1)}, bf16[2,2,128,768]{3,2,1,0:T(8,128)(2,1)}, u32[]{:S(2)}, u32[]{:S(2)}) collective-permute-start(bf16[2,2,128,768]{3,2,1,0:T(8,128)(2,1)} %dynamic-slice_bitcast_fusion.1), channel_id=1, source_target_pairs={{0,1},{1,0},{2,3},{3,2},{4,5},{5,4},{6,7},{7,6},{8,9},{9,8},{10,11... | collective-permute-start | bytes 2359304 | tf_op jit(solution)/shard_map/ppermute | solution.py:538
  626.1 20.9 %collective-permute-start.39 = (bf16[2,64,768]{2,1,0:T(8,128)(2,1)S(1)}, bf16[2,64,768]{2,1,0:T(8,128)(2,1)}, u32[]{:S(2)}, u32[]{:S(2)}) collective-permute-start(bf16[2,64,768]{2,1,0:T(8,128)(2,1)S(1)} %add_convert_fusion.5), channel_id=1, source_target_pairs={{0,4},{4,0},{8,12},{12,8},{1,5},{5,1},{9,13},{13,9},{2,6},{6,2},{1... | collective-permute-start | bytes 589832 | tf_op jit(solution)/shard_map/ppermute | solution.py:538
  637.6 59.9 %collective-permute-start.47 = (bf16[2,2,192,1024]{3,2,1,0:T(8,128)(2,1)}, bf16[2,2,192,1024]{3,2,1,0:T(8,128)(2,1)}, u32[]{:S(2)}, u32[]{:S(2)}) collective-permute-start(bf16[2,2,192,1024]{3,2,1,0:T(8,128)(2,1)} %dynamic-slice_bitcast_fusion), channel_id=1, source_target_pairs={{0,8},{4,12},{8,0},{12,4},{1,9},{5,13},{9,1},{13,5},{2,10},{6,14},... | collective-permute-start | bytes 4718600 | tf_op jit(solution)/shard_map/ppermute | solution.py:538
  640.9 54.6 %collective-permute-start.41 = (bf16[2,2,192,576]{3,2,0,1:T(8,128)(2,1)}, bf16[2,2,192,576]{3,2,0,1:T(8,128)(2,1)}, u32[]{:S(2)}, u32[]{:S(2)}) collective-permute-start(bf16[2,2,192,576]{3,2,0,1:T(8,128)(2,1)} %bitcast.197), channel_id=1, source_target_pairs={{0,8},{4,12},{8,0},{12,4},{1,9},{5,13},{9,1},{13,5},{2,10},{6,14},... | collective-permute-start | bytes 2654216 | tf_op jit(solution)/shard_map/ppermute | solution.py:538
  649.5 52.6 %collective-permute-start.54 = (bf16[2,128,768]{2,1,0:T(8,128)(2,1)S(1)}, bf16[2,128,768]{2,1,0:T(8,128)(2,1)S(1)}, u32[]{:S(2)}, u32[]{:S(2)}) collective-permute-start(bf16[2,128,768]{2,1,0:T(8,128)(2,1)S(1)} %dynamic-slice_bitcast_fusion.4), channel_id=1, source_target_pairs={{0,2},{1,3},{2,0},{3,1},{4,6},{5,7},{6,4},{7,5},{8,10},{9,11},{10,... | collective-permute-start | bytes 1179656 | tf_op jit(solution)/shard_map/ppermute | solution.py:538
  699.8 29.8 %collective-permute-start.48 = (bf16[2,192,1024]{2,1,0:T(8,128)(2,1)S(1)}, bf16[2,192,1024]{2,1,0:T(8,128)(2,1)S(1)}, u32[]{:S(2)}, u32[]{:S(2)}) collective-permute-start(bf16[2,192,1024]{2,1,0:T(8,128)(2,1)S(1)} %dynamic-slice_bitcast_fusion.2), channel_id=1, source_target_pairs={{0,1},{1,0},{2,3},{3,2},{4,5},{5,4},{6,7},{7,6},{8,9},{9,8},{10,11... | collective-permute-start | bytes 2359304 | tf_op jit(solution)/shard_map/ppermute | solution.py:538
  702.2 31.4 %collective-permute-start.55 = (bf16[2,128,768]{2,1,0:T(8,128)(2,1)S(1)}, bf16[2,128,768]{2,1,0:T(8,128)(2,1)S(1)}, u32[]{:S(2)}, u32[]{:S(2)}) collective-permute-start(bf16[2,128,768]{2,1,0:T(8,128)(2,1)S(1)} %fusion.10), channel_id=1, source_target_pairs={{0,8},{4,12},{8,0},{12,4},{1,9},{5,13},{9,1},{13,5},{2,10},{6,14},... | collective-permute-start | bytes 1179656 | tf_op jit(solution)/shard_map/ppermute | solution.py:538
  711.6 22.3 %collective-permute-start.43 = (bf16[192,576]{1,0:T(8,128)(2,1)S(1)}, bf16[192,576]{1,0:T(8,128)(2,1)S(1)}, u32[]{:S(2)}, u32[]{:S(2)}) collective-permute-start(bf16[192,576]{1,0:T(8,128)(2,1)S(1)} %dynamic-slice_bitcast_fusion.9), channel_id=1, source_target_pairs={{0,2},{1,3},{2,0},{3,1},{4,6},{5,7},{6,4},{7,5},{8,10},{9,11},{10,... | collective-permute-start | bytes 663560 | tf_op jit(solution)/shard_map/ppermute | solution.py:538
  (64 other events, 950.2 us)
Sparse Core Ops, SparseCore 0:
  470.7 127.5 all-reduce.3

commit v2 on v1

v2 whole, which is shorter than its diff:
```python
import functools

import jax
import jax.numpy as jnp
from jax import lax
from jax.experimental import pallas as pl
from jax.experimental.pallas import tpu as pltpu
from jax.sharding import PartitionSpec as P

D = 768
HEAD_DIM = 64
FF = 2048
PROJ = 128
DOC_LEN = 512
QRY_LEN = 32
QRYS_MB = 8
QRY_ROWS = QRYS_MB * QRY_LEN
MP = 4
QUARTER = D // MP
FQ = FF // MP
HEADS_Q = QUARTER // HEAD_DIM
BLK = 128
NBLK = DOC_LEN // BLK
PAD = 64
SMALL = 32
F_HALF = 3 * FQ // 2
A_HALF = D // 2

bucket_edges = (8, 12, 16, 23, 32, 46, 64, 91)
norm_eps = 1e-06
logit_scale = 16.0
highest = lax.Precision.HIGHEST
f32 = jnp.float32
bf16 = jnp.bfloat16

ACT, IS_DOC, ZPOS, RPOS = range(4)
VMEM_LIMIT = 56 * 1024 * 1024


def mm(a, b):
    return jnp.dot(a, b, preferred_element_type=f32)


def mm_t(a, b):
    return lax.dot_general(a, b, (((1,), (1,)), ((), ())), preferred_element_type=f32)


def t_mm(a, b):
    return lax.dot_general(a, b, (((0,), (0,)), ((), ())), preferred_element_type=f32)


def bucket_of(offset, half_count):
    spread = jnp.abs(offset)
    far_bucket = 7 + sum((spread >= edge).astype(jnp.int32) for edge in bucket_edges)
    near_bucket = jnp.where(spread < 8, spread, far_bucket)
    return near_bucket + half_count * (offset > 0).astype(jnp.int32)


class Copies:
    def __init__(self, sem, first=0):
        self.sem = sem
        self.next = first

    def __call__(self, source, target):
        copy = pltpu.make_async_copy(source, target, self.sem.at[self.next])
        self.next += 1
        copy.start()
        return copy


def wait_all(copies):
    for copy in copies:
        copy.wait()


def weights_of(pieces, lanes, target, sem, z):
    return [
        pltpu.make_async_copy(pieces.at[r, z, :, lanes], target.at[z, pl.ds(r * QUARTER, QUARTER), :], sem.at[z, r])
        for r in range(4)
    ]


def start_all(copies):
    for copy in copies:
        copy.start()


ATTN_LANES = pl.ds(0, D)
FFN_LANES = pl.ds(D, 3 * FQ)


def rows_at(index, size):
    return pl.ds(pl.multiple_of(index * size, size), size)


def bias_matrix(bias_ref, table_ref, head):
    far_up = jnp.full((BLK, BLK), table_ref[31, head], f32)
    far_low = jnp.full((BLK, BLK), table_ref[15, head], f32)
    near = {0: bias_ref[head, 0], 1: bias_ref[head, 1], -1: bias_ref[head, 2]}

    def block(bj, bi):
        if bj - bi in near:
            return near[bj - bi]
        return far_up if bj > bi else far_low

    return jnp.concatenate(
        [jnp.concatenate([block(bj, bi) for bi in range(NBLK)], axis=1) for bj in range(NBLK)], axis=0
    )


def rms_parts(values):
    return lax.rsqrt(jnp.mean(values * values, axis=-1, keepdims=True) + norm_eps)


def rms_back(values, gain, grad):
    scale = rms_parts(values)
    weighted = grad * gain
    inner = jnp.mean(values * weighted, axis=-1, keepdims=True)
    out = scale * (weighted - values * (scale * scale * inner))
    gain_grad = jnp.sum(grad * values * scale, axis=0, keepdims=True)
    return out, gain_grad


def by_kind(flags, body):
    pl.when(flags[IS_DOC] == 1)(lambda: body(DOC_LEN, True))
    pl.when(flags[IS_DOC] == 0)(lambda: body(QRY_ROWS, False))


def head_slices(hh):
    at = hh * HEAD_DIM
    return (
        slice(at, at + HEAD_DIM),
        slice(QUARTER + at, QUARTER + at + HEAD_DIM),
        slice(2 * QUARTER + at, 2 * QUARTER + at + HEAD_DIM),
        slice(PAD + at, PAD + at + HEAD_DIM),
    )


def layer_fwd_kernel(
    flags, table, attn_gain_ref, ffn_gain_ref, x_hbm, bias_hbm, pieces,
    normed_out, qkv_out, lse_out, mixed_out, out_out, low_out, middle_out, normed_ffn_out, hidden_out, ga_out, gb_out,
    x_ref, bias_ref, normed_ref, qkv_ref, lse_ref, mixed_ref, out_ref, low_ref, middle_ref, normed_ffn_ref,
    hidden_ref, ga_ref, gb_ref, wa, wf, sem, asem, fsem, zsem,
):
    copy = Copies(sem)
    get_x = copy(x_hbm, x_ref)
    start_all(weights_of(pieces, ATTN_LANES, wa, asem, 0))
    get_bias = copy(bias_hbm, bias_ref)
    for z in range(1, MP):
        start_all(weights_of(pieces, ATTN_LANES, wa, asem, z))
    get_x.wait()
    first_out = copy.next

    def one_head(z, hh, rows, bias):
        qs, ks, vs, ms = head_slices(hh)
        q, k, v = qkv_ref[z, rows, qs], qkv_ref[z, rows, ks], qkv_ref[z, rows, vs]
        scores = mm_t(k, q) + bias
        peak = jnp.max(scores, axis=0, keepdims=True)
        weights = jnp.exp(scores - peak)
        total = jnp.sum(weights, axis=0, keepdims=True)
        mixed = t_mm(v, weights.astype(bf16)) * (1.0 / total)
        lse_ref[z, hh : hh + 1, rows] = peak + jnp.log(total)
        mixed_ref[z, rows, ms] = mixed.T.astype(bf16)

    def body(rows, doc):
        put = Copies(sem, first_out)
        outs = []

        def send(source, target):
            outs.append(put(source.at[pl.ds(0, rows)], target.at[pl.ds(0, rows)]))

        def parts(z, pairs, at):
            return [
                pltpu.make_async_copy(a.at[z, pl.ds(0, rows)], b.at[z, pl.ds(0, rows)], zsem.at[z, at + i])
                for i, (a, b) in enumerate(pairs)
            ]

        attn_outs = ((qkv_ref, qkv_out), (mixed_ref, mixed_out))
        ffn_outs = ((hidden_ref, hidden_out), (ga_ref, ga_out), (gb_ref, gb_out))
        x = x_ref[:rows].astype(f32)
        normed_ref[:rows] = (x * rms_parts(x) * attn_gain_ref[...]).astype(bf16)
        send(normed_ref, normed_out)
        get_bias.wait()

        @pl.loop(0, MP)
        def _(z):
            wait_all(weights_of(pieces, ATTN_LANES, wa, asem, z))
            start_all(weights_of(pieces, FFN_LANES, wf, fsem, z))
            qkv_ref[z, :rows] = mm(normed_ref[:rows], wa[z]).astype(bf16)
            mixed_ref[z, :rows, :PAD] = jnp.zeros((rows, PAD), bf16)
            for hh in range(HEADS_Q):
                head = z * HEADS_Q + hh
                if doc:
                    one_head(z, hh, slice(0, DOC_LEN), bias_matrix(bias_ref, table, head))
                else:
                    for b in range(QRY_ROWS // BLK):
                        one_head(z, hh, slice(b * BLK, (b + 1) * BLK), bias_ref[head, 0])
            start_all(parts(z, attn_outs, 0))

        outs.append(put(lse_ref, lse_out))
        middle_ref[:rows] = x_ref[:rows].astype(f32)

        @pl.loop(0, MP)
        def _(z):
            middle_ref[:rows] += mm_t(mixed_ref[z, :rows], wa[z, :, 2 * QUARTER + PAD + PAD :])

        middle = middle_ref[:rows]
        send(middle_ref, middle_out)
        normed_ffn_ref[:rows] = (middle * rms_parts(middle) * ffn_gain_ref[...]).astype(bf16)
        send(normed_ffn_ref, normed_ffn_out)
        out_ref[:rows] = middle

        @pl.loop(0, MP)
        def _(z):
            wait_all(weights_of(pieces, FFN_LANES, wf, fsem, z))
            normed = normed_ffn_ref[:rows]
            gate = mm(normed, wf[z, :, :FQ])
            up = mm(normed, wf[z, :, FQ : 2 * FQ])
            coef = 0.7978845608028654
            square = gate * gate
            tanh = jnp.tanh(coef * gate * (1.0 + 0.044715 * square))
            half = 0.5 + 0.5 * tanh
            gelu = gate * half
            slope = half + (0.5 * coef) * gate * (1.0 - tanh * tanh) * (1.0 + 3 * 0.044715 * square)
            hidden = (gelu * up).astype(bf16)
            hidden_ref[z, :rows] = hidden
            ga_ref[z, :rows] = (up * slope).astype(bf16)
            gb_ref[z, :rows] = gelu.astype(bf16)
            start_all(parts(z, ffn_outs, 2))
            out_ref[:rows] += mm_t(hidden, wf[z, :, 2 * FQ :])

        low_ref[:rows] = out_ref[:rows].astype(bf16)
        if not doc:
            out_ref[rows:] = jnp.zeros((DOC_LEN - rows, D), f32)
        outs.append(put(out_ref, out_out))
        send(low_ref, low_out)

        @pl.loop(0, MP)
        def _(z):
            wait_all(parts(z, attn_outs, 0))
            wait_all(parts(z, ffn_outs, 2))

        wait_all(outs)

    by_kind(flags, body)


def ffn_bwd_kernel(
    flags, gain_ref, gout_hbm, middle_hbm, normed_hbm, hidden_hbm, ga_hbm, gb_hbm, pieces,
    *refs,
):
    gmid_out, dgain_out, *df_outs = refs[-22:-16]
    gout_ref, middle_ref, normed_ref, hidden_ref, ga_ref, gb_ref, gmid_ref, dgain_ref = refs[-16:-8]
    wf, gout_t, normed_t, df_buf, gn, sem, fsem, osem = refs[-8:]

    def outs(z, core):
        slot, half = z % 2, D // 2
        copies = []
        for i, out in enumerate(df_outs):
            rows = pl.ds((core if i % 2 == 0 else 1 - core) * half, half)
            lanes = pl.ds(i // 2 * F_HALF, F_HALF)
            copies.append(pltpu.make_async_copy(df_buf.at[slot, rows, lanes], out.at[z], osem.at[slot, i]))
        return copies

    def body(rows, doc):
        core = 0 if doc else 1
        copy = Copies(sem)

        def get(source, target):
            return copy(source.at[pl.ds(0, rows)], target.at[pl.ds(0, rows)])

        get_gout = get(gout_hbm, gout_ref)
        get_normed = get(normed_hbm, normed_ref)
        kept = ((ga_hbm, ga_ref), (gb_hbm, gb_ref), (hidden_hbm, hidden_ref))

        def part(z):
            return weights_of(pieces, FFN_LANES, wf, fsem, z) + [
                pltpu.make_async_copy(a.at[z, pl.ds(0, rows)], b.at[z, pl.ds(0, rows)], fsem.at[z, 4 + i])
                for i, (a, b) in enumerate(kept)
            ]

        start_all(part(0))
        get_middle = get(middle_hbm, middle_ref)
        get_gout.wait()
        gout_t[:, :rows] = gout_ref[:rows].T
        get_normed.wait()
        normed_t[:, :rows] = normed_ref[:rows].T
        gn[:rows] = jnp.zeros((rows, D), f32)

        @pl.loop(0, MP)
        def _(z):
            pl.when(z >= 2)(lambda: wait_all(outs(z - 2, core)))
            pl.when(z + 1 < MP)(lambda: start_all(part(z + 1)))
            wait_all(part(z))
            slot = z % 2
            grad_hidden = mm(gout_ref[:rows], wf[z, :, 2 * FQ :])
            grad_gate = (grad_hidden * ga_ref[z, :rows].astype(f32)).astype(bf16)
            grad_up = (grad_hidden * gb_ref[z, :rows].astype(f32)).astype(bf16)
            df_buf[slot, :, :FQ] = mm(normed_t[:, :rows], grad_gate).astype(bf16)
            df_buf[slot, :, FQ : 2 * FQ] = mm(normed_t[:, :rows], grad_up).astype(bf16)
            df_buf[slot, :, 2 * FQ :] = mm(gout_t[:, :rows], hidden_ref[z, :rows]).astype(bf16)
            start_all(outs(z, core))
            gn[:rows] += mm_t(grad_gate, wf[z, :, :FQ]) + mm_t(grad_up, wf[z, :, FQ : 2 * FQ])

        get_middle.wait()
        back, gain_grad = rms_back(middle_ref[:rows], gain_ref[...], gn[:rows])
        gmid_ref[:rows] = gout_ref[:rows].astype(f32) + back
        dgain_ref[...] = gain_grad
        last = [copy(gmid_ref.at[pl.ds(0, rows)], gmid_out.at[pl.ds(0, rows)]), copy(dgain_ref, dgain_out)]
        for z in (MP - 2, MP - 1):
            wait_all(outs(z, core))
        wait_all(last)

    @pl.when(flags[ACT] == 1)
    def _():
        by_kind(flags, body)


def attn_bwd_kernel(
    flags, table, gain_ref, gmid_hbm, x_hbm, bias_hbm, normed_hbm, qkv_hbm, lse_hbm, mixed_hbm, pieces,
    *refs,
):
    gx_out, dgain_out, diag_out, *da_outs = refs[-28:-21]
    gmid_ref, x_ref, bias_ref, normed_ref, qkv_ref, lse_ref, mixed_ref, gx_ref, dgain_ref, diag_ref = refs[-21:-11]
    wa, gmb, gmid_t, normed_t, gmix, gqkv, da_buf, gn, sem, asem, osem = refs[-11:]

    def one_head(z, hh, rows, bias):
        qs, ks, vs, ms = head_slices(hh)
        q, k, v = qkv_ref[z, rows, qs], qkv_ref[z, rows, ks], qkv_ref[z, rows, vs]
        go = gmix[rows, ms]
        out = mixed_ref[z, rows, ms].astype(f32)
        delta = jnp.sum((go.astype(f32) * out).T, axis=0, keepdims=True)
        probs = jnp.exp(mm_t(k, q) + bias - lse_ref[z, hh : hh + 1, rows])
        grad_scores = probs * (mm_t(v, go) - delta)
        low = grad_scores.astype(bf16)
        gqkv[rows, qs] = t_mm(k, low).T.astype(bf16)
        gqkv[rows, ks] = mm(low, q).astype(bf16)
        gqkv[rows, vs] = mm(probs.astype(bf16), go).astype(bf16)
        return grad_scores

    def band_sums(up, mid, low):
        blank = jnp.zeros((BLK, BLK), f32)
        band = jnp.concatenate([up, mid, low, blank], axis=1)
        width = 4 * BLK

        def left(part, by):
            return pltpu.roll(part, width - by, 1) if by else part

        eight = functools.reduce(jnp.add, [left(band[g : g + 8], g) for g in range(0, BLK, 8)])
        return functools.reduce(jnp.add, [left(eight[r : r + 1], r) for r in range(8)])

    def outs(z, core):
        slot = z % 2
        copies = []
        for i, out in enumerate(da_outs):
            for half in range(2):
                rows = pl.ds((core if i % 2 == 0 else 1 - core) * (D // 2) + half * QUARTER, QUARTER)
                lanes = pl.ds(i // 2 * A_HALF, A_HALF)
                target = out.at[z, half, pl.ds(0, QUARTER), :]
                copies.append(pltpu.make_async_copy(da_buf.at[slot, rows, lanes], target, osem.at[slot, 2 * i + half]))
        return copies

    def body(rows, doc):
        core = 0 if doc else 1
        tail = 2 * QUARTER + PAD + PAD
        copy = Copies(sem)

        def get(source, target):
            return copy(source.at[pl.ds(0, rows)], target.at[pl.ds(0, rows)])

        get_gmid = get(gmid_hbm, gmid_ref)
        get_lse = copy(lse_hbm, lse_ref)
        kept = ((qkv_hbm, qkv_ref), (mixed_hbm, mixed_ref))

        def part(z):
            return weights_of(pieces, ATTN_LANES, wa, asem, z) + [
                pltpu.make_async_copy(a.at[z, pl.ds(0, rows)], b.at[z, pl.ds(0, rows)], asem.at[z, 4 + i])
                for i, (a, b) in enumerate(kept)
            ]

        start_all(part(0))
        get_bias = copy(bias_hbm, bias_ref)
        get_normed = get(normed_hbm, normed_ref)
        get_x = get(x_hbm, x_ref)
        get_gmid.wait()
        gmb[:rows] = gmid_ref[:rows].astype(bf16)
        gmid_t[:, :rows] = gmb[:rows].T
        gqkv[:rows, 3 * QUARTER :] = jnp.zeros((rows, QUARTER), bf16)
        gn[:rows] = jnp.zeros((rows, D), f32)
        get_lse.wait()
        get_normed.wait()
        normed_t[:, :rows] = normed_ref[:rows].T
        get_bias.wait()

        @pl.loop(0, MP)
        def _(z):
            pl.when(z >= 2)(lambda: wait_all(outs(z - 2, core)))
            pl.when(z + 1 < MP)(lambda: start_all(part(z + 1)))
            wait_all(part(z))
            slot = z % 2
            gmix[:rows] = mm(gmb[:rows], wa[z, :, tail:]).astype(bf16)
            for hh in range(HEADS_Q):
                head = z * HEADS_Q + hh
                if doc:
                    grads = one_head(z, hh, slice(0, DOC_LEN), bias_matrix(bias_ref, table, head))

                    def blocks(test):
                        picked = [
                            grads[bj * BLK : (bj + 1) * BLK, bi * BLK : (bi + 1) * BLK]
                            for bj in range(NBLK)
                            for bi in range(NBLK)
                            if test(bj - bi)
                        ]
                        return functools.reduce(jnp.add, picked)

                    sums = band_sums(blocks(lambda d: d == 1), blocks(lambda d: d == 0), blocks(lambda d: d == -1))
                    far_up = jnp.sum(blocks(lambda d: d > 1), axis=0, keepdims=True)
                    far_low = jnp.sum(blocks(lambda d: d < -1), axis=0, keepdims=True)
                    diag_ref[z, hh : hh + 1, :] = jnp.concatenate([sums, far_up, far_low], axis=1)
                else:
                    grads = jnp.zeros((BLK, BLK), f32)
                    for b in range(QRY_ROWS // BLK):
                        grads = grads + one_head(z, hh, slice(b * BLK, (b + 1) * BLK), bias_ref[head, 0])
                    blank = jnp.zeros((BLK, BLK), f32)
                    sums = band_sums(blank, grads, blank)
                    diag_ref[z, hh : hh + 1, :] = jnp.concatenate([sums, jnp.zeros((1, 2 * BLK), f32)], axis=1)
            grads = gqkv[:rows]
            main = mm(normed_t[:, :rows], grads)
            extra = mm(gmid_t[:, :rows], mixed_ref[z, :rows])
            da_buf[slot, :, :tail] = main[:, :tail].astype(bf16)
            da_buf[slot, :, tail:] = (main[:, tail:] + extra).astype(bf16)
            start_all(outs(z, core))
            gn[:rows] += mm_t(grads, wa[z])

        get_x.wait()
        back, gain_grad = rms_back(x_ref[:rows].astype(f32), gain_ref[...], gn[:rows])
        gx_ref[:rows] = (gmid_ref[:rows] + back).astype(bf16)
        dgain_ref[...] = gain_grad
        last = [
            copy(gx_ref.at[pl.ds(0, rows)], gx_out.at[pl.ds(0, rows)]),
            copy(dgain_ref, dgain_out),
            copy(diag_ref, diag_out),
        ]
        for z in (MP - 2, MP - 1):
            wait_all(outs(z, core))
        wait_all(last)

    @pl.when(flags[ACT] == 1)
    def _():
        by_kind(flags, body)


def put_all(refs):
    count = len(refs) // 2
    copies = [pltpu.make_async_copy(refs[count + i], refs[i], refs[-1].at[i]) for i in range(count)]
    start_all(copies)
    wait_all(copies)


def finish_ffn_kernel(flags, mine1, other1, mine2, other2, *refs):
    gate_ref, up_ref, down_ref = refs[3:6]
    core = flags[RPOS] % 2
    half = D // 2
    for side, first, second in ((core, mine1, mine2), (1 - core, other1, other2)):
        rows = rows_at(side, half)
        low = first[...].reshape(half, F_HALF).astype(f32)
        high = second[...].reshape(half, F_HALF).astype(f32)
        gate_ref[rows, :] = low[:, :FQ]
        up_ref[rows, : F_HALF - FQ] = low[:, FQ:]
        up_ref[rows, F_HALF - FQ :] = high[:, : 2 * FQ - F_HALF]
        down = high[:, 2 * FQ - F_HALF :].T

        @pl.when(side == 0)
        def _():
            down_ref[:, :half] = down

        @pl.when(side == 1)
        def _():
            down_ref[:, half:] = down

    put_all(refs)


def finish_attn_kernel(flags, mine1, other1, mine2, other2, *refs):
    q_ref, k_ref, v_ref, o_ref = refs[4:8]
    core = flags[RPOS] % 2
    half = D // 2
    for side, first, second in ((core, mine1, mine2), (1 - core, other1, other2)):
        rows = rows_at(side, half)
        low = first[...].reshape(half, A_HALF).astype(f32)
        high = second[:, :QUARTER].reshape(half, A_HALF).astype(f32)
        q_ref[rows, :] = low[:, :QUARTER]
        k_ref[rows, :] = low[:, QUARTER:]
        v_ref[rows, :] = high[:, :QUARTER]
        out = high[:, QUARTER:].T

        @pl.when(side == 0)
        def _():
            o_ref[:, :half] = out

        @pl.when(side == 1)
        def _():
            o_ref[:, half:] = out

    put_all(refs)


def vmem():
    return pl.BlockSpec(memory_space=pltpu.VMEM)


def smem():
    return pl.BlockSpec(memory_space=pltpu.SMEM)


def hbm():
    return pl.BlockSpec(memory_space=pl.ANY)


def shape(dims, kind):
    return jax.ShapeDtypeStruct(dims, kind)


def params():
    return pltpu.CompilerParams(vmem_limit_bytes=VMEM_LIMIT)


def cost(microseconds):
    return pl.CostEstimate(flops=int(microseconds * 1e9), bytes_accessed=16 * 1024 * 1024, transcendentals=0)


def count_kernel(flags, hits_ref, counts_ref):
    @pl.when(flags[ACT] == 1)
    def _():
        places = lax.broadcasted_iota(jnp.int32, counts_ref.shape, 1)
        hits = hits_ref[...]
        total = jnp.zeros(counts_ref.shape, f32)
        for k in range(hits.shape[1]):
            total = total + (hits[:, k : k + 1] == places).astype(f32)
        counts_ref[...] = total

    @pl.when(flags[ACT] == 0)
    def _():
        counts_ref[...] = jnp.zeros_like(counts_ref)


def count_hits(flags, hits):
    rows, topk = hits.shape
    block = min(rows, 128)
    return pl.pallas_call(
        count_kernel,
        grid=(rows // block,),
        in_specs=[smem(), pl.BlockSpec((block, topk), lambda i: (i, 0))],
        out_specs=pl.BlockSpec((block, DOC_LEN), lambda i: (i, 0)),
        out_shape=shape((rows, DOC_LEN), f32),
        compiler_params=params(),
        cost_estimate=cost(10),
        name="count_hits",
    )(flags, hits)


QUARTERS = (MP, DOC_LEN, FQ)
ROWS = (DOC_LEN, D)


def on_vmem(shapes):
    return [pltpu.VMEM(s.shape, s.dtype) for s in shapes]


def layer_fwd(flags, table, x, attn_gain, ffn_gain, bias, pieces):
    results = [
        shape(ROWS, bf16),
        shape((MP, DOC_LEN, D), bf16),
        shape((MP, 8, DOC_LEN), f32),
        shape((MP, DOC_LEN, PAD + QUARTER), bf16),
        shape(ROWS, f32),
        shape(ROWS, bf16),
        shape(ROWS, f32),
        shape(ROWS, bf16),
        shape(QUARTERS, bf16),
        shape(QUARTERS, bf16),
        shape(QUARTERS, bf16),
    ]
    return pl.pallas_call(
        layer_fwd_kernel,
        in_specs=[smem()] * 2 + [vmem()] * 2 + [hbm()] * 3,
        out_specs=[hbm()] * 11,
        out_shape=results,
        scratch_shapes=on_vmem([shape(ROWS, bf16), shape(bias.shape, f32)] + results)
        + [
            pltpu.VMEM((MP, D, D), bf16),
            pltpu.VMEM((MP, D, 3 * FQ), bf16),
            pltpu.SemaphoreType.DMA((8,)),
            pltpu.SemaphoreType.DMA((MP, 4)),
            pltpu.SemaphoreType.DMA((MP, 4)),
            pltpu.SemaphoreType.DMA((MP, 5)),
        ],
        compiler_params=params(),
        cost_estimate=cost(25),
        name="layer_fwd",
    )(flags, table, attn_gain, ffn_gain, x, bias, pieces)


def finish(kernel, flags, results, *values):
    return pl.pallas_call(
        kernel,
        in_specs=[smem()] + [vmem()] * 4,
        out_specs=[hbm()] * len(results),
        out_shape=[shape(r, f32) for r in results],
        scratch_shapes=on_vmem([shape(r, f32) for r in results]) + [pltpu.SemaphoreType.DMA((len(results),))],
        compiler_params=params(),
        cost_estimate=cost(3),
        name="finish",
    )(flags, *values)


def ffn_bwd(flags, gout, middle, gain, normed, hidden, ga, gb, pieces, prev):
    results = [shape(ROWS, f32), shape((1, D), f32)]
    results += [shape((MP, D // 2, F_HALF), bf16)] * 4
    prev = prev or []
    return pl.pallas_call(
        ffn_bwd_kernel,
        in_specs=[smem(), vmem()] + [hbm()] * (7 + len(prev)),
        out_specs=[hbm()] * 6,
        out_shape=results,
        input_output_aliases={9 + i: 1 + i for i in range(len(prev))},
        scratch_shapes=on_vmem([shape(ROWS, bf16), shape(ROWS, f32), shape(ROWS, bf16)] + [shape(QUARTERS, bf16)] * 3)
        + on_vmem(results[:2])
        + [
            pltpu.VMEM((MP, D, 3 * FQ), bf16),
            pltpu.VMEM((D, DOC_LEN), bf16),
            pltpu.VMEM((D, DOC_LEN), bf16),
            pltpu.VMEM((2, D, 3 * FQ), bf16),
            pltpu.VMEM(ROWS, f32),
            pltpu.SemaphoreType.DMA((8,)),
            pltpu.SemaphoreType.DMA((MP, 7)),
            pltpu.SemaphoreType.DMA((2, 4)),
        ],
        compiler_params=params(),
        cost_estimate=cost(20),
        name="ffn_bwd",
    )(flags, gain, gout, middle, normed, hidden, ga, gb, pieces, *prev)


def attn_bwd(flags, table, gmid, x, gain, bias, normed, qkv, lse, mixed, pieces, prev):
    results = [shape(ROWS, bf16), shape((1, D), f32), shape((MP, 8, 6 * BLK), f32)]
    results += [shape((MP, 2, QUARTER, A_HALF), bf16)] * 2 + [shape((MP, 2, QUARTER + SMALL, A_HALF), bf16)] * 2
    prev = prev or []
    held = (gmid, x, bias, normed, qkv, lse, mixed)
    return pl.pallas_call(
        attn_bwd_kernel,
        in_specs=[smem()] * 2 + [vmem()] + [hbm()] * (8 + len(prev)),
        out_specs=[hbm()] * 7,
        out_shape=results,
        input_output_aliases={11 + i: i for i in range(len(prev))},
        scratch_shapes=on_vmem(held)
        + on_vmem(results[:3])
        + [
            pltpu.VMEM((MP, D, D), bf16),
            pltpu.VMEM(ROWS, bf16),
            pltpu.VMEM((D, DOC_LEN), bf16),
            pltpu.VMEM((D, DOC_LEN), bf16),
            pltpu.VMEM((DOC_LEN, PAD + QUARTER), bf16),
            pltpu.VMEM(ROWS, bf16),
            pltpu.VMEM((2, D, D), bf16),
            pltpu.VMEM(ROWS, f32),
            pltpu.SemaphoreType.DMA((8,)),
            pltpu.SemaphoreType.DMA((MP, 6)),
            pltpu.SemaphoreType.DMA((2, 8)),
        ],
        compiler_params=params(),
        cost_estimate=cost(25),
        name="attn_bwd",
    )(flags, table, gain, gmid, x, bias, normed, qkv, lse, mixed, pieces, *prev)


def swap(values, axis, bit):
    count = lax.axis_size(axis)
    return lax.ppermute(values, axis, [(i, i ^ bit) for i in range(count)])


def swap_cores(values, axis, bit, core):
    dp_count, mp_count = lax.axis_size("dp"), lax.axis_size("mp")
    perm = []
    for i in range(core, dp_count, 2):
        for j in range(mp_count):
            to = (i ^ bit) * mp_count + j if axis == "dp" else i * mp_count + (j ^ bit)
            perm.append((i * mp_count + j, to))
    return lax.ppermute(values, ("dp", "mp"), perm)


def hop(rows, source):
    first = lax.ppermute(rows[:QRY_ROWS], "section", [(source, 1 - source)])
    dp_count = lax.axis_size("dp")
    perm = [(source * dp_count + i, (1 - source) * dp_count + i) for i in range(0, dp_count, 2)]
    return jnp.concatenate([first, lax.ppermute(rows[QRY_ROWS:], ("section", "dp"), perm)])


def gather_all(piece, quad, z):
    if lax.axis_size("dp") == 4:
        return lax.all_gather(piece, ("dp", "mp")).reshape(4, MP, *piece.shape)
    pieces = piece[None]
    for axis, bit in (("mp", 1), ("mp", 2), ("dp", 1), ("dp", 2)):
        pieces = jnp.concatenate([pieces, swap(pieces, axis, bit)])
    return jnp.take(pieces, (quad * MP + z) ^ jnp.arange(4 * MP), axis=0).reshape(4, MP, *piece.shape)


def pick(values, axis, index):
    return lax.dynamic_index_in_dim(values, index, axis, keepdims=False)


def add_low(a, b):
    return (a.astype(f32) + b.astype(f32)).astype(bf16)


def fence(*values):
    return lax.optimization_barrier(values)


def total_of(terms):
    return functools.reduce(jnp.add, [term.astype(f32) for term in terms]).astype(bf16)


def give(terms, dim, axis, bit, mine):
    return swap(total_of([pick(term, dim, 1 - mine) for term in terms]), axis, bit)


def take(terms, dim, mine, got):
    return [pick(term, dim, mine) for term in terms] + [got]


def in_order(mine, values, other):
    return jnp.where(mine == 0, jnp.stack([values, other]), jnp.stack([other, values]))


def over_rest(total):
    bit = 4
    while bit < lax.axis_size("dp"):
        total = add_low(total, swap(total, "dp", bit))
        bit *= 2
    return total


def spread_tokens(tokens, place, pairs):
    core, _, z = place
    got = []
    for turn in range(2):
        perm = []
        for j in range(pairs):
            for c in range(2):
                for zz in range(MP):
                    u = (turn + zz) % 2
                    perm.append(((2 * j + c) * MP + zz, (2 * j + zz // 2) * MP + 2 * c + u))
        block = pick(tokens, 0, (turn + z) % 2)
        got.append(lax.ppermute(block, ("dp", "mp"), perm))
    low, high = jnp.where(z % 2 == 0, jnp.stack(got), jnp.stack(got[::-1]))
    cut = DOC_LEN - 2 * QUARTER
    tail = swap(low[:cut], "dp", 1)
    doc = jnp.concatenate([low, high, tail])
    qry = jnp.concatenate([low[cut:], high, jnp.zeros((DOC_LEN - QRY_ROWS, D), low.dtype)])
    return jnp.where(core == 0, doc, qry)


def collect_rows(rows, place, pairs):
    core, _, z = place
    cut = DOC_LEN - 2 * QUARTER
    tail = swap(rows[2 * QUARTER :], "dp", 1)
    low_q = jnp.concatenate([tail, rows[: QUARTER - cut]])
    high_q = rows[QUARTER - cut : QRY_ROWS]
    low = jnp.where(core == 0, rows[:QUARTER], low_q)
    high = jnp.where(core == 0, rows[QUARTER : 2 * QUARTER], high_q)
    got = []
    for turn in range(2):
        perm = []
        for j in range(pairs):
            for c in range(2):
                for zz in range(MP):
                    u = (turn + zz) % 2
                    perm.append(((2 * j + zz // 2) * MP + 2 * c + u, (2 * j + c) * MP + zz))
        block = jnp.where((z + turn) % 2 == 0, low, high)
        got.append(lax.ppermute(block, ("dp", "mp"), perm))
    return jnp.where(z % 2 == 0, jnp.stack(got), jnp.stack(got[::-1]))


def gather_slots(values, steps, core):
    for axis, bit in steps:
        values = jnp.concatenate([values, swap_cores(values, axis, bit, core)])
    return values


def scatter_slots(values, steps, core):
    for axis, bit in reversed(steps):
        half = values.shape[0] // 2
        values = add_low(values[:half], swap_cores(values[half:], axis, bit, core))
    return values[0]


def on_device(
    tokens,
    attn_gain,
    w_query,
    w_key,
    w_value,
    w_out,
    ffn_gain,
    w_gate,
    w_up,
    w_down,
    rel_table,
    final_gain,
    w_proj,
    positives,
    retrieved,
):
    section = lax.axis_index("section")
    dp = lax.axis_index("dp")
    dp_count = lax.axis_size("dp")
    z = lax.axis_index("mp")
    core, y = dp % 2, (dp // 2) % 2
    place = (core, y, z)
    pairs = dp_count // 2
    chip = (dp // 2) * MP + z
    chips = pairs * MP
    is_doc = core == 0
    first = section == 0
    quad = dp % 4

    rows = [lax.dynamic_slice_in_dim(w[0], quad * QUARTER, QUARTER, 0) for w in (w_query, w_key, w_value)]
    rows.append(lax.dynamic_slice_in_dim(w_out[0], quad * QUARTER, QUARTER, 1).T)
    rows += [lax.dynamic_slice_in_dim(w[0], quad * QUARTER, QUARTER, 0) for w in (w_gate, w_up)]
    rows.append(lax.dynamic_slice_in_dim(w_down[0], quad * QUARTER, QUARTER, 1).T)
    pieces = gather_all(jnp.concatenate(rows, axis=1), quad, z)
    x_first = spread_tokens(tokens, place, pairs)

    heads_dev = rel_table.shape[1]
    buckets = rel_table.shape[0]
    half_count = buckets // 2
    table = jnp.stack([rel_table, swap(rel_table, "mp", 1)])
    table = jnp.concatenate([table, swap(table, "mp", 2)])
    table = jnp.take(table, z ^ jnp.arange(MP), axis=0)
    table = jnp.swapaxes(table, 0, 1).reshape(rel_table.shape[0], -1)
    at = jnp.arange(BLK, dtype=jnp.int32)
    offset = at[:, None] - at[None, :]
    offsets = jnp.stack([offset, offset + BLK, offset - BLK])
    bucket_ids = jnp.arange(buckets, dtype=jnp.int32)
    pick_near = (bucket_of(offsets, half_count)[..., None] == bucket_ids).astype(f32)
    bias = jnp.einsum("bh,mjib->hmji", table, pick_near, precision=highest)
    same_query = (at[:, None] // QRY_LEN) == (at[None, :] // QRY_LEN)
    bias = jnp.where(jnp.logical_or(is_doc, same_query), bias, -1e30)

    def flags_for(active):
        return jnp.stack([jnp.asarray(active).astype(jnp.int32), is_doc.astype(jnp.int32), z, quad])

    slot_ids = jnp.arange(chips, dtype=jnp.int32)
    mb_of_slot = chip ^ slot_ids
    topk = retrieved.shape[2]
    hits = jnp.concatenate([retrieved.reshape(retrieved.shape[0], -1), positives], axis=1)[None]
    bit = 1
    while bit < dp_count:
        hits = jnp.concatenate([hits, swap(hits, "dp", bit)])
        bit *= 2
    hits = jnp.take(hits, dp ^ jnp.arange(dp_count), axis=0).reshape(chips * QRYS_MB, -1)
    all_positives = hits[:, QRY_LEN * topk :]
    slot_retrieved = jnp.take(hits[:, : QRY_LEN * topk].reshape(chips, QRY_ROWS, topk), mb_of_slot, axis=0)
    counts = count_hits(flags_for(jnp.logical_not(first)), slot_retrieved.reshape(-1, topk) - chip * DOC_LEN)
    x_first, counts = lax.optimization_barrier((x_first, counts))

    flags_f = flags_for(1)
    kept = []
    x = x_first
    for step in range(2):
        normed, qkv, lse, mixed, out, low, middle, normed_ffn, hidden, ga, gb = layer_fwd(
            flags_f, table, x, attn_gain, ffn_gain, bias, pieces
        )
        kept.append((x, normed, qkv, lse, mixed, middle, normed_ffn, hidden, ga, gb))
        if step == 0:
            x = hop(low, 0)

    scale = PROJ ** (-0.5)
    normed_final = (out * rms_parts(out) * final_gain).astype(bf16)
    embed = mm(normed_final, w_proj).astype(bf16)
    steps = [("mp", 1), ("mp", 2)]
    bit = 2
    while bit < dp_count:
        steps.append(("dp", bit))
        bit *= 2
    query_slots = swap(gather_slots(embed[None, :QRY_ROWS], steps, 1), "dp", 1).reshape(-1, PROJ)
    sims = mm_t(query_slots, embed)
    weighted = jnp.exp(sims * scale) * counts
    mass = jnp.sum(weighted, axis=1)
    logit = logit_scale * jnp.mean(jnp.log1p(mass).reshape(chips * QRYS_MB, QRY_LEN), axis=1)
    logit = jnp.take(logit.reshape(chips, QRYS_MB), mb_of_slot, axis=0).reshape(1, -1)
    logits = gather_slots(logit, steps, 0)
    chosen = jnp.any(all_positives[None] == mb_of_slot[:, None, None], axis=2).astype(f32)
    peak = jnp.max(logits, axis=0)
    spread = jnp.exp(logits - peak)
    all_total = jnp.sum(spread, axis=0)
    pos_total = jnp.sum(chosen * spread, axis=0)
    n_queries = logits.shape[1]
    loss_here = jnp.sum(jnp.log(all_total) - jnp.log(pos_total)) / n_queries
    grad_logit = (spread[0] / all_total - chosen[0] * spread[0] / pos_total) / n_queries
    grad_logit = jnp.take(grad_logit.reshape(chips, QRYS_MB), mb_of_slot, axis=0).reshape(-1)
    coef = jnp.repeat(grad_logit * (logit_scale / QRY_LEN * scale), QRY_LEN) / (1.0 + mass)
    grad_sims = (weighted * coef[:, None]).astype(bf16)
    grad_doc = t_mm(grad_sims, query_slots).astype(bf16)
    grad_query = mm(grad_sims, embed).astype(bf16).reshape(chips, QRY_ROWS, PROJ)
    grad_query = scatter_slots(swap(grad_query, "dp", 1), steps, 1)
    grad_query = jnp.concatenate([grad_query, jnp.zeros((DOC_LEN - QRY_ROWS, PROJ), bf16)])
    grad_embed = jnp.where(is_doc, grad_doc, grad_query)
    grad_final, grad_final_gain = rms_back(out, final_gain, mm_t(grad_embed, w_proj))
    live = jnp.logical_not(first)
    lead = jnp.logical_and(live, jnp.logical_and(dp == 0, z == 0))
    loss_here = jnp.where(lead, loss_here, 0.0)
    loss_high = loss_here.astype(bf16)
    loss_low = (loss_here - loss_high.astype(f32)).astype(bf16)
    early = jnp.concatenate(
        [
            t_mm(grad_embed, normed_final).astype(bf16),
            grad_final_gain.astype(bf16),
            jnp.full((1, D), loss_high),
            jnp.full((1, D), loss_low),
        ]
    )
    early = jnp.where(live, early, 0.0)
    early = early + swap(early, "section", 1)

    def ffn_back(step, grad_out, prev):
        x, normed, qkv, lse, mixed, middle, normed_ffn, hidden, ga, gb = kept[step]
        flags = flags_for(section == step)
        return ffn_bwd(flags, grad_out, middle, ffn_gain, normed_ffn, hidden, ga, gb, pieces, prev)

    def attn_back(step, gmid, prev):
        x, normed, qkv, lse, mixed, middle, normed_ffn, hidden, ga, gb = kept[step]
        flags = flags_for(section == step)
        return attn_bwd(flags, table, gmid, x, attn_gain, bias, normed, qkv, lse, mixed, pieces, prev)

    gmid, *ffn_prev = ffn_back(1, grad_final.astype(bf16), None)
    attn_prev = attn_back(1, gmid, None)
    gmid, grad_ffn_gain, f1_keep, f1_send, f2_keep, f2_send = ffn_back(0, hop(attn_prev[0], 1), ffn_prev)

    zl, zh = z % 2, z // 2

    def parts(values):
        return values.reshape(2, 2, 2, -1, values.shape[-1])

    f1 = [parts(f1_keep), parts(swap(f1_send, "dp", 1))]
    f2 = [parts(f2_keep), parts(swap(f2_send, "dp", 1))]
    f1, f2, gmid = fence(f1, f2, gmid)

    f1_got = give(f1, 2, "dp", 2, y)
    f2_got = give(f2, 1, "mp", 1, zl)
    gx, grad_attn_gain, diag, *attn_grads = attn_back(0, gmid, attn_prev)
    lanes = jnp.arange(4 * BLK, dtype=jnp.int32)
    band_offset = jnp.where(lanes <= 2 * BLK + BLK - 1, BLK - lanes, 5 * BLK - lanes)
    band_bucket = jnp.concatenate(
        [
            bucket_of(band_offset, half_count),
            jnp.full((BLK,), buckets - 1, jnp.int32),
            jnp.full((BLK,), half_count - 1, jnp.int32),
        ]
    )
    pick_band = (band_bucket[:, None] == bucket_ids).astype(f32)
    table_part = jnp.einsum("zhc,cb->zhb", diag[:, :heads_dev], pick_band, precision=highest)
    table_rows = jnp.pad(table_part.reshape(MP, 1, -1), ((0, 0), (0, 0), (0, A_HALF - heads_dev * buckets)))
    shared = jnp.concatenate([grad_attn_gain.astype(bf16), grad_ffn_gain.astype(bf16), early[PROJ:]]).reshape(-1, A_HALF)
    small = jnp.concatenate([table_rows.astype(bf16), jnp.broadcast_to(shared[None], (MP,) + shared.shape)], axis=1)
    n_small = SMALL - 16
    small = jnp.pad(small, ((0, 0), (0, n_small - small.shape[1]), (0, 0)))
    small = jnp.broadcast_to(small[:, None], (MP, 2, n_small, A_HALF))
    proj_parts = early[:PROJ].reshape(MP, 2, 2, 16, A_HALF)

    def with_small(values, half):
        rows = jnp.concatenate([small, pick(proj_parts, 1, half)], axis=2)
        return lax.dynamic_update_slice_in_dim(values, rows, QUARTER, 2)

    a1_keep, a1_send, a2_keep, a2_send = attn_grads
    a2_keep, a2_send = with_small(a2_keep, core), with_small(a2_send, 1 - core)
    f1, f1_got, f2, f2_got, a1_keep, a1_send, a2_keep, a2_send, gx = fence(
        f1, f1_got, f2, f2_got, a1_keep, a1_send, a2_keep, a2_send, gx
    )

    a1 = [parts(a1_keep), parts(swap(a1_send, "dp", 1))]
    a2 = [parts(a2_keep), parts(swap(a2_send, "dp", 1))]
    f1, f2 = take(f1, 2, y, f1_got), take(f2, 1, zl, f2_got)
    f1_got = give(f1, 1, "mp", 1, zl)
    f2_got = give(f2, 0, "mp", 2, zh)
    a1_got = give(a1, 2, "dp", 2, y)
    f1, f1_got, f2, f2_got, a1, a1_got, a2, gx = fence(f1, f1_got, f2, f2_got, a1, a1_got, a2, gx)

    f1, f2, a1 = take(f1, 1, zl, f1_got), take(f2, 0, zh, f2_got), take(a1, 2, y, a1_got)
    f1_got = give(f1, 0, "mp", 2, zh)
    f2 = total_of(f2)
    f2_got = swap(f2, "dp", 2)
    a1_got = give(a1, 1, "mp", 1, zl)
    a2_got = give(a2, 1, "mp", 1, zl)
    f1, f1_got, f2, f2_got, a1, a1_got, a2, a2_got, gx = fence(f1, f1_got, f2, f2_got, a1, a1_got, a2, a2_got, gx)

    a1, a2 = take(a1, 1, zl, a1_got), take(a2, 1, zl, a2_got)
    a1_got = give(a1, 0, "mp", 2, zh)
    a2_got = give(a2, 0, "mp", 2, zh)
    f1 = over_rest(total_of(take(f1, 0, zh, f1_got)))
    f1_got = swap(f1, "dp", 2)
    f2 = over_rest(add_low(f2, f2_got))
    f2_other = swap(f2, "dp", 1)
    f1, f1_got, f2, f2_other, a1, a1_got, a2, a2_got, gx = fence(
        f1, f1_got, f2, f2_other, a1, a1_got, a2, a2_got, gx
    )

    a1, a2 = total_of(take(a1, 0, zh, a1_got)), total_of(take(a2, 0, zh, a2_got))
    a1 = over_rest(a1)
    a1_got = swap(a1, "dp", 2)
    a2_got = swap(a2, "dp", 2)
    f1 = in_order(y, f1, f1_got)
    f1_other = swap(f1, "dp", 1)
    d_inputs = collect_rows(gx, place, pairs)[None]
    flags_end = flags_for(1)
    ffn_sums = finish(finish_ffn_kernel, flags_end, [(D, FQ), (D, FQ), (FQ, D)], f1, f1_other, f2, f2_other)
    ffn_sums, a1, a1_got, a2, a2_got, d_inputs = fence(ffn_sums, a1, a1_got, a2, a2_got, d_inputs)

    a1 = in_order(y, a1, a1_got)
    a2 = over_rest(add_low(a2, a2_got))
    a1_other, a2_other = swap(a1, "dp", 1), swap(a2, "dp", 1)
    small_sum = a2[0, QUARTER : QUARTER + n_small].astype(f32)
    table_other = swap(small_sum[:1], "section", 1)
    attn_sums = finish(
        finish_attn_kernel, flags_end, [(D, QUARTER)] * 3 + [(QUARTER, D)], a1, a1_other, a2, a2_other
    )
    proj_sum = in_order(core, a2[:, QUARTER + n_small :], a2_other[:, QUARTER + n_small :])
    proj_sum = proj_sum.astype(f32).reshape(PROJ // MP, D)
    shared_sum = small_sum[1 : 1 + shared.shape[0]].reshape(-1, D)
    grad_table = (small_sum[:1] + table_other)[0, : heads_dev * buckets].reshape(heads_dev, buckets).T
    return (
        shared_sum[3, 0] + shared_sum[4, 0],
        d_inputs,
        shared_sum[0:1],
        attn_sums[0][None],
        attn_sums[1][None],
        attn_sums[2][None],
        attn_sums[3][None],
        shared_sum[1:2],
        ffn_sums[0][None],
        ffn_sums[1][None],
        ffn_sums[2][None],
        grad_table,
        shared_sum[2],
        proj_sum.T,
    )


def solution(mesh):
    return jax.shard_map(
        on_device,
        mesh=mesh,
        in_specs=(
            P("dp", "mp", None),
            P("section", None),
            P("section", None, "mp"),
            P("section", None, "mp"),
            P("section", None, "mp"),
            P("section", "mp", None),
            P("section", None),
            P("section", None, "mp"),
            P("section", None, "mp"),
            P("section", "mp", None),
            P(None, "mp"),
            P(),
            P(),
            P("dp", None),
            P("dp", None, None),
        ),
        out_specs=(
            P(),
            P("section", "dp", "mp", None),
            P("section", None),
            P("section", None, "mp"),
            P("section", None, "mp"),
            P("section", None, "mp"),
            P("section", "mp", None),
            P("section", None),
            P("section", None, "mp"),
            P("section", None, "mp"),
            P("section", "mp", None),
            P(None, "mp"),
            P(),
            P(None, "mp"),
        ),
        check_vma=False,
    )
```

time: 789 us -> 507 us (0.64)
  waiting for transfers between devices: 369 us -> 195 us
  blocking collectives: 48.6 us -> 0 us
  other arithmetic: 80.1 us -> 39.6 us
  Pallas kernels: 136 us -> 110 us
  starting transfers between devices: 63.2 us -> 83.7 us
    psum x1 -> x0, waiting for transfers between devices: 122 us -> none  [on_device(): early = lax.psum(early, ('section', 'dp', 'mp'))]
    ppermute x51 -> x32, waiting for transfers between devices: 188 us -> 68.8 us  [swap(): return lax.ppermute(values, axis, [(i, i ^ bit) for i in range(count)])]
    all_gather x0 -> x1, waiting for transfers between devices: none -> 54.8 us  [gather_all(): return lax.all_gather(piece, ('dp', 'mp')).reshape(4, MP, *piece.shape)]
    all_gather x3 -> x0, blocking collectives: 48.6 us -> none  [the longest x1 33 us: on_device(): table = lax.all_gather(rel_table, 'mp', axis=1, tiled=True)]
    pallas_call x8 -> x9, Pallas kernels: 136 us -> 110 us  [the longest x2 48.7 us: layer_fwd(): pl.pallas_call(layer_fwd_kernel, in_specs=[smem()] * 2 + [vmem()] * 2 + [...]
    reduce_sum x1 -> x0, other arithmetic: 24.2 us -> none  [on_device(): jnp.sum((slot_retrieved.reshape(-1, topk)[:, :, None] == places).astype(f...]
    ppermute x2 -> x13, starting transfers between devices: 4.73 us -> 22.6 us  [the longest x9 15.3 us: swap_cores(): return lax.ppermute(values, ('dp', 'mp'), perm)]
    convert_element_type x7 -> x18, other arithmetic: 5.55 us -> 22.5 us  [the longest x14 20.5 us: total_of(): functools.reduce(jnp.add, [term.astype(f32) for term in terms]).astype(bf16)]
  transfers between devices with their start and end apart: 58 -> 50, of which waited for: 25 -> 21; matrix products, arithmetic and copies ran while one was open for 14% -> 10% of each run, Pallas kernels for 2% -> 8%
where the time goes in v2:
time: 507 us; the launch traced here: 498 us
  waiting for transfers between devices  195 us (38%)
  Pallas kernels  110 us (22%)
  starting transfers between devices  83.7 us (17%)
  other arithmetic  39.6 us (8%)
  local copies, waits for them, and re-layouts  38.3 us (8%)
  between operations  19.1 us (4%)
  matrix products  11.8 us (2%)
    ppermute x32, waiting for transfers between devices, swap(): return lax.ppermute(values, axis, [(i, i ^ bit) for i in range(count)])  68.8 us
    ppermute x32, starting transfers between devices, swap(): return lax.ppermute(values, axis, [(i, i ^ bit) for i in range(count)])  55.2 us
    all_gather x1, waiting for transfers between devices, gather_all(): return lax.all_gather(piece, ('dp', 'mp')).reshape(4, MP, *piece.shape)  54.8 us
    pallas_call x2, Pallas kernels, layer_fwd(): pl.pallas_call(layer_fwd_kernel, in_specs=[smem()] * 2 + [vmem()] * 2 + [...  48.7 us
    ppermute x2, waiting for transfers between devices, hop(): first = lax.ppermute(rows[:QRY_ROWS], 'section', [(source, 1 - source)])  47.9 us
    pallas_call x2, Pallas kernels, attn_bwd(): pl.pallas_call(attn_bwd_kernel, in_specs=[smem()] * 2 + [vmem()] + [hbm()...  25.6 us
    convert_element_type x14, other arithmetic, total_of(): functools.reduce(jnp.add, [term.astype(f32) for term in terms]).astype(bf16)  20.5 us
    pallas_call x2, Pallas kernels, ffn_bwd(): pl.pallas_call(ffn_bwd_kernel, in_specs=[smem(), vmem()] + [hbm()] * (7 +...  18.3 us
  transfers between devices with their start and end apart: 50, of which 21 were waited for; matrix products, arithmetic and copies ran while one was open for 10% of the time, Pallas kernels for 8%

profile of v2, /device:TPU:8, one launch (start us, length us, event | category | flops | bytes accessed | tf_op | source)
XLA Modules:
  0.0 497.8 jit_solution(9616641151798084304)
XLA Ops:
  15.6 3.7 collective-permute-start.2
  22.4 10.0 %collective-permute-done = f32[32,3]{0,1:T(4,128)S(1)} collective-permute-done((f32[32,3]{0,1:T(4,128)S(1)}, f32[32,3]{0,1:T(4,128)S(1)}, u32[]{:S(2)}, u32[]{:S(2)}) %collective-permute-start) | collective-permute-done | bytes 416 | tf_op jit(solution)/shard_map/ppermute | solution.py:679
  32.4 4.4 collective-permute-start.1
  49.6 9.6 %count_hits.1 = f32[2048,512]{1,0:T(8,128)} custom-call(s32[4]{0:T(128)} %add_add_fusion.3.flags, s32[2048,32]{1,0:T(8,128)} %fusion.8.hits_ref), custom_call_target="tpu_custom_call" | custom-call | flops 10000000000 | bytes 16777216 | tf_op jit(solution)/shard_map/count_hits/pallas_call | solution.py:550
  60.6 15.1 %collective-permute-start.4 = (bf16[128,768]{1,0:T(8,128)(2,1)S(1)}, bf16[128,768]{1,0:T(8,128)(2,1)S(1)}, u32[]{:S(2)}, u32[]{:S(2)}) collective-permute-start(bf16[128,768]{1,0:T(8,128)(2,1)S(1)} %slice_bitcast_fusion.2), channel_id=1, source_target_pairs={{0,4},{4,0},{8,12},{12,8},{1,5},{5,1},{9,13},{13,9},{2,6},{6,2},{1... | collective-permute-start | bytes 589832 | tf_op jit(solution)/shard_map/ppermute | solution.py:679
  78.2 54.8 %all-gather.3.cloned.1.call-done = bf16[3072,2304]{1,0:T(8,128)(2,1)} async-done(((bf16[192,2304]{1,0:T(8,128)(2,1)}), bf16[3072,2304]{1,0:T(8,128)(2,1)}) %all-gather.3.cloned.1.call-update) | async-done | bytes 14155792 | tf_op jit(solution)/shard_map/all_gather | solution.py:701
  133.0 24.0 %layer_fwd.2 = (bf16[512,768]{1,0:T(8,128)(2,1)}, bf16[4,512,768]{2,1,0:T(8,128)(2,1)}, f32[4,8,512]{2,1,0:T(8,128)}, bf16[4,512,256]{2,1,0:T(8,128)(2,1)}, f32[...) custom-call(s32[4]{0:T(128)} %get-tuple-element.328.flags, ...), custom_call_target="tpu_custom_call" | custom-call | flops 24999999488 | bytes 16777216 | tf_op jit(solution)/shard_map/layer_fwd/pallas_call | solution.py:584
  158.2 3.4 collective-permute-start.7
  162.9 3.9 collective-permute-done.7
  166.9 4.2 collective-permute-done.8
  172.0 24.7 %layer_fwd.3 = (bf16[512,768]{1,0:T(8,128)(2,1)}, bf16[4,512,768]{2,1,0:T(8,128)(2,1)}, f32[4,8,512]{2,1,0:T(8,128)}, bf16[4,512,256]{2,1,0:T(8,128)(2,1)}, f32[...) custom-call(s32[4]{0:T(128)} %get-tuple-element.328.flags, ...), custom_call_target="tpu_custom_call" | custom-call | flops 24999999488 | bytes 16777216 | tf_op jit(solution)/shard_map/layer_fwd/pallas_call | solution.py:584
  203.4 3.0 fusion.48
  207.4 4.7 collective-permute-start.13
  213.6 4.2 collective-permute-start.14
  222.5 2.9 collective-permute-done.15
  226.6 3.1 convolution_convert_fusion
  244.2 43.9 %collective-permute-done.20 = bf16[256,768]{1,0:T(8,128)(2,1)S(1)} collective-permute-done((bf16[256,768]{1,0:T(8,128)(2,1)S(1)}, bf16[256,768]{1,0:T(8,128)(2,1)S(1)}, u32[]{:S(2)}, u32[]{:S(2)}) %collective-permute-start.20) | collective-permute-done | bytes 393248 | tf_op jit(solution)/shard_map/ppermute | solution.py:693
  288.1 7.1 %collective-permute-done.21 = bf16[256,768]{1,0:T(8,128)(2,1)S(1)} collective-permute-done((bf16[256,768]{1,0:T(8,128)(2,1)S(1)}, bf16[256,768]{1,0:T(8,128)(2,1)S(1)}, u32[]{:S(2)}, u32[]{:S(2)}) %collective-permute-start.21) | collective-permute-done | bytes 393248 | tf_op jit(solution)/shard_map/ppermute | solution.py:696
  296.2 17.1 %ffn_bwd.3 = (f32[512,768]{1,0:T(8,128)}, f32[1,768]{1,0:T(1,128)}, bf16[4,384,768]{2,1,0:T(8,128)(2,1)}, bf16[4,384,768]{2,1,0:T(8,128)(2,1)}, bf16[4,384,768]{...) custom-call(s32[4]{0:T(128)} %add_add_fusion.1.flags, ...), custom_call_target="tpu_custom_call", output_to_operand_aliasing={{1}: (9, {}), {2}: (10, {}), {3}: (11, {}), {4}: (12, {}), ... | custom-call | flops 20000000000 | bytes 16777216 | tf_op jit(solution)/shard_map/ffn_bwd/pallas_call | solution.py:621
  316.0 7.1 %collective-permute-done.26 = bf16[131,768]{1,0:T(8,128)(2,1)S(1)} collective-permute-done((bf16[131,768]{1,0:T(8,128)(2,1)S(1)}, bf16[131,768]{1,0:T(8,128)(2,1)S(1)}, u32[]{:S(2)}, u32[]{:S(2)}) %collective-permute-start.26) | collective-permute-done | bytes 201248 | tf_op jit(solution)/shard_map/ppermute | solution.py:679
  323.5 3.1 fusion.3
  328.8 2.6 fusion.2
  332.0 24.1 %attn_bwd.3 = (bf16[512,768]{1,0:T(8,128)(2,1)}, f32[1,768]{1,0:T(1,128)}, f32[4,8,768]{2,1,0:T(8,128)}, bf16[4,2,192,384]{3,2,1,0:T(8,128)(2,1)}, bf16[4,2,192,...) custom-call(s32[4]{0:T(128)} %add_add_fusion.1.flags, ...), custom_call_target="tpu_custom_call", output_to_operand_aliasing={{0}: (11, {}), {1}: (12, {}), {2}: (13, {}), {3}: (14, {}),... | custom-call | flops 24999999488 | bytes 16777216 | tf_op jit(solution)/shard_map/attn_bwd/pallas_call | solution.py:650
  372.9 15.6 %collective-permute-done.28 = bf16[2,192,768]{2,1,0:T(8,128)(2,1)} collective-permute-done((bf16[2,192,768]{2,1,0:T(8,128)(2,1)}, bf16[2,192,768]{2,1,0:T(8,128)(2,1)}, u32[]{:S(2)}, u32[]{:S(2)}) %collective-permute-start.28) | collective-permute-done | bytes 589856 | tf_op jit(solution)/shard_map/ppermute | solution.py:679
  399.3 4.4 collective-permute-start.32
  406.1 13.2 %collective-permute-done.34 = bf16[2,192,384]{2,1,0:T(8,128)(2,1)S(1)} collective-permute-done((bf16[2,192,384]{2,1,0:T(8,128)(2,1)S(1)}, bf16[2,192,384]{2,1,0:T(8,128)(2,1)S(1)}, u32[]{:S(2)}, u32[]{:S(2)}) %collective-permute-start.34) | collective-permute-done | bytes 294944 | tf_op jit(solution)/shard_map/ppermute | solution.py:679
  419.4 4.0 collective-permute-done.32
  433.5 11.2 %collective-permute-done.38 = bf16[192,384]{1,0:T(8,128)(2,1)S(1)} collective-permute-done((bf16[192,384]{1,0:T(8,128)(2,1)S(1)}, bf16[192,384]{1,0:T(8,128)(2,1)S(1)}, u32[]{:S(2)}, u32[]{:S(2)}) %collective-permute-start.38) | collective-permute-done | bytes 147488 | tf_op jit(solution)/shard_map/ppermute | solution.py:679
  453.8 6.0 %collective-permute-done.45 = bf16[192,768]{1,0:T(8,128)(2,1)S(1)} collective-permute-done((bf16[192,768]{1,0:T(8,128)(2,1)S(1)}, bf16[192,768]{1,0:T(8,128)(2,1)S(1)}, u32[]{:S(2)}, u32[]{:S(2)}) %collective-permute-start.45) | collective-permute-done | bytes 294944 | tf_op jit(solution)/shard_map/ppermute | solution.py:781
  461.4 4.3 finish.2
  465.9 8.2 %collective-permute-start.47 = (bf16[2,224,384]{2,1,0:T(8,128)(2,1)S(1)}, bf16[2,224,384]{2,1,0:T(8,128)(2,1)S(1)}, u32[]{:S(2)}, u32[]{:S(2)}) collective-permute-start(bf16[2,224,384]{2,1,0:T(8,128)(2,1)S(1)} %add_convert_fusion.5.mine2), channel_id=1, source_target_pairs={{0,4},{4,0},{8,12},{12,8},{1,5},{5,1},{9,13},{13,9},{2,6},{6,2},{1... | collective-permute-start | bytes 1032200 | tf_op jit(solution)/shard_map/ppermute | solution.py:679
  480.2 3.5 finish.3
  (350 shorter events, 127.7 us)
Async XLA Ops:
  7.2 125.8 %all-gather.3.cloned.1.call-start = ((), (), s32[]{:S(2)}) async-start(), calls=%async_computation | async-start | bytes 15040512 | tf_op jit(solution)/shard_map/all_gather | solution.py:701
  14.7 26.7 %collective-permute-start.5 = (s32[1,16,1028]{2,1,0:T(8,128)S(1)}, s32[1,16,1028]{2,1,0:T(8,128)S(1)}, u32[]{:S(2)}, u32[]{:S(2)}) collective-permute-start(s32[1,16,1028]{2,1,0:T(8,128)S(1)} %add_bitcast_fusion), channel_id=1, source_target_pairs={{0,4},{4,0},{8,12},{12,8},{1,5},{5,1},{9,13},{13,9},{2,6},{6,2},{1... | collective-permute-start | bytes 197384 | tf_op jit(solution)/shard_map/ppermute | solution.py:679
  15.6 43.6 %collective-permute-start.2 = (bf16[192,768]{1,0:T(8,128)(2,1)}, bf16[192,768]{1,0:T(8,128)(2,1)}, u32[]{:S(2)}, u32[]{:S(2)}) collective-permute-start(bf16[192,768]{1,0:T(8,128)(2,1)} %get-tuple-element.314), channel_id=1, source_target_pairs={{0,0},{1,1},{2,4},{3,5},{4,2},{5,3},{6,6},{7,7},{8,8},{9,9},{10,12... | collective-permute-start | bytes 884744 | tf_op jit(solution)/shard_map/ppermute | solution.py:755
  19.3 39.9 %collective-permute-start.3 = (bf16[192,768]{1,0:T(8,128)(2,1)S(1)}, bf16[192,768]{1,0:T(8,128)(2,1)}, u32[]{:S(2)}, u32[]{:S(2)}) collective-permute-start(bf16[192,768]{1,0:T(8,128)(2,1)S(1)} %get-tuple-element.315), channel_id=1, source_target_pairs={{0,1},{1,0},{2,5},{3,4},{4,3},{5,2},{6,7},{7,6},{8,9},{9,8},{10,13... | collective-permute-start | bytes 884744 | tf_op jit(solution)/shard_map/ppermute | solution.py:755
  19.3 13.1 %collective-permute-start = (f32[32,3]{0,1:T(4,128)S(1)}, f32[32,3]{0,1:T(4,128)S(1)}, u32[]{:S(2)}, u32[]{:S(2)}) collective-permute-start(f32[32,3]{0,1:T(4,128)S(1)} %copy-done.31), channel_id=1, source_target_pairs={{0,1},{1,0},{2,3},{3,2},{4,5},{5,4},{6,7},{7,6},{8,9},{9,8},{10,11... | collective-permute-start | bytes 1160 | tf_op jit(solution)/shard_map/ppermute | solution.py:679
  60.6 16.4 %collective-permute-start.4 = (bf16[128,768]{1,0:T(8,128)(2,1)S(1)}, bf16[128,768]{1,0:T(8,128)(2,1)S(1)}, u32[]{:S(2)}, u32[]{:S(2)}) collective-permute-start(bf16[128,768]{1,0:T(8,128)(2,1)S(1)} %slice_bitcast_fusion.2), channel_id=1, source_target_pairs={{0,4},{4,0},{8,12},{12,8},{1,5},{5,1},{9,13},{13,9},{2,6},{6,2},{1... | collective-permute-start | bytes 589832 | tf_op jit(solution)/shard_map/ppermute | solution.py:679
  158.2 8.7 %collective-permute-start.7 = (bf16[256,768]{1,0:T(8,128)(2,1)S(1)}, bf16[256,768]{1,0:T(8,128)(2,1)S(1)}, u32[]{:S(2)}, u32[]{:S(2)}) collective-permute-start(bf16[256,768]{1,0:T(8,128)(2,1)S(1)} %get-tuple-element.311), channel_id=1, source_target_pairs={{0,16},{1,17},{2,18},{3,19},{4,20},{5,21},{6,22},{7,23},{8,24},{9,... | collective-permute-start | bytes 1179656 | tf_op jit(solution)/shard_map/ppermute | solution.py:693
  161.6 9.5 %collective-permute-start.8 = (bf16[256,768]{1,0:T(8,128)(2,1)S(1)}, bf16[256,768]{1,0:T(8,128)(2,1)S(1)}, u32[]{:S(2)}, u32[]{:S(2)}) collective-permute-start(bf16[256,768]{1,0:T(8,128)(2,1)S(1)} %get-tuple-element.310), channel_id=1, source_target_pairs={{0,16},{8,24},{1,17},{9,25},{2,18},{10,26},{3,19},{11,27}} | collective-permute-start | bytes 1179656 | tf_op jit(solution)/shard_map/ppermute | solution.py:696
  241.0 47.1 %collective-permute-start.20 = (bf16[256,768]{1,0:T(8,128)(2,1)S(1)}, bf16[256,768]{1,0:T(8,128)(2,1)S(1)}, u32[]{:S(2)}, u32[]{:S(2)}) collective-permute-start(bf16[256,768]{1,0:T(8,128)(2,1)S(1)} %get-tuple-element.308), channel_id=1, source_target_pairs={{16,0},{17,1},{18,2},{19,3},{20,4},{21,5},{22,6},{23,7},{24,8},{25... | collective-permute-start | bytes 1179656 | tf_op jit(solution)/shard_map/ppermute | solution.py:693
  242.3 53.0 %collective-permute-start.21 = (bf16[256,768]{1,0:T(8,128)(2,1)S(1)}, bf16[256,768]{1,0:T(8,128)(2,1)S(1)}, u32[]{:S(2)}, u32[]{:S(2)}) collective-permute-start(bf16[256,768]{1,0:T(8,128)(2,1)S(1)} %get-tuple-element.309), channel_id=1, source_target_pairs={{16,0},{24,8},{17,1},{25,9},{18,2},{26,10},{19,3},{27,11}} | collective-permute-start | bytes 1179656 | tf_op jit(solution)/shard_map/ppermute | solution.py:696
  313.3 10.2 %collective-permute-start.22 = (bf16[4,384,768]{2,1,0:T(8,128)(2,1)}, bf16[4,384,768]{2,1,0:T(8,128)(2,1)}, u32[]{:S(2)}, u32[]{:S(2)}) collective-permute-start(bf16[4,384,768]{2,1,0:T(8,128)(2,1)} %get-tuple-element.163), channel_id=1, source_target_pairs={{0,4},{4,0},{8,12},{12,8},{1,5},{5,1},{9,13},{13,9},{2,6},{6,2},{1... | collective-permute-start | bytes 7077896 | tf_op jit(solution)/shard_map/ppermute | solution.py:679
  313.4 10.1 %collective-permute-start.23 = (bf16[4,384,768]{2,1,0:T(8,128)(2,1)}, bf16[4,384,768]{2,1,0:T(8,128)(2,1)}, u32[]{:S(2)}, u32[]{:S(2)}) collective-permute-start(bf16[4,384,768]{2,1,0:T(8,128)(2,1)} %get-tuple-element.165), channel_id=1, source_target_pairs={{0,4},{4,0},{8,12},{12,8},{1,5},{5,1},{9,13},{13,9},{2,6},{6,2},{1... | collective-permute-start | bytes 7077896 | tf_op jit(solution)/shard_map/ppermute | solution.py:679
  315.9 7.2 %collective-permute-start.26 = (bf16[131,768]{1,0:T(8,128)(2,1)S(1)}, bf16[131,768]{1,0:T(8,128)(2,1)S(1)}, u32[]{:S(2)}, u32[]{:S(2)}) collective-permute-start(bf16[131,768]{1,0:T(8,128)(2,1)S(1)} %maximum_select_fusion.6), channel_id=1, source_target_pairs={{0,16},{16,0},{1,17},{17,1},{2,18},{18,2},{3,19},{19,3},{4,20},{20... | collective-permute-start | bytes 603656 | tf_op jit(solution)/shard_map/ppermute | solution.py:679
  326.6 32.3 %collective-permute-start.25 = (bf16[2,2,192,768]{3,2,1,0:T(8,128)(2,1)}, bf16[2,2,192,768]{3,2,1,0:T(8,128)(2,1)}, u32[]{:S(2)}, u32[]{:S(2)}) collective-permute-start(bf16[2,2,192,768]{3,2,1,0:T(8,128)(2,1)} %fusion.3), channel_id=1, source_target_pairs={{0,1},{1,0},{2,3},{3,2},{4,5},{5,4},{6,7},{7,6},{8,9},{9,8},{10,11... | collective-permute-start | bytes 3538952 | tf_op jit(solution)/shard_map/ppermute | solution.py:679
  331.4 27.4 %collective-permute-start.24 = (bf16[2,2,192,768]{3,2,0,1:T(8,128)(2,1)}, bf16[2,2,192,768]{3,2,0,1:T(8,128)(2,1)}, u32[]{:S(2)}, u32[]{:S(2)}) collective-permute-start(bf16[2,2,192,768]{3,2,0,1:T(8,128)(2,1)} %fusion.2), channel_id=1, source_target_pairs={{0,8},{4,12},{8,0},{12,4},{1,9},{5,13},{9,1},{13,5},{2,10},{6,14},... | collective-permute-start | bytes 3538952 | tf_op jit(solution)/shard_map/ppermute | solution.py:679
  358.9 30.9 %collective-permute-start.31 = (bf16[4,2,224,384]{3,2,1,0:T(8,128)(2,1)}, bf16[4,2,224,384]{3,2,1,0:T(8,128)(2,1)}, u32[]{:S(2)}, u32[]{:S(2)}) collective-permute-start(bf16[4,2,224,384]{3,2,1,0:T(8,128)(2,1)} %get-tuple-element.199), channel_id=1, source_target_pairs={{0,4},{4,0},{8,12},{12,8},{1,5},{5,1},{9,13},{13,9},{2,6},{6,2},{1... | collective-permute-start | bytes 4128776 | tf_op jit(solution)/shard_map/ppermute | solution.py:679
  361.8 26.7 %collective-permute-start.28 = (bf16[2,192,768]{2,1,0:T(8,128)(2,1)}, bf16[2,192,768]{2,1,0:T(8,128)(2,1)}, u32[]{:S(2)}, u32[]{:S(2)}) collective-permute-start(bf16[2,192,768]{2,1,0:T(8,128)(2,1)} %fusion.4), channel_id=1, source_target_pairs={{0,2},{1,3},{2,0},{3,1},{4,6},{5,7},{6,4},{7,5},{8,10},{9,11},{10,... | collective-permute-start | bytes 1769480 | tf_op jit(solution)/shard_map/ppermute | solution.py:679
  365.0 24.8 %collective-permute-start.27 = (bf16[2,192,768]{2,1,0:T(8,128)(2,1)}, bf16[2,192,768]{2,1,0:T(8,128)(2,1)}, u32[]{:S(2)}, u32[]{:S(2)}) collective-permute-start(bf16[2,192,768]{2,1,0:T(8,128)(2,1)} %fusion.5), channel_id=1, source_target_pairs={{0,1},{1,0},{2,3},{3,2},{4,5},{5,4},{6,7},{7,6},{8,9},{9,8},{10,11... | collective-permute-start | bytes 1769480 | tf_op jit(solution)/shard_map/ppermute | solution.py:679
  367.8 22.0 %collective-permute-start.30 = (bf16[2,2,192,384]{3,2,0,1:T(8,128)(2,1)}, bf16[2,2,192,384]{3,2,0,1:T(8,128)(2,1)S(1)}, u32[]{:S(2)}, u32[]{:S(2)}) collective-permute-start(bf16[2,2,192,384]{3,2,0,1:T(8,128)(2,1)} %fusion.12), channel_id=1, source_target_pairs={{0,8},{4,12},{8,0},{12,4},{1,9},{5,13},{9,1},{13,5},{2,10},{6,14},... | collective-permute-start | bytes 1769480 | tf_op jit(solution)/shard_map/ppermute | solution.py:679
  391.3 32.1 %collective-permute-start.35 = (bf16[2,2,224,384]{3,2,1,0:T(8,128)(2,1)S(1)}, bf16[2,2,224,384]{3,2,1,0:T(8,128)(2,1)S(1)}, u32[]{:S(2)}, u32[]{:S(2)}) collective-permute-start(bf16[2,2,224,384]{3,2,1,0:T(8,128)(2,1)S(1)} %fusion.9), channel_id=1, source_target_pairs={{0,1},{1,0},{2,3},{3,2},{4,5},{5,4},{6,7},{7,6},{8,9},{9,8},{10,11... | collective-permute-start | bytes 2064392 | tf_op jit(solution)/shard_map/ppermute | solution.py:679
  394.9 24.5 %collective-permute-start.34 = (bf16[2,192,384]{2,1,0:T(8,128)(2,1)S(1)}, bf16[2,192,384]{2,1,0:T(8,128)(2,1)S(1)}, u32[]{:S(2)}, u32[]{:S(2)}) collective-permute-start(bf16[2,192,384]{2,1,0:T(8,128)(2,1)S(1)} %fusion.13), channel_id=1, source_target_pairs={{0,1},{1,0},{2,3},{3,2},{4,5},{5,4},{6,7},{7,6},{8,9},{9,8},{10,11... | collective-permute-start | bytes 884744 | tf_op jit(solution)/shard_map/ppermute | solution.py:679
  396.5 26.9 %collective-permute-start.33 = (bf16[2,192,768]{2,1,0:T(8,128)(2,1)S(1)}, bf16[2,192,768]{2,1,0:T(8,128)(2,1)S(1)}, u32[]{:S(2)}, u32[]{:S(2)}) collective-permute-start(bf16[2,192,768]{2,1,0:T(8,128)(2,1)S(1)} %fusion.6), channel_id=1, source_target_pairs={{0,8},{4,12},{8,0},{12,4},{1,9},{5,13},{9,1},{13,5},{2,10},{6,14},... | collective-permute-start | bytes 1769480 | tf_op jit(solution)/shard_map/ppermute | solution.py:679
  399.3 24.1 %collective-permute-start.32 = (bf16[192,768]{1,0:T(8,128)(2,1)S(1)}, bf16[192,768]{1,0:T(8,128)(2,1)S(1)}, u32[]{:S(2)}, u32[]{:S(2)}) collective-permute-start(bf16[192,768]{1,0:T(8,128)(2,1)S(1)} %fusion.14), channel_id=1, source_target_pairs={{0,2},{1,3},{2,0},{3,1},{4,6},{5,7},{6,4},{7,5},{8,10},{9,11},{10,... | collective-permute-start | bytes 884744 | tf_op jit(solution)/shard_map/ppermute | solution.py:679
  424.5 20.1 %collective-permute-start.39 = (bf16[2,224,384]{2,1,0:T(8,128)(2,1)S(1)}, bf16[2,224,384]{2,1,0:T(8,128)(2,1)S(1)}, u32[]{:S(2)}, u32[]{:S(2)}) collective-permute-start(bf16[2,224,384]{2,1,0:T(8,128)(2,1)S(1)} %fusion.10), channel_id=1, source_target_pairs={{0,2},{1,3},{2,0},{3,1},{4,6},{5,7},{6,4},{7,5},{8,10},{9,11},{10,... | collective-permute-start | bytes 1032200 | tf_op jit(solution)/shard_map/ppermute | solution.py:679
  426.6 18.0 %collective-permute-start.37 = (bf16[2,192,768]{2,1,0:T(8,128)(2,1)S(1)}, bf16[2,192,768]{2,1,0:T(8,128)(2,1)S(1)}, u32[]{:S(2)}, u32[]{:S(2)}) collective-permute-start(bf16[2,192,768]{2,1,0:T(8,128)(2,1)S(1)} %add_convert_fusion.3.mine2), channel_id=1, source_target_pairs={{0,4},{4,0},{8,12},{12,8},{1,5},{5,1},{9,13},{13,9},{2,6},{6,2},{1... | collective-permute-start | bytes 1769480 | tf_op jit(solution)/shard_map/ppermute | solution.py:679
  428.0 16.6 %collective-permute-start.36 = (bf16[192,768]{1,0:T(8,128)(2,1)S(1)}, bf16[192,768]{1,0:T(8,128)(2,1)}, u32[]{:S(2)}, u32[]{:S(2)}) collective-permute-start(bf16[192,768]{1,0:T(8,128)(2,1)S(1)} %fusion.15), channel_id=1, source_target_pairs={{0,8},{4,12},{8,0},{12,4},{1,9},{5,13},{9,1},{13,5},{2,10},{6,14},... | collective-permute-start | bytes 884744 | tf_op jit(solution)/shard_map/ppermute | solution.py:679
  431.5 13.1 %collective-permute-start.38 = (bf16[192,384]{1,0:T(8,128)(2,1)S(1)}, bf16[192,384]{1,0:T(8,128)(2,1)S(1)}, u32[]{:S(2)}, u32[]{:S(2)}) collective-permute-start(bf16[192,384]{1,0:T(8,128)(2,1)S(1)} %fusion.16), channel_id=1, source_target_pairs={{0,2},{1,3},{2,0},{3,1},{4,6},{5,7},{6,4},{7,5},{8,10},{9,11},{10,... | collective-permute-start | bytes 442376 | tf_op jit(solution)/shard_map/ppermute | solution.py:679
  447.6 13.1 %collective-permute-start.40 = (bf16[2,192,768]{2,1,0:T(8,128)(2,1)S(1)}, bf16[2,192,768]{2,1,0:T(8,128)(2,1)S(1)}, u32[]{:S(2)}, u32[]{:S(2)}) collective-permute-start(bf16[2,192,768]{2,1,0:T(8,128)(2,1)S(1)} %maximum_select_fusion.2.mine1), channel_id=1, source_target_pairs={{0,4},{4,0},{8,12},{12,8},{1,5},{5,1},{9,13},{13,9},{2,6},{6,2},{1... | collective-permute-start | bytes 1769480 | tf_op jit(solution)/shard_map/ppermute | solution.py:679
  449.9 9.8 %collective-permute-start.45 = (bf16[192,768]{1,0:T(8,128)(2,1)S(1)}, bf16[192,768]{1,0:T(8,128)(2,1)S(1)}, u32[]{:S(2)}, u32[]{:S(2)}) collective-permute-start(bf16[192,768]{1,0:T(8,128)(2,1)S(1)} %get-tuple-element.307), channel_id=1, source_target_pairs={{1,0},{0,1},{5,2},{4,3},{3,4},{2,5},{7,6},{6,7},{9,8},{8,9},{13,10... | collective-permute-start | bytes 884744 | tf_op jit(solution)/shard_map/ppermute | solution.py:781
  451.5 14.3 %collective-permute-start.42 = (bf16[2,224,384]{2,1,0:T(8,128)(2,1)S(1)}, bf16[2,224,384]{2,1,0:T(8,128)(2,1)S(1)}, u32[]{:S(2)}, u32[]{:S(2)}) collective-permute-start(bf16[2,224,384]{2,1,0:T(8,128)(2,1)S(1)} %fusion.11), channel_id=1, source_target_pairs={{0,8},{4,12},{8,0},{12,4},{1,9},{5,13},{9,1},{13,5},{2,10},{6,14},... | collective-permute-start | bytes 1032200 | tf_op jit(solution)/shard_map/ppermute | solution.py:679
  453.0 12.8 %collective-permute-start.41 = (bf16[192,384]{1,0:T(8,128)(2,1)S(1)}, bf16[192,384]{1,0:T(8,128)(2,1)S(1)}, u32[]{:S(2)}, u32[]{:S(2)}) collective-permute-start(bf16[192,384]{1,0:T(8,128)(2,1)S(1)} %fusion.17), channel_id=1, source_target_pairs={{0,8},{4,12},{8,0},{12,4},{1,9},{5,13},{9,1},{13,5},{2,10},{6,14},... | collective-permute-start | bytes 442376 | tf_op jit(solution)/shard_map/ppermute | solution.py:679
  465.9 12.8 %collective-permute-start.47 = (bf16[2,224,384]{2,1,0:T(8,128)(2,1)S(1)}, bf16[2,224,384]{2,1,0:T(8,128)(2,1)S(1)}, u32[]{:S(2)}, u32[]{:S(2)}) collective-permute-start(bf16[2,224,384]{2,1,0:T(8,128)(2,1)S(1)} %add_convert_fusion.5.mine2), channel_id=1, source_target_pairs={{0,4},{4,0},{8,12},{12,8},{1,5},{5,1},{9,13},{13,9},{2,6},{6,2},{1... | collective-permute-start | bytes 1032200 | tf_op jit(solution)/shard_map/ppermute | solution.py:679
  (56 other events, 302.5 us)
Sparse Core Ops, SparseCore 0:
  14.6 118.3 all-gather.2
